TPU v7x, 128 devices: a whole 4x4x4 slice. The times are simulated.
128 devices in a mesh: dp: 4 (over y_hi, core), seq: 32 (over z, y_lo, x).
Axes of the slice: x: 4, y: 4 (y_hi: 2, y_lo: 2; y = y_hi * 2 + y_lo), z: 4, core: 2. Of those that a mesh axis runs over, the one named last changes fastest.
Arguments:
- query: bfloat16 [4, 8192, 1152], P('dp', 'seq'), may hold values from -14 to 14
- key: bfloat16 [4, 8192, 1152], P('dp', 'seq'), may hold values from -14 to 14
- value: bfloat16 [4, 8192, 1152], P('dp', 'seq'), may hold values from -6 to 6
- grad_out: bfloat16 [4, 8192, 1152], P('dp', 'seq'), may hold values from -6 to 6
- out_proj: bfloat16 [1152, 1152], replicated, may hold values from -0.1875 to 0.1875
- lengths: int32 [4, 32], P('dp'), may hold values from 1 to 512, 8192 in all within a row
Outputs:
- grad_query: bfloat16 [4, 8192, 1152], P('dp', 'seq')
- grad_key: bfloat16 [4, 8192, 1152], P('dp', 'seq')
- grad_value: bfloat16 [4, 8192, 1152], P('dp', 'seq')
- grad_proj: float32 [1152, 1152], P('seq')
All inputs are finite; a program needn't handle non-finite values.
Results may differ from a plain program's by a relative error of at most 0.025.
Values may be sent and summed in bfloat16 or wider, within the bound.
No kernel may reach another device: no remote copies, remote signals or barrier semaphores. Data moves between devices by JAX's collectives and lax.ppermute only.
A program may use at most 128 MiB of HBM per device.

v0:
```python
import jax
import jax.numpy as jnp
from jax import lax
from jax.sharding import PartitionSpec as P

HEADS = 16
HEAD_DIM = 72
SPAN = 2


def from_behind(block, axis, distance):
    devices = range(lax.axis_size(axis))
    route = [(i - distance, i) for i in devices if i - distance in devices]
    return lax.ppermute(block, axis, route)


def heads_of(array):
    return array.reshape(array.shape[0], HEADS, HEAD_DIM)


def tile_scores(q_heads, q_ids, k_heads, k_ids):
    scores = jnp.einsum(
        "qhd,khd->hqk", q_heads, k_heads, preferred_element_type=jnp.float32
    ) * HEAD_DIM ** (-0.5)
    allowed = (q_ids[:, None] == k_ids[None, :])[None, :, :]
    return (scores, allowed)


def tile_grads(q_heads, q_ids, do_heads, log_block, dots_block, k_heads, v_heads, k_ids):
    scores, allowed = tile_scores(q_heads, q_ids, k_heads, k_ids)
    weights = jnp.where(allowed, jnp.exp(scores - log_block[:, :, None]), 0.0)
    dprob = jnp.einsum("qhd,khd->hqk", do_heads, v_heads, preferred_element_type=jnp.float32)
    dscore = (weights * (dprob - dots_block[:, :, None]) * HEAD_DIM ** (-0.5)).astype(jnp.bfloat16)
    return (weights.astype(jnp.bfloat16), dscore)


def per_device(query, key, value, grad_out, out_proj, lengths):
    row_count = query.shape[1]
    model_width = query.shape[2]
    seq_count = lax.axis_size("seq")
    seq_index = lax.axis_index("seq")
    seq_total = row_count * seq_count
    image_ends = jnp.cumsum(lengths[0])

    def image_ids(first_row):
        positions = first_row + jnp.arange(row_count, dtype=jnp.int32)
        found = jnp.sum((image_ends[None, :] <= positions[:, None]).astype(jnp.int32), axis=1)
        inside = (positions >= 0) & (positions < seq_total)
        return jnp.where(inside, found, -1)

    own_ids = image_ids(seq_index * row_count)
    own_query = query[0]
    own_keys = key[0]
    own_values = value[0]
    own_grads = grad_out[0]
    q_heads = heads_of(own_query)
    block_shifts = [0]
    for reach in range(1, SPAN + 1):
        block_shifts = block_shifts + [reach, -reach]
    key_tiles = []
    for shift_by in block_shifts:
        if shift_by == 0:
            k_block, v_block = (own_keys, own_values)
        else:
            k_block, v_block = from_behind((own_keys, own_values), "seq", shift_by)
        key_tiles.append(
            (
                shift_by,
                heads_of(k_block),
                heads_of(v_block),
                image_ids((seq_index - shift_by) * row_count),
            )
        )
    row_top = jnp.full((HEADS, row_count), -jnp.inf, jnp.float32)
    exp_total = jnp.zeros((HEADS, row_count), jnp.float32)
    for shift_by, k_heads, v_heads, k_ids in key_tiles:
        scores, allowed = tile_scores(q_heads, own_ids, k_heads, k_ids)
        new_top = jnp.maximum(row_top, jnp.max(jnp.where(allowed, scores, -jnp.inf), axis=2))
        exp_total = exp_total * jnp.exp(row_top - new_top) + jnp.sum(
            jnp.where(allowed, jnp.exp(scores - new_top[:, :, None]), 0.0), axis=2
        )
        row_top = new_top
    log_total = row_top + jnp.log(exp_total)
    mixed = jnp.zeros((row_count, HEADS, HEAD_DIM), jnp.float32)
    for shift_by, k_heads, v_heads, k_ids in key_tiles:
        scores, allowed = tile_scores(q_heads, own_ids, k_heads, k_ids)
        probs = jnp.where(allowed, jnp.exp(scores - log_total[:, :, None]), 0.0).astype(
            jnp.bfloat16
        )
        mixed = mixed + jnp.einsum(
            "hqk,khd->qhd", probs, v_heads, preferred_element_type=jnp.float32
        )
    attn = mixed.astype(jnp.bfloat16).reshape(row_count, model_width)
    d_attn = jnp.dot(own_grads, out_proj, preferred_element_type=jnp.float32).astype(jnp.bfloat16)
    do_heads = heads_of(d_attn)
    row_dots = jnp.einsum(
        "qhd,qhd->hq", do_heads.astype(jnp.float32), heads_of(attn).astype(jnp.float32)
    )
    proj_share = lax.psum_scatter(
        jnp.dot(jnp.transpose(own_grads), attn, preferred_element_type=jnp.float32),
        "seq",
        scatter_dimension=0,
        tiled=True,
    )
    grad_proj = lax.psum(proj_share, "dp")
    grad_q = jnp.zeros((row_count, HEADS, HEAD_DIM), jnp.float32)
    grad_k = jnp.zeros((row_count, HEADS, HEAD_DIM), jnp.float32)
    grad_v = jnp.zeros((row_count, HEADS, HEAD_DIM), jnp.float32)
    for shift_by, k_heads, v_heads, k_ids in key_tiles:
        probs, dscore = tile_grads(
            q_heads, own_ids, do_heads, log_total, row_dots, k_heads, v_heads, k_ids
        )
        grad_q = grad_q + jnp.einsum(
            "hqk,khd->qhd", dscore, k_heads, preferred_element_type=jnp.float32
        )
        key_part = jnp.einsum("hqk,qhd->khd", dscore, q_heads, preferred_element_type=jnp.float32)
        value_part = jnp.einsum("hqk,qhd->khd", probs, do_heads, preferred_element_type=jnp.float32)
        if shift_by != 0:
            key_part, value_part = from_behind((key_part, value_part), "seq", -shift_by)
        grad_k = grad_k + key_part
        grad_v = grad_v + value_part
    grad_query = grad_q.astype(jnp.bfloat16).reshape(1, row_count, model_width)
    grad_key = grad_k.astype(jnp.bfloat16).reshape(1, row_count, model_width)
    grad_value = grad_v.astype(jnp.bfloat16).reshape(1, row_count, model_width)
    return (grad_query, grad_key, grad_value, grad_proj)


def solution(mesh):
    placed = (
        P("dp", "seq", None),
        P("dp", "seq", None),
        P("dp", "seq", None),
        P("dp", "seq", None),
        P(),
        P("dp", None),
    )
    return jax.shard_map(
        per_device,
        mesh=mesh,
        in_specs=placed,
        out_specs=(
            P("dp", "seq", None),
            P("dp", "seq", None),
            P("dp", "seq", None),
            P("seq", None),
        ),
        check_vma=False,
    )
```

profile of v0, /device:TPU:1, one launch (start us, length us, event | category | flops | bytes accessed | tf_op | source)
XLA Modules:
  0.0 573.2 jit_solution(15690076021697331054)
XLA Ops:
  8.7 7.0 %collective-permute-start.2 = (bf16[256,1152]{1,0:T(8,128)(2,1)}, bf16[256,1152]{1,0:T(8,128)(2,1)}, u32[]{:S(2)}, u32[]{:S(2)}) collective-permute-start(bf16[256,1152]{1,0:T(8,128)(2,1)} %bitcast.171), channel_id=1, source_target_pairs={{0,2},{1,3},{2,4},{3,5},{4,6},{5,7},{6,8},{7,9},{8,10},{9,11},{10,... | collective-permute-start | bytes 1769480 | tf_op jit(solution)/shard_map/ppermute | solution.py:14
  16.9 4.8 collective-permute-start
  21.7 3.4 collective-permute-start.4
  31.8 2.9 convolution_convert_fusion
  42.4 6.5 %collective-permute-start.6 = (bf16[256,1152]{1,0:T(8,128)(2,1)}, bf16[256,1152]{1,0:T(8,128)(2,1)}, u32[]{:S(2)}, u32[]{:S(2)}) collective-permute-start(bf16[256,1152]{1,0:T(8,128)(2,1)} %bitcast.15), channel_id=1, source_target_pairs={{0,2},{1,3},{2,4},{3,5},{4,6},{5,7},{6,8},{7,9},{8,10},{9,11},{10,... | collective-permute-start | bytes 1769480 | tf_op jit(solution)/shard_map/ppermute | solution.py:14
  52.9 2.8 select_reduce_fusion.5
  58.6 2.9 select_reduce_fusion.6
  61.5 2.8 select_reduce_fusion.7
  84.0 5.6 collective-permute-start.13
  90.9 4.3 fusion.28
  97.3 4.2 fusion.25
  101.5 6.6 %collective-permute-start.15 = (f32[256,16,72]{0,2,1:T(8,128)}, f32[256,16,72]{0,2,1:T(8,128)}, u32[]{:S(2)}, u32[]{:S(2)}) collective-permute-start(f32[256,16,72]{0,2,1:T(8,128)} %convolution_bitcast_fusion.1), channel_id=1, source_target_pairs={{0,2},{1,3},{2,4},{3,5},{4,6},{5,7},{6,8},{7,9},{8,10},{9,11},{10,... | collective-permute-start | bytes 3538952 | tf_op jit(solution)/shard_map/ppermute | solution.py:14
  109.4 3.6 convolution_add_fusion.3
  115.2 4.3 fusion.21
  119.6 2.7 multiply_convert_fusion.2
  122.3 3.3 convolution_bitcast_fusion
  127.5 5.7 collective-permute-start.9
  133.2 4.1 multiply_convert_fusion.1
  153.6 6.7 %collective-permute-start.11 = (f32[256,16,72]{0,2,1:T(8,128)}, f32[256,16,72]{0,2,1:T(8,128)}, u32[]{:S(2)}, u32[]{:S(2)}) collective-permute-start(f32[256,16,72]{0,2,1:T(8,128)} %convolution_bitcast_fusion.6), channel_id=1, source_target_pairs={{0,2},{1,3},{2,4},{3,5},{4,6},{5,7},{6,8},{7,9},{8,10},{9,11},{10,... | collective-permute-start | bytes 3538952 | tf_op jit(solution)/shard_map/ppermute | solution.py:14
  163.9 5.5 fusion.18
  169.4 333.2 %all-reduce.6.cloned.1.call-done = f32[1152,1152]{0,1:T(8,128)} async-done(((f32[1152,1152]{0,1:T(8,128)}), f32[1152,1152]{0,1:T(8,128)}) %all-reduce.6.cloned.1.call-update) | async-done | bytes 5308432
  502.6 2.3 constant_dynamic-slice_fusion
  505.0 4.7 fusion.17
  514.0 50.2 %all-reduce.4.cloned.1.call-done = f32[36,1152]{0,1:T(8,128)} async-done(((f32[36,1152]{0,1:T(8,128)}), f32[36,1152]{0,1:T(8,128)}) %all-reduce.4.cloned.1.call-update) | async-done | bytes 165904 | tf_op jit(solution)/shard_map/psum | solution.py:105
  (152 shorter events, 77.5 us)
Async XLA Ops:
  7.2 24.6 %copy-start = (bf16[1152,1152]{1,0:T(8,128)(2,1)S(1)}, bf16[1152,1152]{1,0:T(8,128)(2,1)}, u32[]{:S(2)}) copy-start(bf16[1152,1152]{1,0:T(8,128)(2,1)} %param.10) | copy-start | bytes 7962628
  7.2 495.4 %all-reduce.6.cloned.1.call-start = ((), (), s32[]{:S(2)}) async-start(), calls=%async_computation.1 | async-start | bytes 10616832
  7.2 35.2 %collective-permute-start.3 = (bf16[256,1152]{1,0:T(8,128)(2,1)}, bf16[256,1152]{1,0:T(8,128)(2,1)}, u32[]{:S(2)}, u32[]{:S(2)}) collective-permute-start(bf16[256,1152]{1,0:T(8,128)(2,1)} %bitcast.170), channel_id=1, source_target_pairs={{2,0},{3,1},{4,2},{5,3},{6,4},{7,5},{8,6},{9,7},{10,8},{11,9},{12,... | collective-permute-start | bytes 1769480 | tf_op jit(solution)/shard_map/ppermute | solution.py:14
  8.7 41.6 %collective-permute-start.2 = (bf16[256,1152]{1,0:T(8,128)(2,1)}, bf16[256,1152]{1,0:T(8,128)(2,1)}, u32[]{:S(2)}, u32[]{:S(2)}) collective-permute-start(bf16[256,1152]{1,0:T(8,128)(2,1)} %bitcast.171), channel_id=1, source_target_pairs={{0,2},{1,3},{2,4},{3,5},{4,6},{5,7},{6,8},{7,9},{8,10},{9,11},{10,... | collective-permute-start | bytes 1769480 | tf_op jit(solution)/shard_map/ppermute | solution.py:14
  15.6 40.1 %collective-permute-start.1 = (bf16[256,1152]{1,0:T(8,128)(2,1)}, bf16[256,1152]{1,0:T(8,128)(2,1)}, u32[]{:S(2)}, u32[]{:S(2)}) collective-permute-start(bf16[256,1152]{1,0:T(8,128)(2,1)} %bitcast.172), channel_id=1, source_target_pairs={{1,0},{2,1},{3,2},{4,3},{5,4},{6,5},{7,6},{8,7},{9,8},{10,9},{11,1... | collective-permute-start | bytes 1769480 | tf_op jit(solution)/shard_map/ppermute | solution.py:14
  16.9 47.4 %collective-permute-start = (bf16[256,1152]{1,0:T(8,128)(2,1)}, bf16[256,1152]{1,0:T(8,128)(2,1)}, u32[]{:S(2)}, u32[]{:S(2)}) collective-permute-start(bf16[256,1152]{1,0:T(8,128)(2,1)} %bitcast.173), channel_id=1, source_target_pairs={{0,1},{1,2},{2,3},{3,4},{4,5},{5,6},{6,7},{7,8},{8,9},{9,10},{10,1... | collective-permute-start | bytes 1769480 | tf_op jit(solution)/shard_map/ppermute | solution.py:14
  21.7 79.8 %collective-permute-start.4 = (bf16[256,1152]{1,0:T(8,128)(2,1)}, bf16[256,1152]{1,0:T(8,128)(2,1)}, u32[]{:S(2)}, u32[]{:S(2)}) collective-permute-start(bf16[256,1152]{1,0:T(8,128)(2,1)} %bitcast.15), channel_id=1, source_target_pairs={{0,1},{1,2},{2,3},{3,4},{4,5},{5,6},{6,7},{7,8},{8,9},{9,10},{10,1... | collective-permute-start | bytes 1769480 | tf_op jit(solution)/shard_map/ppermute | solution.py:14
  36.0 79.2 %copy-start.13 = (bf16[256,1152]{0,1:T(8,128)(2,1)}, bf16[256,1152]{0,1:T(8,128)(2,1)S(1)}, u32[]{:S(2)}) copy-start(bf16[256,1152]{0,1:T(8,128)(2,1)S(1)} %copy.163) | copy-start | bytes 1769476
  42.4 41.5 %collective-permute-start.6 = (bf16[256,1152]{1,0:T(8,128)(2,1)}, bf16[256,1152]{1,0:T(8,128)(2,1)}, u32[]{:S(2)}, u32[]{:S(2)}) collective-permute-start(bf16[256,1152]{1,0:T(8,128)(2,1)} %bitcast.15), channel_id=1, source_target_pairs={{0,2},{1,3},{2,4},{3,5},{4,6},{5,7},{6,8},{7,9},{8,10},{9,11},{10,... | collective-permute-start | bytes 1769480 | tf_op jit(solution)/shard_map/ppermute | solution.py:14
  50.3 44.9 %collective-permute-start.7 = (bf16[256,1152]{1,0:T(8,128)(2,1)}, bf16[256,1152]{1,0:T(8,128)(2,1)S(1)}, u32[]{:S(2)}, u32[]{:S(2)}) collective-permute-start(bf16[256,1152]{1,0:T(8,128)(2,1)} %bitcast.15), channel_id=1, source_target_pairs={{2,0},{3,1},{4,2},{5,3},{6,4},{7,5},{8,6},{9,7},{10,8},{11,9},{12,... | collective-permute-start | bytes 1769480 | tf_op jit(solution)/shard_map/ppermute | solution.py:14
  55.7 57.3 %collective-permute-start.5 = (bf16[256,1152]{1,0:T(8,128)(2,1)}, bf16[256,1152]{1,0:T(8,128)(2,1)}, u32[]{:S(2)}, u32[]{:S(2)}) collective-permute-start(bf16[256,1152]{1,0:T(8,128)(2,1)} %bitcast.15), channel_id=1, source_target_pairs={{1,0},{2,1},{3,2},{4,3},{5,4},{6,5},{7,6},{8,7},{9,8},{10,9},{11,1... | collective-permute-start | bytes 1769480 | tf_op jit(solution)/shard_map/ppermute | solution.py:14
  80.8 70.2 %collective-permute-start.12 = (f32[256,16,72]{0,2,1:T(8,128)}, f32[256,16,72]{0,2,1:T(8,128)}, u32[]{:S(2)}, u32[]{:S(2)}) collective-permute-start(f32[256,16,72]{0,2,1:T(8,128)} %convolution_bitcast_fusion.4), channel_id=1, source_target_pairs={{1,0},{2,1},{3,2},{4,3},{5,4},{6,5},{7,6},{8,7},{9,8},{10,9},{11,1... | collective-permute-start | bytes 3538952 | tf_op jit(solution)/shard_map/ppermute | solution.py:14
  84.0 68.3 %collective-permute-start.13 = (f32[256,16,72]{0,2,1:T(8,128)}, f32[256,16,72]{0,2,1:T(8,128)}, u32[]{:S(2)}, u32[]{:S(2)}) collective-permute-start(f32[256,16,72]{0,2,1:T(8,128)} %convolution_bitcast_fusion.3), channel_id=1, source_target_pairs={{0,1},{1,2},{2,3},{3,4},{4,5},{5,6},{6,7},{7,8},{8,9},{9,10},{10,1... | collective-permute-start | bytes 3538952 | tf_op jit(solution)/shard_map/ppermute | solution.py:14
  90.9 10.6 %copy-start.30 = (bf16[256,1152]{0,1:T(8,128)(2,1)}, bf16[256,1152]{0,1:T(8,128)(2,1)S(1)}, u32[]{:S(2)}) copy-start(bf16[256,1152]{0,1:T(8,128)(2,1)S(1)} %copy.170) | copy-start | bytes 1769476
  95.2 58.4 %collective-permute-start.14 = (f32[256,16,72]{0,2,1:T(8,128)}, f32[256,16,72]{0,2,1:T(8,128)}, u32[]{:S(2)}, u32[]{:S(2)}) collective-permute-start(f32[256,16,72]{0,2,1:T(8,128)} %convolution_bitcast_fusion.2), channel_id=1, source_target_pairs={{2,0},{3,1},{4,2},{5,3},{6,4},{7,5},{8,6},{9,7},{10,8},{11,9},{12,... | collective-permute-start | bytes 3538952 | tf_op jit(solution)/shard_map/ppermute | solution.py:14
  97.3 12.1 %copy-start.31 = (bf16[256,1152]{0,1:T(8,128)(2,1)}, bf16[256,1152]{0,1:T(8,128)(2,1)S(1)}, u32[]{:S(2)}) copy-start(bf16[256,1152]{0,1:T(8,128)(2,1)S(1)} %copy.172) | copy-start | bytes 1769476
  101.5 62.3 %collective-permute-start.15 = (f32[256,16,72]{0,2,1:T(8,128)}, f32[256,16,72]{0,2,1:T(8,128)}, u32[]{:S(2)}, u32[]{:S(2)}) collective-permute-start(f32[256,16,72]{0,2,1:T(8,128)} %convolution_bitcast_fusion.1), channel_id=1, source_target_pairs={{0,2},{1,3},{2,4},{3,5},{4,6},{5,7},{6,8},{7,9},{8,10},{9,11},{10,... | collective-permute-start | bytes 3538952 | tf_op jit(solution)/shard_map/ppermute | solution.py:14
  125.7 438.5 %all-reduce.4.cloned.1.call-start = ((), (), s32[]{:S(2)}) async-start(), calls=%async_computation | async-start | bytes 1179648 | tf_op jit(solution)/shard_map/psum | solution.py:105
  127.5 377.5 %collective-permute-start.9 = (f32[256,16,72]{0,2,1:T(8,128)}, f32[256,16,72]{0,2,1:T(8,128)}, u32[]{:S(2)}, u32[]{:S(2)}) collective-permute-start(f32[256,16,72]{0,2,1:T(8,128)} %convolution_bitcast_fusion.8), channel_id=1, source_target_pairs={{0,1},{1,2},{2,3},{3,4},{4,5},{5,6},{6,7},{7,8},{8,9},{9,10},{10,1... | collective-permute-start | bytes 3538952 | tf_op jit(solution)/shard_map/ppermute | solution.py:14
  150.0 10.3 %copy-start.18 = (bf16[256,1152]{0,1:T(8,128)(2,1)S(1)}, bf16[256,1152]{0,1:T(8,128)(2,1)}, u32[]{:S(2)}) copy-start(bf16[256,1152]{0,1:T(8,128)(2,1)} %copy-done.17) | copy-start | bytes 1769476
  151.0 354.0 %collective-permute-start.8 = (f32[256,16,72]{0,2,1:T(8,128)}, f32[256,16,72]{0,2,1:T(8,128)}, u32[]{:S(2)}, u32[]{:S(2)}) collective-permute-start(f32[256,16,72]{0,2,1:T(8,128)} %convolution_bitcast_fusion.9), channel_id=1, source_target_pairs={{1,0},{2,1},{3,2},{4,3},{5,4},{6,5},{7,6},{8,7},{9,8},{10,9},{11,1... | collective-permute-start | bytes 3538952 | tf_op jit(solution)/shard_map/ppermute | solution.py:14
  152.3 352.7 %collective-permute-start.10 = (f32[256,16,72]{0,2,1:T(8,128)}, f32[256,16,72]{0,2,1:T(8,128)}, u32[]{:S(2)}, u32[]{:S(2)}) collective-permute-start(f32[256,16,72]{0,2,1:T(8,128)} %convolution_bitcast_fusion.7), channel_id=1, source_target_pairs={{2,0},{3,1},{4,2},{5,3},{6,4},{7,5},{8,6},{9,7},{10,8},{11,9},{12,... | collective-permute-start | bytes 3538952 | tf_op jit(solution)/shard_map/ppermute | solution.py:14
  153.6 351.4 %collective-permute-start.11 = (f32[256,16,72]{0,2,1:T(8,128)}, f32[256,16,72]{0,2,1:T(8,128)}, u32[]{:S(2)}, u32[]{:S(2)}) collective-permute-start(f32[256,16,72]{0,2,1:T(8,128)} %convolution_bitcast_fusion.6), channel_id=1, source_target_pairs={{0,2},{1,3},{2,4},{3,5},{4,6},{5,7},{6,8},{7,9},{8,10},{9,11},{10,... | collective-permute-start | bytes 3538952 | tf_op jit(solution)/shard_map/ppermute | solution.py:14
  505.0 61.1 %copy-start.1 = (bf16[1152,1152]{1,0:T(8,128)(2,1)S(1)}, bf16[1152,1152]{1,0:T(8,128)(2,1)}, u32[]{:S(2)}) copy-start(bf16[1152,1152]{1,0:T(8,128)(2,1)} %param.10) | copy-start | bytes 7962628
  (28 other events, 108.4 us)
Sparse Core Ops, SparseCore 0:
  125.8 376.7 all-reduce.5
  505.3 58.8 all-reduce.3
where the time goes:
time: 579 us; the launch traced here: 573 us
  waiting for transfers between devices  383 us (66%)
  matrix products  75.5 us (13%)
  starting transfers between devices  57.6 us (10%)
  local copies, waits for them, and re-layouts  36 us (6%)
  between operations  15.6 us (3%)
    unnamed x3, waiting for transfers between devices  333 us
    ppermute x16, starting transfers between devices, from_behind(): return lax.ppermute(block, axis, route)  57.6 us
    psum x1, waiting for transfers between devices, per_device(): grad_proj = lax.psum(proj_share, 'dp')  50.2 us
    unnamed x77, local copies, waits for them, and re-layouts  23.8 us
    dot_general x5, matrix products, per_device(): jnp.einsum('hqk,khd->qhd', probs, v_heads, preferred_element_type=jnp.flo...  18.2 us
    dot_general x5, matrix products, per_device(): jnp.einsum('hqk,qhd->khd', probs, do_heads, preferred_element_type=jnp.fl...  13.3 us
    dot_general x5, matrix products, per_device(): jnp.einsum('hqk,qhd->khd', dscore, q_heads, preferred_element_type=jnp.fl...  12 us
  transfers between devices with their start and end apart: 18, of which 2 were waited for; matrix products, arithmetic and copies ran while one was open for 19% of the time, Pallas kernels for 0%

commit v1 on v0

v1 whole, which is shorter than its diff:
```python
import functools
import jax
import jax.numpy as jnp
from jax import lax
from jax.experimental import pallas as pl
from jax.experimental.pallas import tpu as pltpu
from jax.sharding import PartitionSpec as P

HEADS = 16
HEAD_DIM = 72
ROWS = 256
WIDTH = 1152
WINDOW = 512
REACH = 3 * ROWS
PARTS = 2
PART = WIDTH // PARTS
PART_HEADS = HEADS // PARTS
IMAGES = 32
SCALE = HEAD_DIM ** (-0.5)
LOG2E = 1.4426950408889634
FAR = 1e30
BF16 = jnp.bfloat16
F32 = jnp.float32
VMEM_LIMIT = 56 * 1024 * 1024

NN = (((1,), (0,)), ((), ()))
NT = (((1,), (1,)), ((), ()))
TN = (((0,), (0,)), ((), ()))


def dot(a, b, dims):
    return lax.dot_general(a, b, dims, preferred_element_type=F32)


def call(kernel, out_shape, in_specs, scratch, flops, **more):
    whole = pl.BlockSpec(memory_space=pltpu.VMEM)
    return pl.pallas_call(
        kernel,
        out_shape=out_shape,
        in_specs=[whole if s is None else s for s in in_specs],
        out_specs=jax.tree.map(lambda _: whole, out_shape),
        scratch_shapes=scratch,
        compiler_params=pltpu.CompilerParams(vmem_limit_bytes=VMEM_LIMIT),
        cost_estimate=pl.CostEstimate(flops=flops, bytes_accessed=8 << 20, transcendentals=0),
        **more,
    )


def turn_kernel(q_ref, k_ref, v_ref, *out_refs):
    for at, ref in enumerate((q_ref, k_ref, v_ref)):
        turned = jnp.transpose(ref[...])
        for part in range(PARTS):
            out_refs[part][at * PART : (at + 1) * PART, :] = turned[part * PART : (part + 1) * PART]


def turn(q, k, v):
    shape = jax.ShapeDtypeStruct((3 * PART, ROWS), BF16)
    return call(turn_kernel, (shape,) * PARTS, [None] * 3, [], 1 << 20)(q, k, v)


def attend_kernel(
    place_ref, length_ref, qkv_l, qkv_c, qkv_r, go_l, go_c, go_r, proj_ref,
    attn_ref, back_l, back_c, back_r,
    held, d_attn, result, member, bias,
):
    mine = place_ref[0]
    first = (mine - 1) * ROWS

    def scan(i, carry):
        start, low = carry
        end = start + length_ref[0, i]
        owned = (start + end) // 2 // ROWS == mine
        low = jnp.where(owned, jnp.minimum(low, start - first), low)
        return end, low

    _, low = lax.fori_loop(0, IMAGES, scan, (jnp.int32(0), jnp.int32(REACH - WINDOW)))
    positions = first + low + lax.broadcasted_iota(jnp.int32, (1, WINDOW), 1)

    def mark(i, start):
        end = start + length_ref[0, i]
        owned = (start + end) // 2 // ROWS == mine
        inside = (positions >= start) & (positions < end) & owned
        member[pl.ds(i, 1), :] = jnp.where(inside, 1.0, 0.0)
        return end

    lax.fori_loop(0, IMAGES, mark, jnp.int32(0))
    marks = member[...]
    own = jnp.sum(marks, axis=0, keepdims=True)
    marks = marks.astype(BF16)
    bias[...] = (dot(marks, marks, TN) - 1.0) * FAR
    back_by = REACH - low

    def window(array):
        return pltpu.roll(array.astype(F32), back_by, 1)[:, :WINDOW]

    for at in range(3):
        rows = slice(at * PART, (at + 1) * PART)
        joined = jnp.concatenate([qkv_l[rows, :], qkv_c[rows, :], qkv_r[rows, :]], axis=1)
        held[rows, :] = window(joined).astype(BF16)
    turned = jnp.concatenate(
        [dot(proj_ref[...], ref[...], NT).astype(BF16) for ref in (go_l, go_c, go_r)], axis=1
    )
    d_attn[...] = (window(turned) * own).astype(BF16)

    def head(q, k, v, do):
        scores = dot(k, q, TN) + bias[...]
        top = jnp.max(scores, axis=0, keepdims=True)
        weights = jnp.exp2((scores - top) * (SCALE * LOG2E))
        inverse = 1.0 / jnp.sum(weights, axis=0, keepdims=True)
        weights = weights.astype(BF16)
        attn = (dot(v, weights, NN) * (inverse * own)).astype(BF16)
        do = (do.astype(F32) * inverse).astype(BF16)
        dots = jnp.sum(do.astype(F32) * attn.astype(F32), axis=0, keepdims=True)
        dscore = (weights.astype(F32) * (dot(v, do, TN) - dots)).astype(BF16)
        return (
            attn,
            (dot(k, dscore, NN) * SCALE).astype(BF16),
            (dot(q, dscore, NT) * SCALE).astype(BF16),
            dot(do, weights, NT).astype(BF16),
        )

    def pair(at, _):
        base = pl.multiple_of(at * 2 * HEAD_DIM, 2 * HEAD_DIM)
        slabs = [held[pl.ds(a * PART + base, 2 * HEAD_DIM), :] for a in range(3)]
        slabs.append(d_attn[pl.ds(base, 2 * HEAD_DIM), :])
        both = [head(*(s[h * HEAD_DIM : (h + 1) * HEAD_DIM] for s in slabs)) for h in range(2)]
        joined = [jnp.concatenate([one, two], axis=0) for one, two in zip(*both)]
        for a in range(4):
            result[pl.ds(a * PART + base, 2 * HEAD_DIM), :] = joined[a]
        return 0

    lax.fori_loop(0, PART_HEADS // 2, pair, 0)

    for at in range(4):
        found = result[at * PART : (at + 1) * PART, :].astype(F32)
        wide = jnp.concatenate([found, jnp.zeros((PART, REACH - WINDOW), F32)], axis=1)
        wide = pltpu.roll(wide, low, 1).astype(BF16)
        if at == 0:
            attn_ref[...] = wide
        else:
            rows = slice((at - 1) * PART, at * PART)
            back_l[rows, :] = wide[:, :ROWS]
            back_c[rows, :] = wide[:, ROWS : 2 * ROWS]
            back_r[rows, :] = wide[:, 2 * ROWS :]


def attend(place, lengths, qkv, go, proj):
    block = jax.ShapeDtypeStruct((3 * PART, ROWS), BF16)
    scalar = pl.BlockSpec(memory_space=pltpu.SMEM)
    return call(
        attend_kernel,
        (jax.ShapeDtypeStruct((PART, REACH), BF16), block, block, block),
        [scalar, scalar] + [None] * 7,
        [
            pltpu.VMEM((3 * PART, WINDOW), BF16),
            pltpu.VMEM((PART, WINDOW), BF16),
            pltpu.VMEM((4 * PART, WINDOW), BF16),
            pltpu.VMEM((IMAGES, WINDOW), F32),
            pltpu.VMEM((WINDOW, WINDOW), F32),
        ],
        12 * 10**9,
    )(place, lengths, *qkv, *go, proj)


def finish_kernel(*refs):
    terms, outs = refs[: 3 * PARTS], refs[3 * PARTS :]
    for at in range(3):
        rows = slice(at * PART, (at + 1) * PART)
        whole = []
        for part in range(PARTS):
            one, two, three = (ref[rows, :].astype(F32) for ref in terms[3 * part : 3 * part + 3])
            whole.append((one + two + three).astype(BF16))
        outs[at][...] = jnp.transpose(jnp.concatenate(whole, axis=0))


def finish(terms):
    shape = jax.ShapeDtypeStruct((ROWS, WIDTH), BF16)
    return call(finish_kernel, (shape,) * 3, [None] * (3 * PARTS), [], 1 << 20)(*terms)


def send(block, axis, pairs):
    return lax.ppermute(block, axis, pairs)


def reduce_proj(part):
    seq, dp = lax.axis_index("seq"), lax.axis_index("dp")
    core, z, y, x = dp % 2, seq // 8, (seq // 4) % 2, seq % 4
    part = part.reshape(4, 2, 144, WIDTH)
    cores = [(i, i ^ 1) for i in range(4)]
    pick = lambda a, i, axis: lax.dynamic_index_in_dim(a, i, axis, keepdims=False)
    total = pick(part, core, 1) + send(pick(part, 1 - core, 1).astype(BF16), "dp", cores).astype(F32)
    for step, place, count in ((8, z, 4), (1, x, 4)):
        if step == 1:
            total = total.reshape(4, 36, WIDTH)
        summed = pick(total, place, 0)
        for k in range(1, count):
            ring = [
                (i, i - (i // step % 4) * step + ((i // step + k) % 4) * step) for i in range(32)
            ]
            summed = summed + send(pick(total, (place + k) % 4, 0).astype(BF16), "seq", ring).astype(F32)
        total = summed
    total = total + send(total, "seq", [(i, i ^ 4) for i in range(32)])
    total = total + send(total, "dp", [(i, i ^ 2) for i in range(4)])
    other = send(total, "dp", cores)
    return jnp.where(core == y, total, other)


def per_device(query, key, value, grad_out, out_proj, lengths):
    count = lax.axis_size("seq")
    ahead = [(i, i + 1) for i in range(count - 1)]
    behind = [(i + 1, i) for i in range(count - 1)]
    place = lax.axis_index("seq").reshape(1)

    def around(block):
        return send(block, "seq", ahead), block, send(block, "seq", behind)

    go = around(grad_out[0])
    halves = [around(half) for half in turn(query[0], key[0], value[0])]
    proj = jnp.transpose(out_proj)
    terms, attn = [], []
    for part in range(PARTS):
        mine = proj[part * PART : (part + 1) * PART]
        found, back_l, back_c, back_r = attend(place, lengths, halves[part], go, mine)
        attn.append(found)
        terms += [send(back_r, "seq", ahead), back_c, send(back_l, "seq", behind)]
    attn = jnp.concatenate(attn, axis=0)
    part = dot(jnp.concatenate(go, axis=0), attn, (((0,), (1,)), ((), ())))
    grad_proj = reduce_proj(part)
    grads = [g[None] for g in finish(terms)]
    return (*grads, grad_proj)


def solution(mesh):
    rows = P("dp", "seq", None)
    return jax.shard_map(
        per_device,
        mesh=mesh,
        in_specs=(rows, rows, rows, rows, P(), P("dp", None)),
        out_specs=(rows, rows, rows, P("seq", None)),
        check_vma=False,
    )
```

time: 579 us -> 195 us (0.34)
  waiting for transfers between devices: 383 us -> 72.6 us
  matrix products: 75.5 us -> 4.03 us
  Pallas kernels: 0 us -> 46.9 us
  local copies, waits for them, and re-layouts: 36 us -> 13.3 us
  between operations: 15.6 us -> 0.86 us
  starting transfers between devices: 57.6 us -> 49.8 us
    unnamed x3 -> x0, waiting for transfers between devices: 333 us -> none
    ppermute x16 -> x20, waiting for transfers between devices: 0.04 us -> 72.6 us  [send(): return lax.ppermute(block, axis, pairs)]
    dot_general x32 -> x1, matrix products: 75.5 us -> 4.03 us  [dot(): return lax.dot_general(a, b, dims, preferred_element_type=F32)]
    psum x1 -> x0, waiting for transfers between devices: 50.2 us -> none  [per_device(): grad_proj = lax.psum(proj_share, 'dp')]
    pallas_call x0 -> x4, Pallas kernels: none -> 46.9 us  [the longest x2 39.8 us: attend(): call(attend_kernel, (jax.ShapeDtypeStruct((PART, REACH), BF16), block, bl...]
    unnamed x77 -> x19, local copies, waits for them, and re-layouts: 23.8 us -> 9.81 us
    ppermute x8 -> x0, local copies, waits for them, and re-layouts: 10.2 us -> none  [from_behind(): return lax.ppermute(block, axis, route)]
    ppermute x16 -> x20, starting transfers between devices: 57.6 us -> 49.8 us  [send(): return lax.ppermute(block, axis, pairs)]
  transfers between devices with their start and end apart: 18 -> 20, of which waited for: 2 -> 7; matrix products, arithmetic and copies ran while one was open for 19% -> 4% of each run, Pallas kernels for 0% -> 12%
where the time goes in v1:
time: 195 us; the launch traced here: 193 us
  waiting for transfers between devices  72.6 us (37%)
  starting transfers between devices  49.8 us (26%)
  Pallas kernels  46.9 us (24%)
  local copies, waits for them, and re-layouts  13.3 us (7%)
  other arithmetic  5.47 us (3%)
  matrix products  4.03 us (2%)
    ppermute x20, waiting for transfers between devices, send(): return lax.ppermute(block, axis, pairs)  72.6 us
    ppermute x20, starting transfers between devices, send(): return lax.ppermute(block, axis, pairs)  49.8 us
    pallas_call x2, Pallas kernels, attend(): call(attend_kernel, (jax.ShapeDtypeStruct((PART, REACH), BF16), block, bl...  39.8 us
    unnamed x19, local copies, waits for them, and re-layouts  9.81 us
    pallas_call x1, Pallas kernels, finish(): call(finish_kernel, (shape,) * 3, [None] * (3 * PARTS), [], 1 << 20)(*terms)  4.05 us
    dot_general x1, matrix products, dot(): return lax.dot_general(a, b, dims, preferred_element_type=F32)  4.03 us
  transfers between devices with their start and end apart: 20, of which 7 were waited for; matrix products, arithmetic and copies ran while one was open for 4% of the time, Pallas kernels for 12%

profile of v1, /device:TPU:1, one launch (start us, length us, event | category | flops | bytes accessed | tf_op | source)
XLA Modules:
  0.0 192.9 jit_solution(12817767430152724303)
XLA Ops:
  0.6 3.1 %shard_map.93 = (bf16[1728,256]{1,0:T(8,128)(2,1)}, bf16[1728,256]{1,0:T(8,128)(2,1)}) custom-call(bf16[256,1152]{1,0:T(8,128)(2,1)} %bitcast.45, bf16[256,1152]{1,0:T(8,128)(2,1)} %bitcast.46, bf16[256,1152]{1,0:T(8,128)(2,1)} %bitcast.47), custom_call_target="tpu_custom_call" | custom-call | flops 1048576 | bytes 8388608 | tf_op jit(solution)/shard_map/pallas_call | solution.py:58
  3.7 4.0 %collective-permute-start = (bf16[1728,256]{1,0:T(8,128)(2,1)}, bf16[1728,256]{1,0:T(8,128)(2,1)S(1)}, u32[]{:S(2)}, u32[]{:S(2)}) collective-permute-start(bf16[1728,256]{1,0:T(8,128)(2,1)} %get-tuple-element.17.qkv_c), channel_id=1, source_target_pairs={{0,1},{1,2},{2,3},{3,4},{4,5},{5,6},{6,7},{7,8},{8,9},{9,10},{10,1... | collective-permute-start | bytes 2654216 | tf_op jit(solution)/shard_map/ppermute | solution.py:182
  9.0 4.8 %collective-permute-start.2 = (bf16[256,1152]{1,0:T(8,128)(2,1)}, bf16[256,1152]{1,0:T(8,128)(2,1)}, u32[]{:S(2)}, u32[]{:S(2)}) collective-permute-start(bf16[256,1152]{1,0:T(8,128)(2,1)} %bitcast.48), channel_id=1, source_target_pairs={{0,1},{1,2},{2,3},{3,4},{4,5},{5,6},{6,7},{7,8},{8,9},{9,10},{10,1... | collective-permute-start | bytes 1769480 | tf_op jit(solution)/shard_map/ppermute | solution.py:182
  15.1 5.0 %collective-permute-start.6 = (bf16[1728,256]{1,0:T(8,128)(2,1)}, bf16[1728,256]{1,0:T(8,128)(2,1)}, u32[]{:S(2)}, u32[]{:S(2)}) collective-permute-start(bf16[1728,256]{1,0:T(8,128)(2,1)} %get-tuple-element.21.qkv_c), channel_id=1, source_target_pairs={{0,1},{1,2},{2,3},{3,4},{4,5},{5,6},{6,7},{7,8},{8,9},{9,10},{10,1... | collective-permute-start | bytes 2654216 | tf_op jit(solution)/shard_map/ppermute | solution.py:182
  20.1 4.1 %copy.11 = bf16[1152,1152]{0,1:T(8,128)(2,1)S(1)} copy(bf16[1152,1152]{1,0:T(8,128)(2,1)} %param.10) | data formatting | bytes 5308416 | tf_op args[4]
  26.0 12.9 %collective-permute-done.2.go_l = bf16[256,1152]{1,0:T(8,128)(2,1)} collective-permute-done((bf16[256,1152]{1,0:T(8,128)(2,1)}, bf16[256,1152]{1,0:T(8,128)(2,1)}, u32[]{:S(2)}, u32[]{:S(2)}) %collective-permute-start.2) | collective-permute-done | bytes 589856 | tf_op jit(solution)/shard_map/ppermute | solution.py:182
  40.2 2.6 %collective-permute-done.3.go_r = bf16[256,1152]{1,0:T(8,128)(2,1)} collective-permute-done((bf16[256,1152]{1,0:T(8,128)(2,1)}, bf16[256,1152]{1,0:T(8,128)(2,1)}, u32[]{:S(2)}, u32[]{:S(2)}) %collective-permute-start.3) | collective-permute-done | bytes 589856 | tf_op jit(solution)/shard_map/ppermute | solution.py:182
  43.7 19.8 %shard_map.94 = (bf16[576,768]{1,0:T(8,128)(2,1)}, bf16[1728,256]{1,0:T(8,128)(2,1)}, bf16[1728,256]{1,0:T(8,128)(2,1)}, bf16[1728,256]{1,0:T(8,128)(2,1)}) custom-call(s32[1]{0:T(128)} %bitcast.place_ref, s32[1,32]{1,0:T(1,128)} %length_ref.3, bf16[1728,256]{1,0:T(8,128)(2,1)} %copy-done.5, bf16[1728,256]{1,0:T(8,128)(2,1)} %get-tuple-element.17.qkv_c, ...), custom_call_target="tpu_custom_call" | custom-call | flops 12000000000 | bytes 8388608 | tf_op jit(solution)/shard_map/pallas_call | solution.py:150
  64.4 20.0 %shard_map.95 = (bf16[576,768]{1,0:T(8,128)(2,1)}, bf16[1728,256]{1,0:T(8,128)(2,1)}, bf16[1728,256]{1,0:T(8,128)(2,1)}, bf16[1728,256]{1,0:T(8,128)(2,1)}) custom-call(s32[1]{0:T(128)} %bitcast.place_ref, s32[1,32]{1,0:T(1,128)} %length_ref.3, bf16[1728,256]{1,0:T(8,128)(2,1)} %collective-permute-done.6.qkv_l, bf16[1728,256]{1,0:T(8,128)(2,1)} %get-tuple-element.21.qkv_c, ...), custom_call_target="tpu_custom_call" | custom-call | flops 12000000000 | bytes 8388608 | tf_op jit(solution)/shard_map/pallas_call | solution.py:150
  84.4 4.0 %fusion = f32[1152,1152]{1,0:T(8,128)S(1)} fusion(bf16[256,1152]{1,0:T(8,128)(2,1)} %collective-permute-done.3.go_r, bf16[256,1152]{1,0:T(8,128)(2,1)S(1)} %bitcast.52, bf16[256,1152]{1,0:T(8,128)(2,1)} %collective-permute-done.2.go_l, bf16[576,768]{1,0:T(8,128)(2,1)} %get-tuple-element.29, bf16[576,768]{1,0:T(8,128)(2,1)S(1)} %copy-done.8), kind=kOutput, calls=%fused_computation.2 | convolution fusion | flops 2047279104 | bytes 8847360 | tf_op jit(solution)/shard_map/dot_general | solution.py:32
  88.5 2.4 %copy-done = f32[1152,1152]{1,0:T(8,128)} copy-done((f32[1152,1152]{1,0:T(8,128)}, f32[1152,1152]{1,0:T(8,128)S(1)}, u32[]{:S(2)}) %copy-start) | copy-done | bytes 5308440
  91.0 1.9 %collective-permute-start.10 = (bf16[4,144,1152]{2,1,0:T(8,128)(2,1)S(1)}, bf16[4,144,1152]{2,1,0:T(8,128)(2,1)}, u32[]{:S(2)}, u32[]{:S(2)}) collective-permute-start(bf16[4,144,1152]{2,1,0:T(8,128)(2,1)S(1)} %fusion.9), channel_id=1, source_target_pairs={{0,32},{32,0},{64,96},{96,64},{1,33},{33,1},{65,97},{97,65},{2,34}... | collective-permute-start | bytes 3981320 | tf_op jit(solution)/shard_map/ppermute | solution.py:182
  92.9 2.8 %collective-permute-done.10 = bf16[4,144,1152]{2,1,0:T(8,128)(2,1)} collective-permute-done((bf16[4,144,1152]{2,1,0:T(8,128)(2,1)S(1)}, bf16[4,144,1152]{2,1,0:T(8,128)(2,1)}, u32[]{:S(2)}, u32[]{:S(2)}) %collective-permute-start.10) | collective-permute-done | bytes 1327136 | tf_op jit(solution)/shard_map/ppermute | solution.py:182
  95.8 2.4 %bitcast_add_fusion = f32[4,144,1152]{2,1,0:T(8,128)S(1)} fusion(bf16[4,144,1152]{2,1,0:T(8,128)(2,1)} %collective-permute-done.10, f32[4,2,144,1152]{3,2,1,0:T(8,128)} %bitcast.44, s32[]{:T(128)S(6)} %select_n.91), kind=kLoop, calls=%fused_computation.1 | loop fusion | flops 1327104 | bytes 6635524 | tf_op jit(solution)/shard_map/add | solution.py:191
  99.0 7.3 %collective-permute-start.13 = (bf16[144,1152]{1,0:T(8,128)(2,1)}, bf16[144,1152]{1,0:T(8,128)(2,1)}, u32[]{:S(2)}, u32[]{:S(2)}) collective-permute-start(bf16[144,1152]{1,0:T(8,128)(2,1)} %get-tuple-element.31), channel_id=1, source_target_pairs={{0,24},{1,25},{2,26},{3,27},{4,28},{5,29},{6,30},{7,31},{8,0},{9,1... | collective-permute-start | bytes 995336 | tf_op jit(solution)/shard_map/ppermute | solution.py:182
  106.9 13.7 %collective-permute-done.13 = bf16[144,1152]{1,0:T(8,128)(2,1)} collective-permute-done((bf16[144,1152]{1,0:T(8,128)(2,1)}, bf16[144,1152]{1,0:T(8,128)(2,1)}, u32[]{:S(2)}, u32[]{:S(2)}) %collective-permute-start.13) | collective-permute-done | bytes 331808 | tf_op jit(solution)/shard_map/ppermute | solution.py:182
  120.5 3.6 %collective-permute-done.11 = bf16[144,1152]{1,0:T(8,128)(2,1)} collective-permute-done((bf16[144,1152]{1,0:T(8,128)(2,1)S(1)}, bf16[144,1152]{1,0:T(8,128)(2,1)}, u32[]{:S(2)}, u32[]{:S(2)}) %collective-permute-start.11) | collective-permute-done | bytes 331808 | tf_op jit(solution)/shard_map/ppermute | solution.py:182
  129.1 2.7 %collective-permute-start.4 = (bf16[1728,256]{1,0:T(8,128)(2,1)}, bf16[1728,256]{1,0:T(8,128)(2,1)S(1)}, u32[]{:S(2)}, u32[]{:S(2)}) collective-permute-start(bf16[1728,256]{1,0:T(8,128)(2,1)} %get-tuple-element.18), channel_id=1, source_target_pairs={{0,1},{1,2},{2,3},{3,4},{4,5},{5,6},{6,7},{7,8},{8,9},{9,10},{10,1... | collective-permute-start | bytes 2654216 | tf_op jit(solution)/shard_map/ppermute | solution.py:182
  133.2 4.0 %collective-permute-start.8 = (bf16[1728,256]{1,0:T(8,128)(2,1)}, bf16[1728,256]{1,0:T(8,128)(2,1)S(1)}, u32[]{:S(2)}, u32[]{:S(2)}) collective-permute-start(bf16[1728,256]{1,0:T(8,128)(2,1)} %get-tuple-element.22), channel_id=1, source_target_pairs={{0,1},{1,2},{2,3},{3,4},{4,5},{5,6},{6,7},{7,8},{8,9},{9,10},{10,1... | collective-permute-start | bytes 2654216 | tf_op jit(solution)/shard_map/ppermute | solution.py:182
  139.6 5.9 %collective-permute-start.17 = (f32[36,1152]{1,0:T(8,128)S(1)}, f32[36,1152]{1,0:T(8,128)S(1)}, u32[]{:S(2)}, u32[]{:S(2)}) collective-permute-start(f32[36,1152]{1,0:T(8,128)S(1)} %fusion.16), channel_id=1, source_target_pairs={{0,4},{1,5},{2,6},{3,7},{4,0},{5,1},{6,2},{7,3},{8,12},{9,13},{10,... | collective-permute-start | bytes 497672 | tf_op jit(solution)/shard_map/ppermute | solution.py:182
  145.5 32.4 %collective-permute-done.17 = f32[36,1152]{1,0:T(8,128)S(1)} collective-permute-done((f32[36,1152]{1,0:T(8,128)S(1)}, f32[36,1152]{1,0:T(8,128)S(1)}, u32[]{:S(2)}, u32[]{:S(2)}) %collective-permute-start.17) | collective-permute-done | bytes 165920 | tf_op jit(solution)/shard_map/ppermute | solution.py:182
  177.9 2.7 %collective-permute-start.18 = (f32[36,1152]{1,0:T(8,128)S(1)}, f32[36,1152]{1,0:T(8,128)S(1)}, u32[]{:S(2)}, u32[]{:S(2)}) collective-permute-start(f32[36,1152]{1,0:T(8,128)S(1)} %add.141), channel_id=1, source_target_pairs={{0,64},{32,96},{64,0},{96,32},{1,65},{33,97},{65,1},{97,33},{2,66}... | collective-permute-start | bytes 497672 | tf_op jit(solution)/shard_map/ppermute | solution.py:182
  180.6 4.6 %collective-permute-done.18 = f32[36,1152]{1,0:T(8,128)S(1)} collective-permute-done((f32[36,1152]{1,0:T(8,128)S(1)}, f32[36,1152]{1,0:T(8,128)S(1)}, u32[]{:S(2)}, u32[]{:S(2)}) %collective-permute-start.18) | collective-permute-done | bytes 165920 | tf_op jit(solution)/shard_map/ppermute | solution.py:182
  188.2 4.1 %shard_map.96 = (bf16[256,1152]{1,0:T(8,128)(2,1)}, bf16[256,1152]{1,0:T(8,128)(2,1)}, bf16[256,1152]{1,0:T(8,128)(2,1)}) custom-call(bf16[1728,256]{1,0:T(8,128)(2,1)} %copy-done.1, bf16[1728,256]{1,0:T(8,128)(2,1)} %get-tuple-element.19.refs_1_, bf16[1728,256]{1,0:T(8,128)(2,1)} %copy-done.2, bf16[1728,256]{1,0:T(8,128)(2,1)} %copy-done.3, ...), custom_call_target="tpu_custom_call" | custom-call | flops 1048576 | bytes 8388608 | tf_op jit(solution)/shard_map/pallas_call | solution.py:178
  (51 shorter events, 21.3 us)
Async XLA Ops:
  3.7 39.0 %collective-permute-start = (bf16[1728,256]{1,0:T(8,128)(2,1)}, bf16[1728,256]{1,0:T(8,128)(2,1)S(1)}, u32[]{:S(2)}, u32[]{:S(2)}) collective-permute-start(bf16[1728,256]{1,0:T(8,128)(2,1)} %get-tuple-element.17.qkv_c), channel_id=1, source_target_pairs={{0,1},{1,2},{2,3},{3,4},{4,5},{5,6},{6,7},{7,8},{8,9},{9,10},{10,1... | collective-permute-start | bytes 2654216 | tf_op jit(solution)/shard_map/ppermute | solution.py:182
  7.7 35.1 %collective-permute-start.1 = (bf16[1728,256]{1,0:T(8,128)(2,1)}, bf16[1728,256]{1,0:T(8,128)(2,1)}, u32[]{:S(2)}, u32[]{:S(2)}) collective-permute-start(bf16[1728,256]{1,0:T(8,128)(2,1)} %get-tuple-element.17.qkv_c), channel_id=1, source_target_pairs={{1,0},{2,1},{3,2},{4,3},{5,4},{6,5},{7,6},{8,7},{9,8},{10,9},{11,1... | collective-permute-start | bytes 2654216 | tf_op jit(solution)/shard_map/ppermute | solution.py:182
  9.0 29.9 %collective-permute-start.2 = (bf16[256,1152]{1,0:T(8,128)(2,1)}, bf16[256,1152]{1,0:T(8,128)(2,1)}, u32[]{:S(2)}, u32[]{:S(2)}) collective-permute-start(bf16[256,1152]{1,0:T(8,128)(2,1)} %bitcast.48), channel_id=1, source_target_pairs={{0,1},{1,2},{2,3},{3,4},{4,5},{5,6},{6,7},{7,8},{8,9},{9,10},{10,1... | collective-permute-start | bytes 1769480 | tf_op jit(solution)/shard_map/ppermute | solution.py:182
  13.8 28.9 %collective-permute-start.3 = (bf16[256,1152]{1,0:T(8,128)(2,1)}, bf16[256,1152]{1,0:T(8,128)(2,1)}, u32[]{:S(2)}, u32[]{:S(2)}) collective-permute-start(bf16[256,1152]{1,0:T(8,128)(2,1)} %bitcast.49), channel_id=1, source_target_pairs={{1,0},{2,1},{3,2},{4,3},{5,4},{6,5},{7,6},{8,7},{9,8},{10,9},{11,1... | collective-permute-start | bytes 1769480 | tf_op jit(solution)/shard_map/ppermute | solution.py:182
  15.1 48.3 %collective-permute-start.6 = (bf16[1728,256]{1,0:T(8,128)(2,1)}, bf16[1728,256]{1,0:T(8,128)(2,1)}, u32[]{:S(2)}, u32[]{:S(2)}) collective-permute-start(bf16[1728,256]{1,0:T(8,128)(2,1)} %get-tuple-element.21.qkv_c), channel_id=1, source_target_pairs={{0,1},{1,2},{2,3},{3,4},{4,5},{5,6},{6,7},{7,8},{8,9},{9,10},{10,1... | collective-permute-start | bytes 2654216 | tf_op jit(solution)/shard_map/ppermute | solution.py:182
  24.3 14.7 %copy-start.4 = (bf16[1728,256]{1,0:T(8,128)(2,1)S(1)}, bf16[1728,256]{1,0:T(8,128)(2,1)}, u32[]{:S(2)}) copy-start(bf16[1728,256]{1,0:T(8,128)(2,1)} %get-tuple-element.21.qkv_c) | copy-start | bytes 2654212
  38.9 24.5 %collective-permute-start.7 = (bf16[1728,256]{1,0:T(8,128)(2,1)S(1)}, bf16[1728,256]{1,0:T(8,128)(2,1)S(1)}, u32[]{:S(2)}, u32[]{:S(2)}) collective-permute-start(bf16[1728,256]{1,0:T(8,128)(2,1)S(1)} %copy-done.4), channel_id=1, source_target_pairs={{1,0},{2,1},{3,2},{4,3},{5,4},{6,5},{7,6},{8,7},{9,8},{10,9},{11,1... | collective-permute-start | bytes 2654216 | tf_op jit(solution)/shard_map/ppermute | solution.py:182
  64.4 20.0 %copy-start.7 = (bf16[1,256,1152]{2,1,0:T(8,128)(2,1)S(1)}, bf16[1,256,1152]{2,1,0:T(8,128)(2,1)}, u32[]{:S(2)}) copy-start(bf16[1,256,1152]{2,1,0:T(8,128)(2,1)} %param.9) | copy-start | bytes 1769476
  64.4 20.0 %copy-start.8 = (bf16[576,768]{1,0:T(8,128)(2,1)S(1)}, bf16[576,768]{1,0:T(8,128)(2,1)}, u32[]{:S(2)}) copy-start(bf16[576,768]{1,0:T(8,128)(2,1)} %get-tuple-element.28) | copy-start | bytes 2654212
  88.5 2.4 %copy-start = (f32[1152,1152]{1,0:T(8,128)}, f32[1152,1152]{1,0:T(8,128)S(1)}, u32[]{:S(2)}) copy-start(f32[1152,1152]{1,0:T(8,128)S(1)} %fusion) | copy-start | bytes 15925252
  91.0 4.8 %collective-permute-start.10 = (bf16[4,144,1152]{2,1,0:T(8,128)(2,1)S(1)}, bf16[4,144,1152]{2,1,0:T(8,128)(2,1)}, u32[]{:S(2)}, u32[]{:S(2)}) collective-permute-start(bf16[4,144,1152]{2,1,0:T(8,128)(2,1)S(1)} %fusion.9), channel_id=1, source_target_pairs={{0,32},{32,0},{64,96},{96,64},{1,33},{33,1},{65,97},{97,65},{2,34}... | collective-permute-start | bytes 3981320 | tf_op jit(solution)/shard_map/ppermute | solution.py:182
  99.0 21.5 %collective-permute-start.13 = (bf16[144,1152]{1,0:T(8,128)(2,1)}, bf16[144,1152]{1,0:T(8,128)(2,1)}, u32[]{:S(2)}, u32[]{:S(2)}) collective-permute-start(bf16[144,1152]{1,0:T(8,128)(2,1)} %get-tuple-element.31), channel_id=1, source_target_pairs={{0,24},{1,25},{2,26},{3,27},{4,28},{5,29},{6,30},{7,31},{8,0},{9,1... | collective-permute-start | bytes 995336 | tf_op jit(solution)/shard_map/ppermute | solution.py:182
  106.3 14.2 %collective-permute-start.12 = (bf16[144,1152]{1,0:T(8,128)(2,1)S(1)}, bf16[144,1152]{1,0:T(8,128)(2,1)}, u32[]{:S(2)}, u32[]{:S(2)}) collective-permute-start(bf16[144,1152]{1,0:T(8,128)(2,1)S(1)} %get-tuple-element.32), channel_id=1, source_target_pairs={{0,16},{1,17},{2,18},{3,19},{4,20},{5,21},{6,22},{7,23},{8,24},{9,... | collective-permute-start | bytes 995336 | tf_op jit(solution)/shard_map/ppermute | solution.py:182
  106.3 17.8 %collective-permute-start.11 = (bf16[144,1152]{1,0:T(8,128)(2,1)S(1)}, bf16[144,1152]{1,0:T(8,128)(2,1)}, u32[]{:S(2)}, u32[]{:S(2)}) collective-permute-start(bf16[144,1152]{1,0:T(8,128)(2,1)S(1)} %get-tuple-element.30), channel_id=1, source_target_pairs={{0,8},{1,9},{2,10},{3,11},{4,12},{5,13},{6,14},{7,15},{8,16},{9,17... | collective-permute-start | bytes 995336 | tf_op jit(solution)/shard_map/ppermute | solution.py:182
  126.2 6.9 %collective-permute-start.16 = (bf16[36,1152]{1,0:T(8,128)(2,1)S(1)}, bf16[36,1152]{1,0:T(8,128)(2,1)}, u32[]{:S(2)}, u32[]{:S(2)}) collective-permute-start(bf16[36,1152]{1,0:T(8,128)(2,1)S(1)} %get-tuple-element.36), channel_id=1, source_target_pairs={{0,3},{1,0},{2,1},{3,2},{4,7},{5,4},{6,5},{7,6},{8,11},{9,8},{10,9... | collective-permute-start | bytes 248840 | tf_op jit(solution)/shard_map/ppermute | solution.py:182
  127.2 10.0 %collective-permute-start.15 = (bf16[36,1152]{1,0:T(8,128)(2,1)}, bf16[36,1152]{1,0:T(8,128)(2,1)}, u32[]{:S(2)}, u32[]{:S(2)}) collective-permute-start(bf16[36,1152]{1,0:T(8,128)(2,1)} %get-tuple-element.37), channel_id=1, source_target_pairs={{0,2},{1,3},{2,0},{3,1},{4,6},{5,7},{6,4},{7,5},{8,10},{9,11},{10,... | collective-permute-start | bytes 248840 | tf_op jit(solution)/shard_map/ppermute | solution.py:182
  129.1 9.4 %collective-permute-start.14 = (bf16[36,1152]{1,0:T(8,128)(2,1)S(1)}, bf16[36,1152]{1,0:T(8,128)(2,1)}, u32[]{:S(2)}, u32[]{:S(2)}) collective-permute-start(bf16[36,1152]{1,0:T(8,128)(2,1)S(1)} %get-tuple-element.35), channel_id=1, source_target_pairs={{0,1},{1,2},{2,3},{3,0},{4,5},{5,6},{6,7},{7,4},{8,9},{9,10},{10,1... | collective-permute-start | bytes 248840 | tf_op jit(solution)/shard_map/ppermute | solution.py:182
  129.1 57.5 %collective-permute-start.4 = (bf16[1728,256]{1,0:T(8,128)(2,1)}, bf16[1728,256]{1,0:T(8,128)(2,1)S(1)}, u32[]{:S(2)}, u32[]{:S(2)}) collective-permute-start(bf16[1728,256]{1,0:T(8,128)(2,1)} %get-tuple-element.18), channel_id=1, source_target_pairs={{0,1},{1,2},{2,3},{3,4},{4,5},{5,6},{6,7},{7,8},{8,9},{9,10},{10,1... | collective-permute-start | bytes 2654216 | tf_op jit(solution)/shard_map/ppermute | solution.py:182
  131.8 54.8 %collective-permute-start.5 = (bf16[1728,256]{1,0:T(8,128)(2,1)}, bf16[1728,256]{1,0:T(8,128)(2,1)S(1)}, u32[]{:S(2)}, u32[]{:S(2)}) collective-permute-start(bf16[1728,256]{1,0:T(8,128)(2,1)} %get-tuple-element.20), channel_id=1, source_target_pairs={{1,0},{2,1},{3,2},{4,3},{5,4},{6,5},{7,6},{8,7},{9,8},{10,9},{11,1... | collective-permute-start | bytes 2654216 | tf_op jit(solution)/shard_map/ppermute | solution.py:182
  133.2 53.5 %collective-permute-start.8 = (bf16[1728,256]{1,0:T(8,128)(2,1)}, bf16[1728,256]{1,0:T(8,128)(2,1)S(1)}, u32[]{:S(2)}, u32[]{:S(2)}) collective-permute-start(bf16[1728,256]{1,0:T(8,128)(2,1)} %get-tuple-element.22), channel_id=1, source_target_pairs={{0,1},{1,2},{2,3},{3,4},{4,5},{5,6},{6,7},{7,8},{8,9},{9,10},{10,1... | collective-permute-start | bytes 2654216 | tf_op jit(solution)/shard_map/ppermute | solution.py:182
  137.2 49.5 %collective-permute-start.9 = (bf16[1728,256]{1,0:T(8,128)(2,1)}, bf16[1728,256]{1,0:T(8,128)(2,1)}, u32[]{:S(2)}, u32[]{:S(2)}) collective-permute-start(bf16[1728,256]{1,0:T(8,128)(2,1)} %get-tuple-element.24), channel_id=1, source_target_pairs={{1,0},{2,1},{3,2},{4,3},{5,4},{6,5},{7,6},{8,7},{9,8},{10,9},{11,1... | collective-permute-start | bytes 2654216 | tf_op jit(solution)/shard_map/ppermute | solution.py:182
  139.6 38.4 %collective-permute-start.17 = (f32[36,1152]{1,0:T(8,128)S(1)}, f32[36,1152]{1,0:T(8,128)S(1)}, u32[]{:S(2)}, u32[]{:S(2)}) collective-permute-start(f32[36,1152]{1,0:T(8,128)S(1)} %fusion.16), channel_id=1, source_target_pairs={{0,4},{1,5},{2,6},{3,7},{4,0},{5,1},{6,2},{7,3},{8,12},{9,13},{10,... | collective-permute-start | bytes 497672 | tf_op jit(solution)/shard_map/ppermute | solution.py:182
  177.9 7.3 %collective-permute-start.18 = (f32[36,1152]{1,0:T(8,128)S(1)}, f32[36,1152]{1,0:T(8,128)S(1)}, u32[]{:S(2)}, u32[]{:S(2)}) collective-permute-start(f32[36,1152]{1,0:T(8,128)S(1)} %add.141), channel_id=1, source_target_pairs={{0,64},{32,96},{64,0},{96,32},{1,65},{33,97},{65,1},{97,33},{2,66}... | collective-permute-start | bytes 497672 | tf_op jit(solution)/shard_map/ppermute | solution.py:182
  185.3 7.0 %collective-permute-start.19 = (f32[36,1152]{1,0:T(8,128)S(1)}, f32[36,1152]{1,0:T(8,128)S(1)}, u32[]{:S(2)}, u32[]{:S(2)}) collective-permute-start(f32[36,1152]{1,0:T(8,128)S(1)} %add.142), channel_id=1, source_target_pairs={{0,32},{32,0},{64,96},{96,64},{1,33},{33,1},{65,97},{97,65},{2,34}... | collective-permute-start | bytes 497672 | tf_op jit(solution)/shard_map/ppermute | solution.py:182
  (5 other events, 5.5 us)

commit v2 on v0

v2 whole, which is shorter than its diff:
```python
import jax
import jax.numpy as jnp
from jax import lax
from jax.experimental import pallas as pl
from jax.experimental.pallas import tpu as pltpu
from jax.sharding import PartitionSpec as P

HEADS = 16
HEAD_DIM = 72
ROWS = 256
WIDTH = 1152
IMAGES = 32
GROUP = 8
PAIR = 2 * HEAD_DIM
SLAB = 4 * PAIR
GRADS = 3 * PAIR
SPAN = GROUP * ROWS
WINDOW = 512
REACH = WINDOW + 128
FRAME = SPAN + WINDOW
EDGE = 2 * WINDOW
SCALE = HEAD_DIM ** (-0.5)
LOG2E = 1.4426950408889634
FAR = 1e30
BF16 = jnp.bfloat16
F32 = jnp.float32
VMEM_LIMIT = 56 * 1024 * 1024

NN = (((1,), (0,)), ((), ()))
NT = (((1,), (1,)), ((), ()))
TN = (((0,), (0,)), ((), ()))
TNT = (((0,), (1,)), ((), ()))
SCALAR = pl.BlockSpec(memory_space=pltpu.SMEM)
WHOLE = pl.BlockSpec(memory_space=pltpu.VMEM)


def dot(a, b, dims):
    return lax.dot_general(a, b, dims, preferred_element_type=F32)


def call(kernel, out_shape, in_specs, scratch, flops):
    return pl.pallas_call(
        kernel,
        out_shape=out_shape,
        in_specs=in_specs,
        out_specs=jax.tree.map(lambda _: WHOLE, out_shape),
        scratch_shapes=scratch,
        compiler_params=pltpu.CompilerParams(vmem_limit_bytes=VMEM_LIMIT),
        cost_estimate=pl.CostEstimate(flops=flops, bytes_accessed=1000, transcendentals=0),
    )


def pack_kernel(q_ref, k_ref, v_ref, go_ref, proj_ref, out_ref, go_out):
    go = jnp.transpose(go_ref[...])
    for g in range(GROUP):
        for z in range(4):
            at = (2 * z + g // 4) * PAIR
            go_out[g, z * PAIR : (z + 1) * PAIR, :] = go[at : at + PAIR]
    d_attn = dot(proj_ref[...], go, TN).astype(BF16)
    turned = [jnp.transpose(ref[...]) for ref in (q_ref, k_ref, v_ref)] + [d_attn]
    for at in range(4):
        for g in range(GROUP):
            out_ref[g, at * PAIR : (at + 1) * PAIR, :] = turned[at][g * PAIR : (g + 1) * PAIR]


def pack(q, k, v, go, proj):
    shape = jax.ShapeDtypeStruct((GROUP, SLAB, ROWS), BF16)
    return call(pack_kernel, (shape, shape), [WHOLE] * 5, [], 4 * 10**9)(q, k, v, go, proj)


def attend(slab, marks):
    own = jnp.sum(marks, axis=0, keepdims=True)
    marks = marks.astype(BF16)
    bias = (dot(marks, marks, TN) - 1.0) * FAR
    heads = []
    for h in range(2):
        q, k, v, do = (
            slab[a * PAIR + h * HEAD_DIM : a * PAIR + (h + 1) * HEAD_DIM] for a in range(4)
        )
        heads.append((q, k.astype(BF16), v.astype(BF16), do * own))
    scores = [dot(k, q.astype(BF16), TN) + bias for q, k, v, do in heads]
    dprob = [dot(v, do.astype(BF16), TN) for q, k, v, do in heads]
    found = [[], [], [], []]
    for h, (q, k, v, do) in enumerate(heads):
        top = jnp.max(scores[h], axis=0, keepdims=True)
        weights = jnp.exp2((scores[h] - top) * (SCALE * LOG2E))
        inverse = 1.0 / jnp.sum(weights, axis=0, keepdims=True)
        weights = weights.astype(BF16)
        attn = (dot(v, weights, NN) * (inverse * own)).astype(BF16).astype(F32)
        dots = jnp.sum(do * attn, axis=0, keepdims=True)
        dscore = (weights.astype(F32) * (dprob[h] - dots)).astype(BF16)
        found[0].append(dot(k, dscore, NN) * (inverse * SCALE))
        found[1].append(dot((q * inverse).astype(BF16), dscore, NT) * SCALE)
        found[2].append(dot((do * inverse).astype(BF16), weights, NT))
        found[3].append(attn)
    return jnp.concatenate([one for pair in found for one in pair], axis=0)


def ends_of(length_ref):
    lengths = length_ref[...].astype(F32)
    at = lax.broadcasted_iota(jnp.int32, (IMAGES, IMAGES), 0)
    of = lax.broadcasted_iota(jnp.int32, (IMAGES, IMAGES), 1)
    ends = jnp.sum(jnp.where(of <= at, lengths, 0.0), axis=1, keepdims=True)
    starts = jnp.sum(jnp.where(of < at, lengths, 0.0), axis=1, keepdims=True)
    return starts, ends


def marks_of(starts, ends, first, last):
    positions = (first + lax.broadcasted_iota(jnp.int32, (1, WINDOW), 1)).astype(F32)
    inside = (positions >= starts) & (positions < ends)
    whole = (starts >= first.astype(F32)) & (ends <= last.astype(F32))
    return jnp.where(inside & whole, 1.0, 0.0)


def split(total, grads_ref, attn_ref):
    for b in range(GROUP):
        columns = slice(b * ROWS, (b + 1) * ROWS)
        grads_ref[b] = total[:GRADS, columns]
        attn_ref[:, columns] = total[GRADS:, columns]


def inner_kernel(place_ref, count_ref, length_ref, mid_ref, grads_ref, attn_ref, frame, total, window):
    base = place_ref[0] * SPAN

    def scan(i, carry):
        start, n, first = carry
        end = start + count_ref[0, i]
        inside = (start >= base) & (end <= base + SPAN)
        opens = inside & ((n == 0) | (end - first > WINDOW))
        n = jnp.where(opens, n + 1, n)
        first = jnp.where(opens, start, first)

        @pl.when(inside)
        def _():
            window[0, n - 1] = first
            window[1, n - 1] = end

        return end, n, first

    _, count, _ = lax.fori_loop(0, IMAGES, scan, (jnp.int32(0), jnp.int32(0), jnp.int32(0)))
    for b in range(GROUP):
        frame[:, b * ROWS : (b + 1) * ROWS] = mid_ref[b]
    frame[:, SPAN:] = jnp.zeros((SLAB, WINDOW), BF16)
    total[...] = jnp.zeros((SLAB, FRAME), BF16)
    starts, ends = ends_of(length_ref)

    def body(n, _):
        first, last = window[0, n], window[1, n]
        offset = first - base
        low = pl.multiple_of(offset // 128 * 128, 128)
        slab = frame[:, pl.ds(low, REACH)].astype(F32)
        slab = pltpu.roll(slab, lax.rem(REACH - (offset - low), REACH), 1)[:, :WINDOW]
        found = attend(slab, marks_of(starts, ends, first, last))
        wide = jnp.concatenate([found, jnp.zeros((SLAB, REACH - WINDOW), F32)], axis=1)
        wide = pltpu.roll(wide, offset - low, 1)
        old = total[:, pl.ds(low, REACH)].astype(F32)
        total[:, pl.ds(low, REACH)] = (old + wide).astype(BF16)
        return 0

    lax.fori_loop(0, count, body, 0)
    split(total[:, :SPAN], grads_ref, attn_ref)


RESULT = (
    jax.ShapeDtypeStruct((GROUP, GRADS, ROWS), BF16),
    jax.ShapeDtypeStruct((PAIR, SPAN), BF16),
)


def inner(place, lengths, mid):
    scratch = [
        pltpu.VMEM((SLAB, FRAME), BF16),
        pltpu.VMEM((SLAB, FRAME), BF16),
        pltpu.SMEM((2, IMAGES), jnp.int32),
    ]
    specs = [SCALAR, SCALAR, WHOLE, WHOLE]
    return call(inner_kernel, RESULT, specs, scratch, 20 * 10**9)(place, lengths, lengths, mid)


def edge_kernel(
    place_ref, count_ref, length_ref, mid_ref, left_ref, right_ref, grads_in, grads_ref, attn_ref, frame
):
    side = pl.program_id(0)
    border = (place_ref[0] + side) * SPAN
    grads_ref[...] = grads_in[...]
    attn_ref[...] = jnp.zeros((PAIR, WINDOW), BF16)

    def scan(i, carry):
        start, first, last = carry
        end = start + count_ref[0, i]
        over = (start < border) & (end > border)
        return end, jnp.where(over, start, first), jnp.where(over, end, last)

    nothing = jnp.int32(-1)
    _, first, last = lax.fori_loop(0, IMAGES, scan, (jnp.int32(0), nothing, nothing))

    @pl.when(last > 0)
    def _():
        def lay(blocks):
            for at, block in enumerate(blocks):
                frame[:, at * ROWS : (at + 1) * ROWS] = block

        @pl.when(side == 0)
        def _():
            lay([left_ref[0], left_ref[1], mid_ref[0], mid_ref[1]])

        @pl.when(side == 1)
        def _():
            lay([mid_ref[0], mid_ref[1], right_ref[0], right_ref[1]])

        starts, ends = ends_of(length_ref)
        offset = first - (border - WINDOW)
        slab = pltpu.roll(frame[...].astype(F32), EDGE - offset, 1)[:, :WINDOW]
        found = attend(slab, marks_of(starts, ends, first, last))
        wide = jnp.concatenate([found, jnp.zeros((SLAB, EDGE - WINDOW), F32)], axis=1)
        frame[...] = pltpu.roll(wide, offset, 1).astype(BF16)
        mine = frame[:, pl.ds(pl.multiple_of((1 - side) * WINDOW, WINDOW), WINDOW)]
        attn_ref[...] = mine[GRADS:]
        for at in range(2):
            term = mine[:GRADS, at * ROWS : (at + 1) * ROWS]
            grads_ref[at] = (grads_in[at].astype(F32) + term.astype(F32)).astype(BF16)


def edge(place, lengths, mid, left, right, grads):
    ends = lambda rows: pl.BlockSpec((2, rows, ROWS), lambda i: (i * (GROUP // 2 - 1), 0, 0))
    halo = pl.BlockSpec((2, SLAB, ROWS), lambda i: (0, 0, 0))
    return pl.pallas_call(
        edge_kernel,
        grid=(2,),
        out_shape=(RESULT[0], jax.ShapeDtypeStruct((PAIR, EDGE), BF16)),
        in_specs=[
            SCALAR, SCALAR, pl.BlockSpec((1, IMAGES), lambda i: (0, 0)),
            ends(SLAB), halo, halo, ends(GRADS),
        ],
        out_specs=(ends(GRADS), pl.BlockSpec((PAIR, WINDOW), lambda i: (0, i))),
        scratch_shapes=[pltpu.VMEM((SLAB, EDGE), BF16)],
        input_output_aliases={6: 0},
        compiler_params=pltpu.CompilerParams(
            vmem_limit_bytes=VMEM_LIMIT, dimension_semantics=("arbitrary",)
        ),
        cost_estimate=pl.CostEstimate(flops=8 * 10**9, bytes_accessed=4 << 20, transcendentals=0),
    )(place, lengths, lengths, mid, left, right, grads)


def unpack_kernel(back_ref, *out_refs):
    for at, out_ref in enumerate(out_refs):
        rows = slice(at * PAIR, (at + 1) * PAIR)
        whole = jnp.concatenate([back_ref[g, rows, :] for g in range(GROUP)], axis=0)
        out_ref[...] = jnp.transpose(whole)


def unpack(back):
    shape = jax.ShapeDtypeStruct((ROWS, WIDTH), BF16)
    return call(unpack_kernel, (shape,) * 3, [WHOLE], [], 1 << 20)(back)


def columns_of(half_ref, mine_ref, other_ref):
    first = half_ref[0] == 0
    mine, other = mine_ref[...], other_ref[...]
    return jnp.concatenate([jnp.where(first, mine, other), jnp.where(first, other, mine)], axis=0)


def inner_proj_kernel(half_ref, rows_ref, mine_ref, other_ref, out_ref):
    attn = columns_of(half_ref, mine_ref, other_ref)
    total = jnp.zeros((SLAB, 2 * PAIR), F32)
    for b in range(GROUP):
        total = total + dot(rows_ref[b], attn[:, b * ROWS : (b + 1) * ROWS], NT)
    out_ref[...] = total


def inner_proj(half, rows, mine, other):
    shape = jax.ShapeDtypeStruct((SLAB, 2 * PAIR), F32)
    specs = [SCALAR] + [WHOLE] * 3
    return call(inner_proj_kernel, shape, specs, [], 1000)(half, rows, mine, other)


def edge_proj_kernel(half_ref, low_ref, high_ref, mine_ref, other_ref, total_ref, out_ref):
    attn = columns_of(half_ref, mine_ref, other_ref)
    total = total_ref[...]
    for b in range(2):
        total = total + dot(low_ref[b], attn[:, b * ROWS : (b + 1) * ROWS], NT)
        total = total + dot(high_ref[b], attn[:, WINDOW + b * ROWS : WINDOW + (b + 1) * ROWS], NT)
    total = total.astype(BF16)
    for z in range(4):
        out_ref[z] = total[z * PAIR : (z + 1) * PAIR]


def edge_proj(half, rows, mine, other, total):
    pick = lambda at: pl.BlockSpec((2, SLAB, ROWS), lambda i: (at, 0, 0))
    whole = lambda *shape: pl.BlockSpec(shape, lambda i: (0,) * len(shape))
    return pl.pallas_call(
        edge_proj_kernel,
        grid=(1,),
        out_shape=jax.ShapeDtypeStruct((4, PAIR, 2 * PAIR), BF16),
        in_specs=[
            SCALAR, pick(0), pick(GROUP // 2 - 1),
            whole(PAIR, EDGE), whole(PAIR, EDGE), whole(SLAB, 2 * PAIR),
        ],
        out_specs=whole(4, PAIR, 2 * PAIR),
        compiler_params=pltpu.CompilerParams(
            vmem_limit_bytes=VMEM_LIMIT, dimension_semantics=("arbitrary",)
        ),
        cost_estimate=pl.CostEstimate(flops=1000, bytes_accessed=1000, transcendentals=0),
    )(half, rows, rows, mine, other, total)


def per_device(query, key, value, grad_out, out_proj, lengths):
    seq = lax.axis_index("seq")
    place = (seq // GROUP).reshape(1)
    half = ((seq // 4) % 2).reshape(1)
    count = lax.axis_size("seq")
    within_z = [[GROUP * z + g for g in range(GROUP)] for z in range(4)]

    def shift(block, by):
        return lax.ppermute(block, "seq", [(i, i + by) for i in range(count) if 0 <= i + by < count])

    def swap(block, axis, by):
        return lax.ppermute(block, axis, [(i, i ^ by) for i in range(lax.axis_size(axis))])

    def exchange(blocks, groups):
        return lax.all_to_all(blocks, "seq", 0, 0, axis_index_groups=groups)

    packed, rows = pack(query[0], key[0], value[0], grad_out[0], out_proj)
    mid = exchange(packed, within_z)
    left = shift(mid[GROUP - 2 :], GROUP)
    right = shift(mid[:2], -GROUP)
    rows, mid = lax.optimization_barrier((rows, mid))
    rows = exchange(rows, within_z)
    grads, attn = inner(place, lengths, mid)
    other = swap(attn, "seq", 4)
    grads, edges = edge(place, lengths, mid, left, right, grads)
    across = swap(edges, "seq", 4)
    grads, other, across = lax.optimization_barrier((grads, other, across))
    grads = exchange(grads, within_z)
    part = inner_proj(half, rows, attn, other)
    part = edge_proj(half, rows, edges, across, part)

    def others(blocks, step):
        at = (seq // step) % 4
        ring = lambda k: [
            (i, i + ((i // step + k) % 4 - i // step % 4) * step) for i in range(count)
        ]
        pick = lambda k: lax.dynamic_index_in_dim(blocks, (at + k) % 4, 0, keepdims=False)
        return [pick(0)] + [lax.ppermute(pick(k), "seq", ring(k)) for k in range(1, 4)]

    part = sum(one.astype(F32) for one in others(part, GROUP))
    part, grads = lax.optimization_barrier((part, grads))
    found = others(part.reshape(4, 36, 2 * PAIR), 1)
    x = seq % 4
    found = jnp.stack([found[0], *found[:0:-1]])
    found = jnp.roll(found, x, axis=0).reshape(4, 36, 2, PAIR)
    part = jnp.transpose(found, (1, 2, 0, 3)).reshape(36, WIDTH)
    part = part + swap(part, "dp", 2)
    part = part + swap(part, "dp", 1)
    return (*(g[None] for g in unpack(grads)), part)


def solution(mesh):
    rows = P("dp", "seq", None)
    return jax.shard_map(
        per_device,
        mesh=mesh,
        in_specs=(rows, rows, rows, rows, P(), P("dp", None)),
        out_specs=(rows, rows, rows, P("seq", None)),
        check_vma=False,
    )
```

time: 579 us -> 149 us (0.26); the launches traced: 573 us -> 149 us
  waiting for transfers between devices: 383 us -> 53.4 us
  matrix products: 75.5 us -> 0 us
  Pallas kernels: 0 us -> 44 us
  local copies, waits for them, and re-layouts: 36 us -> 5.63 us
  between operations: 15.6 us -> 0.78 us
  starting transfers between devices: 57.6 us -> 43.5 us
    unnamed x3 -> x0, waiting for transfers between devices: 333 us -> none
    dot_general x32 -> x0, matrix products: 75.5 us -> none  [the longest x5 18.2 us: per_device(): jnp.einsum('hqk,khd->qhd', probs, v_heads, preferred_element_type=jnp.flo...]
    psum x1 -> x0, waiting for transfers between devices: 50.2 us -> none  [per_device(): grad_proj = lax.psum(proj_share, 'dp')]
    pallas_call x0 -> x6, Pallas kernels: none -> 44 us  [the longest x1 21.3 us: inner(): call(inner_kernel, RESULT, specs, scratch, 20 * 10 ** 9)]
    all_to_all x0 -> x3, waiting for transfers between devices: none -> 31.4 us  [exchange(): return lax.all_to_all(blocks, 'seq', 0, 0, axis_index_groups=groups)]
    ppermute x16 -> x12, starting transfers between devices: 57.6 us -> 26.6 us  [the longest x4 12.4 us: swap(): lax.ppermute(block, axis, [(i, i ^ by) for i in range(lax.axis_size(axis))])]
    ppermute x16 -> x12, waiting for transfers between devices: 0.04 us -> 22 us  [the longest x4 12.3 us: swap(): lax.ppermute(block, axis, [(i, i ^ by) for i in range(lax.axis_size(axis))])]
    unnamed x77 -> x18, local copies, waits for them, and re-layouts: 23.8 us -> 2.5 us
  transfers between devices with their start and end apart: 18 -> 15, of which waited for: 2 -> 11; matrix products, arithmetic and copies ran while one was open for 19% -> 2% of each run, Pallas kernels for 0% -> 26%
where the time goes in v2:
time: 149 us
  waiting for transfers between devices  53.4 us (36%)
  Pallas kernels  44 us (30%)
  starting transfers between devices  43.5 us (29%)
  local copies, waits for them, and re-layouts  5.63 us (4%)
  other arithmetic  1.69 us (1%)
    all_to_all x3, waiting for transfers between devices, exchange(): return lax.all_to_all(blocks, 'seq', 0, 0, axis_index_groups=groups)  31.4 us
    pallas_call x1, Pallas kernels, inner(): call(inner_kernel, RESULT, specs, scratch, 20 * 10 ** 9)  21.3 us
    all_to_all x3, starting transfers between devices, exchange(): return lax.all_to_all(blocks, 'seq', 0, 0, axis_index_groups=groups)  16.8 us
    ppermute x4, starting transfers between devices, swap(): lax.ppermute(block, axis, [(i, i ^ by) for i in range(lax.axis_size(axis))])  12.4 us
    ppermute x4, waiting for transfers between devices, swap(): lax.ppermute(block, axis, [(i, i ^ by) for i in range(lax.axis_size(axis))])  12.3 us
    ppermute x6, waiting for transfers between devices, others(): lax.ppermute(pick(k), 'seq', ring(k))  9.67 us
    ppermute x6, starting transfers between devices, others(): lax.ppermute(pick(k), 'seq', ring(k))  9.34 us
    pallas_call x1, Pallas kernels, edge(): pl.pallas_call(edge_kernel, grid=(2,), out_shape=(RESULT[0], jax.ShapeDty...  7 us
  transfers between devices with their start and end apart: 15, of which 11 were waited for; matrix products, arithmetic and copies ran while one was open for 2% of the time, Pallas kernels for 26%

profile of v2, /device:TPU:1, one launch (start us, length us, event | category | flops | bytes accessed | tf_op | source)
XLA Modules:
  0.0 149.0 jit_solution(9545460204984265150)
XLA Ops:
  0.6 5.4 %shard_map.93 = (bf16[8,576,256]{2,1,0:T(8,128)(2,1)}, bf16[8,576,256]{2,1,0:T(8,128)(2,1)}) custom-call(bf16[256,1152]{1,0:T(8,128)(2,1)} %bitcast.37, bf16[256,1152]{1,0:T(8,128)(2,1)} %bitcast.38, bf16[256,1152]{1,0:T(8,128)(2,1)} %bitcast.39, bf16[256,1152]{1,0:T(8,128)(2,1)} %bitcast.40, bf16[1152,1152]{1,0:T(8,128)(2,1)} %proj_ref.1), custom_call_target="tpu_custom_call" | custom-call | flops 4000000000 | bytes 1000 | tf_op jit(solution)/shard_map/pallas_call | solution.py:68
  6.0 5.9 %all-to-all-start = ((bf16[8,576,256]{2,1,0:T(8,128)(2,1)}), bf16[8,576,256]{2,1,0:T(8,128)(2,1)S(1)}, u32[]{:S(2)}, u32[]{:S(2)}) async-start(bf16[8,576,256]{2,1,0:T(8,128)(2,1)} %get-tuple-element.21), calls=%async_computation | async-start | bytes 4718592 | tf_op jit(solution)/shard_map/all_to_all | solution.py:321
  11.9 29.9 %all-to-all-done.mid_ref = bf16[8,576,256]{2,1,0:T(8,128)(2,1)S(1)} async-done(((bf16[8,576,256]{2,1,0:T(8,128)(2,1)}), bf16[8,576,256]{2,1,0:T(8,128)(2,1)S(1)}, u32[]{:S(2)}, u32[]{:S(2)}) %all-to-all-start) | async-done | bytes 2359328 | tf_op jit(solution)/shard_map/all_to_all | solution.py:321
  41.7 1.5 copy-done.1
  43.2 6.1 %all-to-all-start.1 = ((bf16[8,576,256]{2,1,0:T(8,128)(2,1)}), bf16[8,576,256]{2,1,0:T(8,128)(2,1)S(1)}, u32[]{:S(2)}, u32[]{:S(2)}) async-start(bf16[8,576,256]{2,1,0:T(8,128)(2,1)} %get-tuple-element.22), calls=%async_computation.1 | async-start | bytes 4718592 | tf_op jit(solution)/shard_map/all_to_all | solution.py:321
  50.6 3.6 %collective-permute-start = (bf16[2,576,256]{2,1,0:T(8,128)(2,1)S(1)}, bf16[2,576,256]{2,1,0:T(8,128)(2,1)S(1)}, u32[]{:S(2)}, u32[]{:S(2)}) collective-permute-start(bf16[2,576,256]{2,1,0:T(8,128)(2,1)S(1)} %get-tuple-element.37), channel_id=1, source_target_pairs={{0,8},{1,9},{2,10},{3,11},{4,12},{5,13},{6,14},{7,15},{8,16},{9,17... | collective-permute-start | bytes 1769480 | tf_op jit(solution)/shard_map/ppermute | solution.py:315
  55.5 21.3 %shard_map.94 = (bf16[8,432,256]{2,1,0:T(8,128)(2,1)}, bf16[144,2048]{1,0:T(8,128)(2,1)}) custom-call(s32[1]{0:T(128)} %bitcast.5.place_ref, s32[1,32]{1,0:T(1,128)} %length_ref.3, s32[1,32]{1,0:T(1,128)} %length_ref.3, bf16[8,576,256]{2,1,0:T(8,128)(2,1)} %copy-done.1), custom_call_target="tpu_custom_call" | custom-call | flops 20000000000 | bytes 1000 | tf_op jit(solution)/shard_map/pallas_call | solution.py:177
  76.7 1.5 collective-permute-start.2
  79.2 7.0 %shard_map.95 = (bf16[8,432,256]{2,1,0:T(8,128)(2,1)}, bf16[144,1024]{1,0:T(8,128)(2,1)}) custom-call(s32[1]{0:T(128)} %bitcast.5.place_ref, s32[1,32]{1,0:T(1,128)} %length_ref.3, s32[1,32]{1,0:T(1,128)} %length_ref.3, bf16[8,576,256]{2,1,0:T(8,128)(2,1)} %copy-done.1, bf16[2,576,256]{2,1,0:T(8,128)(2,1)} %copy-done.4, ...), custom_call_target="tpu_custom_call", output_to_operand_aliasing={{0}: (6, {})} | custom-call | flops 8000000000 | bytes 4194304 | tf_op jit(solution)/shard_map/pallas_call | solution.py:227
  86.2 3.1 %collective-permute-done.2.other_ref = bf16[144,2048]{1,0:T(8,128)(2,1)S(1)} collective-permute-done((bf16[144,2048]{1,0:T(8,128)(2,1)}, bf16[144,2048]{1,0:T(8,128)(2,1)S(1)}, u32[]{:S(2)}, u32[]{:S(2)}) %collective-permute-start.2) | collective-permute-done | bytes 589856 | tf_op jit(solution)/shard_map/ppermute | solution.py:318
  89.3 6.3 %collective-permute-done.3.other_ref = bf16[144,1024]{1,0:T(8,128)(2,1)S(1)} collective-permute-done((bf16[144,1024]{1,0:T(8,128)(2,1)}, bf16[144,1024]{1,0:T(8,128)(2,1)S(1)}, u32[]{:S(2)}, u32[]{:S(2)}) %collective-permute-start.3) | collective-permute-done | bytes 294944 | tf_op jit(solution)/shard_map/ppermute | solution.py:318
  95.6 4.9 %all-to-all-start.2 = ((bf16[8,432,256]{2,1,0:T(8,128)(2,1)}), bf16[8,432,256]{2,1,0:T(8,128)(2,1)}, u32[]{:S(2)}, u32[]{:S(2)}) async-start(bf16[8,432,256]{2,1,0:T(8,128)(2,1)} %get-tuple-element.30), calls=%async_computation.2 | async-start | bytes 3538944 | tf_op jit(solution)/shard_map/all_to_all | solution.py:321
  100.5 4.2 %shard_map.96.total_ref = f32[576,288]{1,0:T(8,128)} custom-call(s32[1]{0:T(128)} %bitcast.half_ref, bf16[8,576,256]{2,1,0:T(8,128)(2,1)} %copy-done, bf16[144,2048]{1,0:T(8,128)(2,1)} %get-tuple-element.27.mine_ref, bf16[144,2048]{1,0:T(8,128)(2,1)} %copy-done.2), custom_call_target="tpu_custom_call" | custom-call | flops 1000 | bytes 1000 | tf_op jit(solution)/shard_map/pallas_call | solution.py:274
  104.8 3.2 %shard_map.97 = bf16[4,144,288]{2,1,0:T(8,128)(2,1)} custom-call(s32[1]{0:T(128)} %bitcast.half_ref, bf16[8,576,256]{2,1,0:T(8,128)(2,1)} %copy-done, bf16[8,576,256]{2,1,0:T(8,128)(2,1)} %copy-done, bf16[144,1024]{1,0:T(8,128)(2,1)} %get-tuple-element.25.mine_ref, bf16[144,1024]{1,0:T(8,128)(2,1)} %copy-done.3, f32[576,288]{1,0:T(8,128)} %shard_map.96.total_ref), custom_call_target="tpu_custom_call" | custom-call | flops 1000 | bytes 1000 | tf_op jit(solution)/shard_map/pallas_call | solution.py:291
  109.1 4.1 %collective-permute-start.6 = (bf16[144,288]{1,0:T(8,128)(2,1)S(1)}, bf16[144,288]{1,0:T(8,128)(2,1)S(1)}, u32[]{:S(2)}, u32[]{:S(2)}) collective-permute-start(bf16[144,288]{1,0:T(8,128)(2,1)S(1)} %get-tuple-element.39), channel_id=1, source_target_pairs={{0,24},{1,25},{2,26},{3,27},{4,28},{5,29},{6,30},{7,31},{8,0},{9,1... | collective-permute-start | bytes 248840 | tf_op jit(solution)/shard_map/ppermute | solution.py:344
  113.2 3.3 %collective-permute-start.5 = (bf16[144,288]{1,0:T(8,128)(2,1)S(1)}, bf16[144,288]{1,0:T(8,128)(2,1)S(1)}, u32[]{:S(2)}, u32[]{:S(2)}) collective-permute-start(bf16[144,288]{1,0:T(8,128)(2,1)S(1)} %get-tuple-element.40), channel_id=1, source_target_pairs={{0,16},{1,17},{2,18},{3,19},{4,20},{5,21},{6,22},{7,23},{8,24},{9,... | collective-permute-start | bytes 248840 | tf_op jit(solution)/shard_map/ppermute | solution.py:344
  117.5 1.4 collective-permute-done.5
  119.0 2.7 %collective-permute-done.4 = bf16[144,288]{1,0:T(8,128)(2,1)S(1)} collective-permute-done((bf16[144,288]{1,0:T(8,128)(2,1)S(1)}, bf16[144,288]{1,0:T(8,128)(2,1)S(1)}, u32[]{:S(2)}, u32[]{:S(2)}) %collective-permute-start.4) | collective-permute-done | bytes 82976 | tf_op jit(solution)/shard_map/ppermute | solution.py:344
  122.6 1.5 %all-to-all-done.2.back_ref = bf16[8,432,256]{2,1,0:T(8,128)(2,1)} async-done(((bf16[8,432,256]{2,1,0:T(8,128)(2,1)}), bf16[8,432,256]{2,1,0:T(8,128)(2,1)}, u32[]{:S(2)}, u32[]{:S(2)}) %all-to-all-start.2) | async-done | bytes 1769504 | tf_op jit(solution)/shard_map/all_to_all | solution.py:321
  127.4 2.7 %collective-permute-done.8 = f32[36,288]{1,0:T(8,128)S(1)} collective-permute-done((f32[36,288]{1,0:T(8,128)S(1)}, f32[36,288]{1,0:T(8,128)S(1)}, u32[]{:S(2)}, u32[]{:S(2)}) %collective-permute-start.8) | collective-permute-done | bytes 41504 | tf_op jit(solution)/shard_map/ppermute | solution.py:344
  131.5 6.0 %collective-permute-start.10 = (f32[36,1152]{1,0:T(8,128)S(1)}, f32[36,1152]{1,0:T(8,128)S(1)}, u32[]{:S(2)}, u32[]{:S(2)}) collective-permute-start(f32[36,1152]{1,0:T(8,128)S(1)} %reshape.29), channel_id=1, source_target_pairs={{0,64},{32,96},{64,0},{96,32},{1,65},{33,97},{65,1},{97,33},{2,66}... | collective-permute-start | bytes 497672 | tf_op jit(solution)/shard_map/ppermute | solution.py:318
  137.4 2.9 %collective-permute-done.10 = f32[36,1152]{1,0:T(8,128)S(1)} collective-permute-done((f32[36,1152]{1,0:T(8,128)S(1)}, f32[36,1152]{1,0:T(8,128)S(1)}, u32[]{:S(2)}, u32[]{:S(2)}) %collective-permute-start.10) | collective-permute-done | bytes 165920 | tf_op jit(solution)/shard_map/ppermute | solution.py:318
  140.4 5.0 %collective-permute-start.11 = (f32[36,1152]{1,0:T(8,128)S(1)}, f32[36,1152]{1,0:T(8,128)S(1)}, u32[]{:S(2)}, u32[]{:S(2)}) collective-permute-start(f32[36,1152]{1,0:T(8,128)S(1)} %add.134), channel_id=1, source_target_pairs={{0,32},{32,0},{64,96},{96,64},{1,33},{33,1},{65,97},{97,65},{2,34}... | collective-permute-start | bytes 497672 | tf_op jit(solution)/shard_map/ppermute | solution.py:318
  145.4 2.9 %shard_map.98 = (bf16[256,1152]{1,0:T(8,128)(2,1)}, bf16[256,1152]{1,0:T(8,128)(2,1)}, bf16[256,1152]{1,0:T(8,128)(2,1)}) custom-call(bf16[8,432,256]{2,1,0:T(8,128)(2,1)} %all-to-all-done.2.back_ref), custom_call_target="tpu_custom_call" | custom-call | flops 1048576 | bytes 1000 | tf_op jit(solution)/shard_map/pallas_call | solution.py:254
  (43 shorter events, 12.0 us)
Async XLA Ops:
  6.0 35.7 %all-to-all-start = ((bf16[8,576,256]{2,1,0:T(8,128)(2,1)}), bf16[8,576,256]{2,1,0:T(8,128)(2,1)S(1)}, u32[]{:S(2)}, u32[]{:S(2)}) async-start(bf16[8,576,256]{2,1,0:T(8,128)(2,1)} %get-tuple-element.21), calls=%async_computation | async-start | bytes 4718592 | tf_op jit(solution)/shard_map/all_to_all | solution.py:321
  41.7 1.5 copy-start.1
  43.2 52.5 %all-to-all-start.1 = ((bf16[8,576,256]{2,1,0:T(8,128)(2,1)}), bf16[8,576,256]{2,1,0:T(8,128)(2,1)S(1)}, u32[]{:S(2)}, u32[]{:S(2)}) async-start(bf16[8,576,256]{2,1,0:T(8,128)(2,1)} %get-tuple-element.22), calls=%async_computation.1 | async-start | bytes 4718592 | tf_op jit(solution)/shard_map/all_to_all | solution.py:321
  50.6 27.6 %collective-permute-start = (bf16[2,576,256]{2,1,0:T(8,128)(2,1)S(1)}, bf16[2,576,256]{2,1,0:T(8,128)(2,1)S(1)}, u32[]{:S(2)}, u32[]{:S(2)}) collective-permute-start(bf16[2,576,256]{2,1,0:T(8,128)(2,1)S(1)} %get-tuple-element.37), channel_id=1, source_target_pairs={{0,8},{1,9},{2,10},{3,11},{4,12},{5,13},{6,14},{7,15},{8,16},{9,17... | collective-permute-start | bytes 1769480 | tf_op jit(solution)/shard_map/ppermute | solution.py:315
  54.2 24.0 %collective-permute-start.1 = (bf16[2,576,256]{2,1,0:T(8,128)(2,1)S(1)}, bf16[2,576,256]{2,1,0:T(8,128)(2,1)S(1)}, u32[]{:S(2)}, u32[]{:S(2)}) collective-permute-start(bf16[2,576,256]{2,1,0:T(8,128)(2,1)S(1)} %get-tuple-element.36), channel_id=1, source_target_pairs={{8,0},{9,1},{10,2},{11,3},{12,4},{13,5},{14,6},{15,7},{16,8},{17,9... | collective-permute-start | bytes 1769480 | tf_op jit(solution)/shard_map/ppermute | solution.py:315
  76.7 12.6 %collective-permute-start.2 = (bf16[144,2048]{1,0:T(8,128)(2,1)}, bf16[144,2048]{1,0:T(8,128)(2,1)S(1)}, u32[]{:S(2)}, u32[]{:S(2)}) collective-permute-start(bf16[144,2048]{1,0:T(8,128)(2,1)} %get-tuple-element.27.mine_ref), channel_id=1, source_target_pairs={{0,4},{1,5},{2,6},{3,7},{4,0},{5,1},{6,2},{7,3},{8,12},{9,13},{10,... | collective-permute-start | bytes 1769480 | tf_op jit(solution)/shard_map/ppermute | solution.py:318
  78.2 0.8 copy-start.4
  78.2 1.0 copy-start.5
  86.2 9.4 %collective-permute-start.3 = (bf16[144,1024]{1,0:T(8,128)(2,1)}, bf16[144,1024]{1,0:T(8,128)(2,1)S(1)}, u32[]{:S(2)}, u32[]{:S(2)}) collective-permute-start(bf16[144,1024]{1,0:T(8,128)(2,1)} %get-tuple-element.25.mine_ref), channel_id=1, source_target_pairs={{0,4},{1,5},{2,6},{3,7},{4,0},{5,1},{6,2},{7,3},{8,12},{9,13},{10,... | collective-permute-start | bytes 884744 | tf_op jit(solution)/shard_map/ppermute | solution.py:318
  89.3 11.2 %copy-start.2 = (bf16[144,2048]{1,0:T(8,128)(2,1)}, bf16[144,2048]{1,0:T(8,128)(2,1)S(1)}, u32[]{:S(2)}) copy-start(bf16[144,2048]{1,0:T(8,128)(2,1)S(1)} %collective-permute-done.2.other_ref) | copy-start | bytes 1769476
  95.6 9.1 %copy-start.3 = (bf16[144,1024]{1,0:T(8,128)(2,1)}, bf16[144,1024]{1,0:T(8,128)(2,1)S(1)}, u32[]{:S(2)}) copy-start(bf16[144,1024]{1,0:T(8,128)(2,1)S(1)} %collective-permute-done.3.other_ref) | copy-start | bytes 884740
  95.6 4.9 %copy-start = (bf16[8,576,256]{2,1,0:T(8,128)(2,1)}, bf16[8,576,256]{2,1,0:T(8,128)(2,1)S(1)}, u32[]{:S(2)}) copy-start(bf16[8,576,256]{2,1,0:T(8,128)(2,1)S(1)} %all-to-all-done.1.rows_ref.low_ref.high_ref) | copy-start | bytes 7077892
  95.6 28.5 %all-to-all-start.2 = ((bf16[8,432,256]{2,1,0:T(8,128)(2,1)}), bf16[8,432,256]{2,1,0:T(8,128)(2,1)}, u32[]{:S(2)}, u32[]{:S(2)}) async-start(bf16[8,432,256]{2,1,0:T(8,128)(2,1)} %get-tuple-element.30), calls=%async_computation.2 | async-start | bytes 3538944 | tf_op jit(solution)/shard_map/all_to_all | solution.py:321
  109.1 8.5 %collective-permute-start.6 = (bf16[144,288]{1,0:T(8,128)(2,1)S(1)}, bf16[144,288]{1,0:T(8,128)(2,1)S(1)}, u32[]{:S(2)}, u32[]{:S(2)}) collective-permute-start(bf16[144,288]{1,0:T(8,128)(2,1)S(1)} %get-tuple-element.39), channel_id=1, source_target_pairs={{0,24},{1,25},{2,26},{3,27},{4,28},{5,29},{6,30},{7,31},{8,0},{9,1... | collective-permute-start | bytes 248840 | tf_op jit(solution)/shard_map/ppermute | solution.py:344
  113.2 5.8 %collective-permute-start.5 = (bf16[144,288]{1,0:T(8,128)(2,1)S(1)}, bf16[144,288]{1,0:T(8,128)(2,1)S(1)}, u32[]{:S(2)}, u32[]{:S(2)}) collective-permute-start(bf16[144,288]{1,0:T(8,128)(2,1)S(1)} %get-tuple-element.40), channel_id=1, source_target_pairs={{0,16},{1,17},{2,18},{3,19},{4,20},{5,21},{6,22},{7,23},{8,24},{9,... | collective-permute-start | bytes 248840 | tf_op jit(solution)/shard_map/ppermute | solution.py:344
  116.4 5.2 %collective-permute-start.4 = (bf16[144,288]{1,0:T(8,128)(2,1)S(1)}, bf16[144,288]{1,0:T(8,128)(2,1)S(1)}, u32[]{:S(2)}, u32[]{:S(2)}) collective-permute-start(bf16[144,288]{1,0:T(8,128)(2,1)S(1)} %get-tuple-element.38), channel_id=1, source_target_pairs={{0,8},{1,9},{2,10},{3,11},{4,12},{5,13},{6,14},{7,15},{8,16},{9,17... | collective-permute-start | bytes 248840 | tf_op jit(solution)/shard_map/ppermute | solution.py:344
  124.2 3.1 %collective-permute-start.7 = (f32[36,288]{1,0:T(8,128)S(1)}, f32[36,288]{1,0:T(8,128)S(1)}, u32[]{:S(2)}, u32[]{:S(2)}) collective-permute-start(f32[36,288]{1,0:T(8,128)S(1)} %get-tuple-element.44), channel_id=1, source_target_pairs={{0,3},{1,0},{2,1},{3,2},{4,7},{5,4},{6,5},{7,6},{8,11},{9,8},{10,9... | collective-permute-start | bytes 124424 | tf_op jit(solution)/shard_map/ppermute | solution.py:344
  125.4 4.6 %collective-permute-start.8 = (f32[36,288]{1,0:T(8,128)S(1)}, f32[36,288]{1,0:T(8,128)S(1)}, u32[]{:S(2)}, u32[]{:S(2)}) collective-permute-start(f32[36,288]{1,0:T(8,128)S(1)} %get-tuple-element.43), channel_id=1, source_target_pairs={{0,2},{1,3},{2,0},{3,1},{4,6},{5,7},{6,4},{7,5},{8,10},{9,11},{10,... | collective-permute-start | bytes 124424 | tf_op jit(solution)/shard_map/ppermute | solution.py:344
  126.0 4.7 %collective-permute-start.9 = (f32[36,288]{1,0:T(8,128)S(1)}, f32[36,288]{1,0:T(8,128)S(1)}, u32[]{:S(2)}, u32[]{:S(2)}) collective-permute-start(f32[36,288]{1,0:T(8,128)S(1)} %get-tuple-element.41), channel_id=1, source_target_pairs={{0,1},{1,2},{2,3},{3,0},{4,5},{5,6},{6,7},{7,4},{8,9},{9,10},{10,1... | collective-permute-start | bytes 124424 | tf_op jit(solution)/shard_map/ppermute | solution.py:344
  131.5 8.9 %collective-permute-start.10 = (f32[36,1152]{1,0:T(8,128)S(1)}, f32[36,1152]{1,0:T(8,128)S(1)}, u32[]{:S(2)}, u32[]{:S(2)}) collective-permute-start(f32[36,1152]{1,0:T(8,128)S(1)} %reshape.29), channel_id=1, source_target_pairs={{0,64},{32,96},{64,0},{96,32},{1,65},{33,97},{65,1},{97,33},{2,66}... | collective-permute-start | bytes 497672 | tf_op jit(solution)/shard_map/ppermute | solution.py:318
  140.4 7.9 %collective-permute-start.11 = (f32[36,1152]{1,0:T(8,128)S(1)}, f32[36,1152]{1,0:T(8,128)S(1)}, u32[]{:S(2)}, u32[]{:S(2)}) collective-permute-start(f32[36,1152]{1,0:T(8,128)S(1)} %add.134), channel_id=1, source_target_pairs={{0,32},{32,0},{64,96},{96,64},{1,33},{33,1},{65,97},{97,65},{2,34}... | collective-permute-start | bytes 497672 | tf_op jit(solution)/shard_map/ppermute | solution.py:318

commit v3 on v2

--- a/solution.py
+++ b/solution.py
@@ -16,7 +16,8 @@
 GRADS = 3 * PAIR
 SPAN = GROUP * ROWS
 WINDOW = 512
-REACH = WINDOW + 128
+SIZES = (256, 384, WINDOW)
+FILL = 256
 FRAME = SPAN + WINDOW
 EDGE = 2 * WINDOW
 SCALE = HEAD_DIM ** (-0.5)
@@ -56,7 +57,7 @@
         for z in range(4):
             at = (2 * z + g // 4) * PAIR
             go_out[g, z * PAIR : (z + 1) * PAIR, :] = go[at : at + PAIR]
-    d_attn = dot(proj_ref[...], go, TN).astype(BF16)
+    d_attn = jnp.transpose(dot(go_ref[...], proj_ref[...], NN).astype(BF16))
     turned = [jnp.transpose(ref[...]) for ref in (q_ref, k_ref, v_ref)] + [d_attn]
     for at in range(4):
         for g in range(GROUP):
@@ -105,28 +106,38 @@
     return starts, ends
 
 
-def marks_of(starts, ends, first, last):
-    positions = (first + lax.broadcasted_iota(jnp.int32, (1, WINDOW), 1)).astype(F32)
+def marks_of(starts, ends, first, last, size):
+    positions = (first + lax.broadcasted_iota(jnp.int32, (1, size), 1)).astype(F32)
     inside = (positions >= starts) & (positions < ends)
     whole = (starts >= first.astype(F32)) & (ends <= last.astype(F32))
     return jnp.where(inside & whole, 1.0, 0.0)
 
 
-def split(total, grads_ref, attn_ref):
-    for b in range(GROUP):
-        columns = slice(b * ROWS, (b + 1) * ROWS)
-        grads_ref[b] = total[:GRADS, columns]
-        attn_ref[:, columns] = total[GRADS:, columns]
-
-
-def inner_kernel(place_ref, count_ref, length_ref, mid_ref, grads_ref, attn_ref, frame, total, window):
+def by_size(rows, step):
+    for small, size in zip((0,) + SIZES, SIZES):
+
+        @pl.when((rows > small) & (rows <= size))
+        def _():
+            step(size)
+
+
+def inner_kernel(
+    place_ref, count_ref, length_ref, mid_ref, grads_ref, attn_ref, frame, total, window, arrived, sent
+):
     base = place_ref[0] * SPAN
+    columns = [pl.ds(b * ROWS, ROWS) for b in range(GROUP)]
+    loads = [
+        pltpu.make_async_copy(mid_ref.at[b], frame.at[:, columns[b]], arrived.at[b])
+        for b in range(GROUP)
+    ]
+    for load in loads:
+        load.start()
 
     def scan(i, carry):
         start, n, first = carry
         end = start + count_ref[0, i]
         inside = (start >= base) & (end <= base + SPAN)
-        opens = inside & ((n == 0) | (end - first > WINDOW))
+        opens = inside & ((n == 0) | (end - first > FILL))
         n = jnp.where(opens, n + 1, n)
         first = jnp.where(opens, start, first)
 
@@ -138,27 +149,42 @@
         return end, n, first
 
     _, count, _ = lax.fori_loop(0, IMAGES, scan, (jnp.int32(0), jnp.int32(0), jnp.int32(0)))
-    for b in range(GROUP):
-        frame[:, b * ROWS : (b + 1) * ROWS] = mid_ref[b]
     frame[:, SPAN:] = jnp.zeros((SLAB, WINDOW), BF16)
     total[...] = jnp.zeros((SLAB, FRAME), BF16)
     starts, ends = ends_of(length_ref)
+    for load in loads:
+        load.wait()
 
     def body(n, _):
         first, last = window[0, n], window[1, n]
         offset = first - base
         low = pl.multiple_of(offset // 128 * 128, 128)
-        slab = frame[:, pl.ds(low, REACH)].astype(F32)
-        slab = pltpu.roll(slab, lax.rem(REACH - (offset - low), REACH), 1)[:, :WINDOW]
-        found = attend(slab, marks_of(starts, ends, first, last))
-        wide = jnp.concatenate([found, jnp.zeros((SLAB, REACH - WINDOW), F32)], axis=1)
-        wide = pltpu.roll(wide, offset - low, 1)
-        old = total[:, pl.ds(low, REACH)].astype(F32)
-        total[:, pl.ds(low, REACH)] = (old + wide).astype(BF16)
+        shift = offset - low
+
+        def step(size):
+            reach = size + 128
+            slab = frame[:, pl.ds(low, reach)].astype(F32)
+            slab = pltpu.roll(slab, lax.rem(reach - shift, reach), 1)[:, :size]
+            found = attend(slab, marks_of(starts, ends, first, last, size))
+            wide = jnp.concatenate([found, jnp.zeros((SLAB, 128), F32)], axis=1)
+            wide = pltpu.roll(wide, shift, 1)
+            old = total[:, pl.ds(low, reach)].astype(F32)
+            total[:, pl.ds(low, reach)] = (old + wide).astype(BF16)
+
+        by_size(last - first, step)
         return 0
 
     lax.fori_loop(0, count, body, 0)
-    split(total[:, :SPAN], grads_ref, attn_ref)
+    stores = [
+        pltpu.make_async_copy(total.at[pl.ds(0, GRADS), columns[b]], grads_ref.at[b], sent.at[b])
+        for b in range(GROUP)
+    ]
+    found = total.at[pl.ds(GRADS, PAIR), pl.ds(0, SPAN)]
+    stores.append(pltpu.make_async_copy(found, attn_ref, sent.at[GROUP]))
+    for store in stores:
+        store.start()
+    for store in stores:
+        store.wait()
 
 
 RESULT = (
@@ -168,13 +194,22 @@
 
 
 def inner(place, lengths, mid):
-    scratch = [
-        pltpu.VMEM((SLAB, FRAME), BF16),
-        pltpu.VMEM((SLAB, FRAME), BF16),
-        pltpu.SMEM((2, IMAGES), jnp.int32),
-    ]
-    specs = [SCALAR, SCALAR, WHOLE, WHOLE]
-    return call(inner_kernel, RESULT, specs, scratch, 20 * 10**9)(place, lengths, lengths, mid)
+    hbm = pl.BlockSpec(memory_space=pl.ANY)
+    return pl.pallas_call(
+        inner_kernel,
+        out_shape=RESULT,
+        in_specs=[SCALAR, SCALAR, WHOLE, hbm],
+        out_specs=(hbm, hbm),
+        scratch_shapes=[
+            pltpu.VMEM((SLAB, FRAME), BF16),
+            pltpu.VMEM((SLAB, FRAME), BF16),
+            pltpu.SMEM((2, IMAGES), jnp.int32),
+            pltpu.SemaphoreType.DMA((GROUP,)),
+            pltpu.SemaphoreType.DMA((GROUP + 1,)),
+        ],
+        compiler_params=pltpu.CompilerParams(vmem_limit_bytes=VMEM_LIMIT),
+        cost_estimate=pl.CostEstimate(flops=20 * 10**9, bytes_accessed=4 << 20, transcendentals=0),
+    )(place, lengths, lengths, mid)
 
 
 def edge_kernel(
@@ -210,10 +245,14 @@
 
         starts, ends = ends_of(length_ref)
         offset = first - (border - WINDOW)
-        slab = pltpu.roll(frame[...].astype(F32), EDGE - offset, 1)[:, :WINDOW]
-        found = attend(slab, marks_of(starts, ends, first, last))
-        wide = jnp.concatenate([found, jnp.zeros((SLAB, EDGE - WINDOW), F32)], axis=1)
-        frame[...] = pltpu.roll(wide, offset, 1).astype(BF16)
+
+        def step(size):
+            slab = pltpu.roll(frame[...].astype(F32), EDGE - offset, 1)[:, :size]
+            found = attend(slab, marks_of(starts, ends, first, last, size))
+            wide = jnp.concatenate([found, jnp.zeros((SLAB, EDGE - size), F32)], axis=1)
+            frame[...] = pltpu.roll(wide, offset, 1).astype(BF16)
+
+        by_size(last - first, step)
         mine = frame[:, pl.ds(pl.multiple_of((1 - side) * WINDOW, WINDOW), WINDOW)]
         attn_ref[...] = mine[GRADS:]
         for at in range(2):
@@ -254,60 +293,66 @@
     return call(unpack_kernel, (shape,) * 3, [WHOLE], [], 1 << 20)(back)
 
 
-def columns_of(half_ref, mine_ref, other_ref):
-    first = half_ref[0] == 0
-    mine, other = mine_ref[...], other_ref[...]
-    return jnp.concatenate([jnp.where(first, mine, other), jnp.where(first, other, mine)], axis=0)
-
-
-def inner_proj_kernel(half_ref, rows_ref, mine_ref, other_ref, out_ref):
-    attn = columns_of(half_ref, mine_ref, other_ref)
-    total = jnp.zeros((SLAB, 2 * PAIR), F32)
-    for b in range(GROUP):
-        total = total + dot(rows_ref[b], attn[:, b * ROWS : (b + 1) * ROWS], NT)
-    out_ref[...] = total
-
-
-def inner_proj(half, rows, mine, other):
-    shape = jax.ShapeDtypeStruct((SLAB, 2 * PAIR), F32)
-    specs = [SCALAR] + [WHOLE] * 3
-    return call(inner_proj_kernel, shape, specs, [], 1000)(half, rows, mine, other)
-
-
-def edge_proj_kernel(half_ref, low_ref, high_ref, mine_ref, other_ref, total_ref, out_ref):
-    attn = columns_of(half_ref, mine_ref, other_ref)
-    total = total_ref[...]
-    for b in range(2):
-        total = total + dot(low_ref[b], attn[:, b * ROWS : (b + 1) * ROWS], NT)
-        total = total + dot(high_ref[b], attn[:, WINDOW + b * ROWS : WINDOW + (b + 1) * ROWS], NT)
-    total = total.astype(BF16)
-    for z in range(4):
-        out_ref[z] = total[z * PAIR : (z + 1) * PAIR]
-
-
-def edge_proj(half, rows, mine, other, total):
-    pick = lambda at: pl.BlockSpec((2, SLAB, ROWS), lambda i: (at, 0, 0))
-    whole = lambda *shape: pl.BlockSpec(shape, lambda i: (0,) * len(shape))
-    return pl.pallas_call(
-        edge_proj_kernel,
-        grid=(1,),
-        out_shape=jax.ShapeDtypeStruct((4, PAIR, 2 * PAIR), BF16),
-        in_specs=[
-            SCALAR, pick(0), pick(GROUP // 2 - 1),
-            whole(PAIR, EDGE), whole(PAIR, EDGE), whole(SLAB, 2 * PAIR),
-        ],
-        out_specs=whole(4, PAIR, 2 * PAIR),
-        compiler_params=pltpu.CompilerParams(
-            vmem_limit_bytes=VMEM_LIMIT, dimension_semantics=("arbitrary",)
-        ),
-        cost_estimate=pl.CostEstimate(flops=1000, bytes_accessed=1000, transcendentals=0),
-    )(half, rows, rows, mine, other, total)
+def proj_kernel(at_ref, rows_ref, mine_ref, other_ref, edge_ref, across_ref, *refs):
+    outs, total = refs[:-1], refs[-1]
+    first = at_ref[1] == 0
+
+    def columns(mine, other):
+        return jnp.concatenate([jnp.where(first, mine, other), jnp.where(first, other, mine)], axis=0)
+
+    attn = columns(mine_ref[...], other_ref[...])
+    edges = columns(edge_ref[...], across_ref[...])
+    low = (attn[:, :WINDOW].astype(F32) + edges[:, :WINDOW].astype(F32)).astype(BF16)
+    high = (attn[:, SPAN - WINDOW :].astype(F32) + edges[:, WINDOW:].astype(F32)).astype(BF16)
+    attn = jnp.concatenate([low, attn[:, WINDOW : SPAN - WINDOW], high], axis=1)
+    rows = jnp.concatenate([rows_ref[b] for b in range(GROUP)], axis=1)
+    total[...] = dot(rows, attn, NT)
+    for k, out_ref in enumerate(outs):
+        begin = pl.multiple_of(lax.rem(at_ref[0] + k, 4) * PAIR, PAIR)
+        out_ref[...] = total[pl.ds(begin, PAIR), :].astype(out_ref.dtype)
+
+
+def partial_proj(at, rows, mine, other, edges, across):
+    block = lambda dtype: jax.ShapeDtypeStruct((PAIR, 2 * PAIR), dtype)
+    shapes = (block(F32),) + (block(BF16),) * 3
+    scratch = [pltpu.VMEM((SLAB, 2 * PAIR), F32)]
+    specs = [SCALAR] + [WHOLE] * 5
+    return call(proj_kernel, shapes, specs, scratch, 1000)(at, rows, mine, other, edges, across)
+
+
+def select(blocks, at):
+    return sum(jnp.where(at == j, block, 0.0) for j, block in enumerate(blocks))
+
+
+def sum_z_kernel(at_ref, *refs):
+    total = refs[0][...] + sum(ref[...].astype(F32) for ref in refs[1:4])
+    blocks = [total[j * 36 : (j + 1) * 36] for j in range(4)]
+    for k, out_ref in enumerate(refs[4:]):
+        out_ref[...] = select(blocks, lax.rem(at_ref[2] + k, 4))
+
+
+def sum_z(at, terms):
+    shape = jax.ShapeDtypeStruct((36, 2 * PAIR), F32)
+    return call(sum_z_kernel, (shape,) * 4, [SCALAR] + [WHOLE] * 4, [], 1000)(at, *terms)
+
+
+def join_x_kernel(at_ref, *refs):
+    terms = [ref[...] for ref in refs[:4]]
+    for j in range(4):
+        block = select(terms, lax.rem(at_ref[2] + 4 - j, 4))
+        for y in range(2):
+            begin = (4 * y + j) * PAIR
+            refs[4][:, begin : begin + PAIR] = block[:, y * PAIR : (y + 1) * PAIR]
+
+
+def join_x(at, terms):
+    shape = jax.ShapeDtypeStruct((36, WIDTH), F32)
+    return call(join_x_kernel, shape, [SCALAR] + [WHOLE] * 4, [], 1000)(at, *terms)
 
 
 def per_device(query, key, value, grad_out, out_proj, lengths):
     seq = lax.axis_index("seq")
-    place = (seq // GROUP).reshape(1)
-    half = ((seq // 4) % 2).reshape(1)
+    place = jnp.stack([seq // GROUP, (seq // 4) % 2, seq % 4])
     count = lax.axis_size("seq")
     within_z = [[GROUP * z + g for g in range(GROUP)] for z in range(4)]
 
@@ -332,27 +377,19 @@
     across = swap(edges, "seq", 4)
     grads, other, across = lax.optimization_barrier((grads, other, across))
     grads = exchange(grads, within_z)
-    part = inner_proj(half, rows, attn, other)
-    part = edge_proj(half, rows, edges, across, part)
-
-    def others(blocks, step):
-        at = (seq // step) % 4
-        ring = lambda k: [
-            (i, i + ((i // step + k) % 4 - i // step % 4) * step) for i in range(count)
-        ]
-        pick = lambda k: lax.dynamic_index_in_dim(blocks, (at + k) % 4, 0, keepdims=False)
-        return [pick(0)] + [lax.ppermute(pick(k), "seq", ring(k)) for k in range(1, 4)]
-
-    part = sum(one.astype(F32) for one in others(part, GROUP))
-    part, grads = lax.optimization_barrier((part, grads))
-    found = others(part.reshape(4, 36, 2 * PAIR), 1)
-    x = seq % 4
-    found = jnp.stack([found[0], *found[:0:-1]])
-    found = jnp.roll(found, x, axis=0).reshape(4, 36, 2, PAIR)
-    part = jnp.transpose(found, (1, 2, 0, 3)).reshape(36, WIDTH)
-    part = part + swap(part, "dp", 2)
-    part = part + swap(part, "dp", 1)
-    return (*(g[None] for g in unpack(grads)), part)
+    part, *away = partial_proj(place, rows, attn, other, edges, across)
+
+    def ahead(block, step, k):
+        to = lambda i: i + ((i // step + k) % 4 - i // step % 4) * step
+        return lax.ppermute(block, "seq", [(i, to(i)) for i in range(count)])
+
+    part, *away = sum_z(place, [part] + [ahead(b, GROUP, k + 1) for k, b in enumerate(away)])
+    away = [ahead(b, 1, k + 1) for k, b in enumerate(away)]
+    grads = unpack(grads)
+    grads, away = lax.optimization_barrier((grads, away))
+    part = join_x(place, [part] + away)
+    part = (part + swap(part, "dp", 1)) + (swap(part, "dp", 2) + swap(part, "dp", 3))
+    return (*(g[None] for g in grads), part)
 
 
 def solution(mesh):

time: 149 us -> 148 us (level); the launches traced: 149 us -> 146 us
  waiting for transfers between devices: 53.4 us -> 61.8 us
  starting transfers between devices: 43.5 us -> 36.8 us
  Pallas kernels: 44 us -> 39.2 us
    ppermute x4 -> x5, waiting for transfers between devices: 12.3 us -> 24.9 us  [swap(): lax.ppermute(block, axis, [(i, i ^ by) for i in range(lax.axis_size(axis))])]
    ppermute x4 -> x5, starting transfers between devices: 12.4 us -> 5.92 us  [swap(): lax.ppermute(block, axis, [(i, i ^ by) for i in range(lax.axis_size(axis))])]
    ppermute x6, waiting for transfers between devices: 9.67 us -> 5.59 us  [ahead(): return lax.ppermute(block, 'seq', [(i, to(i)) for i in range(count)])]
    pallas_call x3 -> x4, Pallas kernels: 28.7 us -> 26 us  [the longest x1 17.9 us: inner(): pl.pallas_call(inner_kernel, out_shape=RESULT, in_specs=[SCALAR, SCALAR,...]
    pallas_call x1, Pallas kernels: 7 us -> 5.19 us  [edge(): pl.pallas_call(edge_kernel, grid=(2,), out_shape=(RESULT[0], jax.ShapeDty...]
    unnamed x18 -> x24, local copies, waits for them, and re-layouts: 2.5 us -> 3.72 us
  transfers between devices with their start and end apart: 15 -> 16, of which waited for: 11 -> 9; matrix products, arithmetic and copies ran while one was open for 2% -> 1% of each run, Pallas kernels for 26% -> 22%
where the time goes in v3:
time: 148 us; the launch traced here: 146 us
  waiting for transfers between devices  61.8 us (42%)
  Pallas kernels  39.2 us (26%)
  starting transfers between devices  36.8 us (25%)
  local copies, waits for them, and re-layouts  5.03 us (3%)
  other arithmetic  2.29 us (2%)
    all_to_all x3, waiting for transfers between devices, exchange(): return lax.all_to_all(blocks, 'seq', 0, 0, axis_index_groups=groups)  31.3 us
    ppermute x5, waiting for transfers between devices, swap(): lax.ppermute(block, axis, [(i, i ^ by) for i in range(lax.axis_size(axis))])  24.9 us
    pallas_call x1, Pallas kernels, inner(): pl.pallas_call(inner_kernel, out_shape=RESULT, in_specs=[SCALAR, SCALAR,...  17.9 us
    all_to_all x3, starting transfers between devices, exchange(): return lax.all_to_all(blocks, 'seq', 0, 0, axis_index_groups=groups)  16.3 us
    ppermute x6, starting transfers between devices, ahead(): return lax.ppermute(block, 'seq', [(i, to(i)) for i in range(count)])  9.1 us
    ppermute x5, starting transfers between devices, swap(): lax.ppermute(block, axis, [(i, i ^ by) for i in range(lax.axis_size(axis))])  5.92 us
    ppermute x6, waiting for transfers between devices, ahead(): return lax.ppermute(block, 'seq', [(i, to(i)) for i in range(count)])  5.59 us
    ppermute x2, starting transfers between devices, shift(): lax.ppermute(block, 'seq', [(i, i + by) for i in range(count) if 0 <= i +...  5.5 us
  transfers between devices with their start and end apart: 16, of which 9 were waited for; matrix products, arithmetic and copies ran while one was open for 1% of the time, Pallas kernels for 22%

profile of v3, /device:TPU:1, one launch (start us, length us, event | category | flops | bytes accessed | tf_op | source)
XLA Modules:
  0.0 145.8 jit_solution(12756986816312439539)
XLA Ops:
  0.6 5.1 %shard_map.93 = (bf16[8,576,256]{2,1,0:T(8,128)(2,1)}, bf16[8,576,256]{2,1,0:T(8,128)(2,1)}) custom-call(bf16[256,1152]{1,0:T(8,128)(2,1)} %bitcast.10, bf16[256,1152]{1,0:T(8,128)(2,1)} %bitcast.11, bf16[256,1152]{1,0:T(8,128)(2,1)} %bitcast.12, bf16[256,1152]{1,0:T(8,128)(2,1)} %bitcast.13, bf16[1152,1152]{1,0:T(8,128)(2,1)} %proj_ref.1), custom_call_target="tpu_custom_call" | custom-call | flops 4000000000 | bytes 1000 | tf_op jit(solution)/shard_map/pallas_call | solution.py:69
  5.7 5.9 %all-to-all-start = ((bf16[8,576,256]{2,1,0:T(8,128)(2,1)}), bf16[8,576,256]{2,1,0:T(8,128)(2,1)S(1)}, u32[]{:S(2)}, u32[]{:S(2)}) async-start(bf16[8,576,256]{2,1,0:T(8,128)(2,1)} %get-tuple-element.33), calls=%async_computation | async-start | bytes 4718592 | tf_op jit(solution)/shard_map/all_to_all | solution.py:366
  12.2 29.2 %all-to-all-done.mid_ref = bf16[8,576,256]{2,1,0:T(8,128)(2,1)S(1)} async-done(((bf16[8,576,256]{2,1,0:T(8,128)(2,1)}), bf16[8,576,256]{2,1,0:T(8,128)(2,1)S(1)}, u32[]{:S(2)}, u32[]{:S(2)}) %all-to-all-start) | async-done | bytes 2359328 | tf_op jit(solution)/shard_map/all_to_all | solution.py:366
  42.8 6.1 %all-to-all-start.2 = ((bf16[8,576,256]{2,1,0:T(8,128)(2,1)}), bf16[8,576,256]{2,1,0:T(8,128)(2,1)S(1)}, u32[]{:S(2)}, u32[]{:S(2)}) async-start(bf16[8,576,256]{2,1,0:T(8,128)(2,1)} %get-tuple-element.43), calls=%async_computation.2 | async-start | bytes 4718592 | tf_op jit(solution)/shard_map/all_to_all | solution.py:366
  51.5 4.2 %collective-permute-start = (bf16[2,576,256]{2,1,0:T(8,128)(2,1)S(1)}, bf16[2,576,256]{2,1,0:T(8,128)(2,1)S(1)}, u32[]{:S(2)}, u32[]{:S(2)}) collective-permute-start(bf16[2,576,256]{2,1,0:T(8,128)(2,1)S(1)} %get-tuple-element.61), channel_id=1, source_target_pairs={{0,8},{1,9},{2,10},{3,11},{4,12},{5,13},{6,14},{7,15},{8,16},{9,17... | collective-permute-start | bytes 1769480 | tf_op jit(solution)/shard_map/ppermute | solution.py:360
  55.7 17.9 %shard_map.94 = (bf16[8,432,256]{2,1,0:T(8,128)(2,1)}, bf16[144,2048]{1,0:T(8,128)(2,1)}) custom-call(s32[3]{0:T(128)} %pad_add_fusion.place_ref.at_ref, s32[1,32]{1,0:T(1,128)} %length_ref.3, s32[1,32]{1,0:T(1,128)} %length_ref.3, bf16[8,576,256]{2,1,0:T(8,128)(2,1)} %copy-done.1), custom_call_target="tpu_custom_call" | custom-call | flops 20000000000 | bytes 4194304 | tf_op jit(solution)/shard_map/pallas_call | solution.py:198
  73.6 1.7 %collective-permute-start.2 = (bf16[144,2048]{1,0:T(8,128)(2,1)}, bf16[144,2048]{1,0:T(8,128)(2,1)S(1)}, u32[]{:S(2)}, u32[]{:S(2)}) collective-permute-start(bf16[144,2048]{1,0:T(8,128)(2,1)} %get-tuple-element.37.mine_ref), channel_id=1, source_target_pairs={{0,4},{1,5},{2,6},{3,7},{4,0},{5,1},{6,2},{7,3},{8,12},{9,13},{10,... | collective-permute-start | bytes 1769480 | tf_op jit(solution)/shard_map/ppermute | solution.py:363
  76.4 5.2 %shard_map.95 = (bf16[8,432,256]{2,1,0:T(8,128)(2,1)}, bf16[144,1024]{1,0:T(8,128)(2,1)}) custom-call(s32[3]{0:T(128)} %pad_add_fusion.place_ref.at_ref, s32[1,32]{1,0:T(1,128)} %length_ref.3, s32[1,32]{1,0:T(1,128)} %length_ref.3, bf16[8,576,256]{2,1,0:T(8,128)(2,1)} %copy-done.1, bf16[2,576,256]{2,1,0:T(8,128)(2,1)} %copy-done.11, ...), custom_call_target="tpu_custom_call", output_to_operand_aliasing={{0}: (6, {})} | custom-call | flops 8000000000 | bytes 4194304 | tf_op jit(solution)/shard_map/pallas_call | solution.py:266
  81.6 10.2 %collective-permute-done.2.other_ref = bf16[144,2048]{1,0:T(8,128)(2,1)S(1)} collective-permute-done((bf16[144,2048]{1,0:T(8,128)(2,1)}, bf16[144,2048]{1,0:T(8,128)(2,1)S(1)}, u32[]{:S(2)}, u32[]{:S(2)}) %collective-permute-start.2) | collective-permute-done | bytes 589856 | tf_op jit(solution)/shard_map/ppermute | solution.py:363
  91.8 6.3 %collective-permute-done.3.across_ref = bf16[144,1024]{1,0:T(8,128)(2,1)S(1)} collective-permute-done((bf16[144,1024]{1,0:T(8,128)(2,1)}, bf16[144,1024]{1,0:T(8,128)(2,1)S(1)}, u32[]{:S(2)}, u32[]{:S(2)}) %collective-permute-start.3) | collective-permute-done | bytes 294944 | tf_op jit(solution)/shard_map/ppermute | solution.py:363
  98.1 4.3 %all-to-all-start.1 = ((bf16[8,432,256]{2,1,0:T(8,128)(2,1)}), bf16[8,432,256]{2,1,0:T(8,128)(2,1)}, u32[]{:S(2)}, u32[]{:S(2)}) async-start(bf16[8,432,256]{2,1,0:T(8,128)(2,1)} %get-tuple-element.39), calls=%async_computation.1 | async-start | bytes 3538944 | tf_op jit(solution)/shard_map/all_to_all | solution.py:366
  102.5 4.5 %shard_map.97 = (f32[144,288]{1,0:T(8,128)}, bf16[144,288]{1,0:T(8,128)(2,1)}, bf16[144,288]{1,0:T(8,128)(2,1)}, bf16[144,288]{1,0:T(8,128)(2,1)}) custom-call(s32[3]{0:T(128)} %pad_add_fusion.place_ref.at_ref, bf16[8,576,256]{2,1,0:T(8,128)(2,1)} %copy-done, bf16[144,2048]{1,0:T(8,128)(2,1)} %get-tuple-element.37.mine_ref, bf16[144,2048]{1,0:T(8,128)(2,1)} %copy-done.2, ...), custom_call_target="tpu_custom_call" | custom-call | flops 1000 | bytes 1000 | tf_op jit(solution)/shard_map/pallas_call | solution.py:320
  108.5 3.4 %collective-permute-start.5 = (bf16[144,288]{1,0:T(8,128)(2,1)}, bf16[144,288]{1,0:T(8,128)(2,1)S(1)}, u32[]{:S(2)}, u32[]{:S(2)}) collective-permute-start(bf16[144,288]{1,0:T(8,128)(2,1)} %get-tuple-element.48), channel_id=1, source_target_pairs={{0,16},{1,17},{2,18},{3,19},{4,20},{5,21},{6,22},{7,23},{8,24},{9,... | collective-permute-start | bytes 248840 | tf_op jit(solution)/shard_map/ppermute | solution.py:384
  111.8 2.1 %collective-permute-done.4.refs_1_ = bf16[144,288]{1,0:T(8,128)(2,1)S(1)} collective-permute-done((bf16[144,288]{1,0:T(8,128)(2,1)}, bf16[144,288]{1,0:T(8,128)(2,1)S(1)}, u32[]{:S(2)}, u32[]{:S(2)}) %collective-permute-start.4) | collective-permute-done | bytes 82976 | tf_op jit(solution)/shard_map/ppermute | solution.py:384
  114.0 3.2 %collective-permute-done.5.refs_2_ = bf16[144,288]{1,0:T(8,128)(2,1)S(1)} collective-permute-done((bf16[144,288]{1,0:T(8,128)(2,1)}, bf16[144,288]{1,0:T(8,128)(2,1)S(1)}, u32[]{:S(2)}, u32[]{:S(2)}) %collective-permute-start.5) | collective-permute-done | bytes 82976 | tf_op jit(solution)/shard_map/ppermute | solution.py:384
  117.9 1.9 %shard_map.98 = (f32[36,288]{1,0:T(8,128)}, f32[36,288]{1,0:T(8,128)}, f32[36,288]{1,0:T(8,128)}, f32[36,288]{1,0:T(8,128)}) custom-call(s32[3]{0:T(128)} %pad_add_fusion.place_ref.at_ref, f32[144,288]{1,0:T(8,128)} %get-tuple-element.46.refs_0_, bf16[144,288]{1,0:T(8,128)(2,1)} %copy-done.4, bf16[144,288]{1,0:T(8,128)(2,1)} %copy-done.5, ...), custom_call_target="tpu_custom_call" | custom-call | flops 1000 | bytes 1000 | tf_op jit(solution)/shard_map/pallas_call | solution.py:336
  120.4 2.4 %collective-permute-start.8 = (f32[36,288]{1,0:T(8,128)}, f32[36,288]{1,0:T(8,128)S(1)}, u32[]{:S(2)}, u32[]{:S(2)}) collective-permute-start(f32[36,288]{1,0:T(8,128)} %get-tuple-element.51), channel_id=1, source_target_pairs={{0,2},{1,3},{2,0},{3,1},{4,6},{5,7},{6,4},{7,5},{8,10},{9,11},{10,... | collective-permute-start | bytes 124424 | tf_op jit(solution)/shard_map/ppermute | solution.py:384
  124.0 2.1 %all-to-all-done.1.back_ref = bf16[8,432,256]{2,1,0:T(8,128)(2,1)} async-done(((bf16[8,432,256]{2,1,0:T(8,128)(2,1)}), bf16[8,432,256]{2,1,0:T(8,128)(2,1)}, u32[]{:S(2)}, u32[]{:S(2)}) %all-to-all-start.1) | async-done | bytes 1769504 | tf_op jit(solution)/shard_map/all_to_all | solution.py:366
  126.1 2.9 %shard_map.96 = (bf16[256,1152]{1,0:T(8,128)(2,1)}, bf16[256,1152]{1,0:T(8,128)(2,1)}, bf16[256,1152]{1,0:T(8,128)(2,1)}) custom-call(bf16[8,432,256]{2,1,0:T(8,128)(2,1)} %all-to-all-done.1.back_ref), custom_call_target="tpu_custom_call" | custom-call | flops 1048576 | bytes 1000 | tf_op jit(solution)/shard_map/pallas_call | solution.py:293
  129.8 1.8 %shard_map.99 = f32[36,1152]{1,0:T(8,128)} custom-call(s32[3]{0:T(128)} %pad_add_fusion.place_ref.at_ref, f32[36,288]{1,0:T(8,128)} %get-tuple-element.56.refs_0_, f32[36,288]{1,0:T(8,128)} %copy-done.7, f32[36,288]{1,0:T(8,128)} %copy-done.8, f32[36,288]{1,0:T(8,128)} %copy-done.9), custom_call_target="tpu_custom_call" | custom-call | flops 1000 | bytes 1000 | tf_op jit(solution)/shard_map/pallas_call | solution.py:350
  131.6 3.1 %collective-permute-start.12 = (f32[36,1152]{1,0:T(8,128)}, f32[36,1152]{1,0:T(8,128)S(1)}, u32[]{:S(2)}, u32[]{:S(2)}) collective-permute-start(f32[36,1152]{1,0:T(8,128)} %shard_map.99), channel_id=1, source_target_pairs={{0,96},{32,64},{64,32},{96,0},{1,97},{33,65},{65,33},{97,1},{2,98}... | collective-permute-start | bytes 497672 | tf_op jit(solution)/shard_map/ppermute | solution.py:363
  135.7 4.2 %collective-permute-done.12 = f32[36,1152]{1,0:T(8,128)S(1)} collective-permute-done((f32[36,1152]{1,0:T(8,128)}, f32[36,1152]{1,0:T(8,128)S(1)}, u32[]{:S(2)}, u32[]{:S(2)}) %collective-permute-start.12) | collective-permute-done | bytes 165920 | tf_op jit(solution)/shard_map/ppermute | solution.py:363
  139.9 4.2 %collective-permute-done.11 = f32[36,1152]{1,0:T(8,128)S(1)} collective-permute-done((f32[36,1152]{1,0:T(8,128)}, f32[36,1152]{1,0:T(8,128)S(1)}, u32[]{:S(2)}, u32[]{:S(2)}) %collective-permute-start.11) | collective-permute-done | bytes 165920 | tf_op jit(solution)/shard_map/ppermute | solution.py:363
  144.2 1.6 %add_add_fusion = f32[36,1152]{1,0:T(8,128)} fusion(f32[36,1152]{1,0:T(8,128)S(1)} %collective-permute-done.11, f32[36,1152]{1,0:T(8,128)S(1)} %collective-permute-done.12, f32[36,1152]{1,0:T(8,128)} %shard_map.99, f32[36,1152]{1,0:T(8,128)S(1)} %collective-permute-done.10), kind=kLoop, calls=%fused_computation | loop fusion | flops 124416 | bytes 829440 | tf_op jit(solution)/shard_map/add | solution.py:391
  (42 shorter events, 11.7 us)
Async XLA Ops:
  5.7 35.7 %all-to-all-start = ((bf16[8,576,256]{2,1,0:T(8,128)(2,1)}), bf16[8,576,256]{2,1,0:T(8,128)(2,1)S(1)}, u32[]{:S(2)}, u32[]{:S(2)}) async-start(bf16[8,576,256]{2,1,0:T(8,128)(2,1)} %get-tuple-element.33), calls=%async_computation | async-start | bytes 4718592 | tf_op jit(solution)/shard_map/all_to_all | solution.py:366
  41.4 1.4 copy-start.1
  42.8 55.3 %all-to-all-start.2 = ((bf16[8,576,256]{2,1,0:T(8,128)(2,1)}), bf16[8,576,256]{2,1,0:T(8,128)(2,1)S(1)}, u32[]{:S(2)}, u32[]{:S(2)}) async-start(bf16[8,576,256]{2,1,0:T(8,128)(2,1)} %get-tuple-element.43), calls=%async_computation.2 | async-start | bytes 4718592 | tf_op jit(solution)/shard_map/all_to_all | solution.py:366
  50.2 25.1 %collective-permute-start.1 = (bf16[2,576,256]{2,1,0:T(8,128)(2,1)S(1)}, bf16[2,576,256]{2,1,0:T(8,128)(2,1)S(1)}, u32[]{:S(2)}, u32[]{:S(2)}) collective-permute-start(bf16[2,576,256]{2,1,0:T(8,128)(2,1)S(1)} %get-tuple-element.60), channel_id=1, source_target_pairs={{8,0},{9,1},{10,2},{11,3},{12,4},{13,5},{14,6},{15,7},{16,8},{17,9... | collective-permute-start | bytes 1769480 | tf_op jit(solution)/shard_map/ppermute | solution.py:360
  51.5 23.9 %collective-permute-start = (bf16[2,576,256]{2,1,0:T(8,128)(2,1)S(1)}, bf16[2,576,256]{2,1,0:T(8,128)(2,1)S(1)}, u32[]{:S(2)}, u32[]{:S(2)}) collective-permute-start(bf16[2,576,256]{2,1,0:T(8,128)(2,1)S(1)} %get-tuple-element.61), channel_id=1, source_target_pairs={{0,8},{1,9},{2,10},{3,11},{4,12},{5,13},{6,14},{7,15},{8,16},{9,17... | collective-permute-start | bytes 1769480 | tf_op jit(solution)/shard_map/ppermute | solution.py:360
  73.6 18.1 %collective-permute-start.2 = (bf16[144,2048]{1,0:T(8,128)(2,1)}, bf16[144,2048]{1,0:T(8,128)(2,1)S(1)}, u32[]{:S(2)}, u32[]{:S(2)}) collective-permute-start(bf16[144,2048]{1,0:T(8,128)(2,1)} %get-tuple-element.37.mine_ref), channel_id=1, source_target_pairs={{0,4},{1,5},{2,6},{3,7},{4,0},{5,1},{6,2},{7,3},{8,12},{9,13},{10,... | collective-permute-start | bytes 1769480 | tf_op jit(solution)/shard_map/ppermute | solution.py:363
  75.4 0.8 copy-start.10
  75.4 1.0 copy-start.11
  81.6 16.5 %collective-permute-start.3 = (bf16[144,1024]{1,0:T(8,128)(2,1)}, bf16[144,1024]{1,0:T(8,128)(2,1)S(1)}, u32[]{:S(2)}, u32[]{:S(2)}) collective-permute-start(bf16[144,1024]{1,0:T(8,128)(2,1)} %get-tuple-element.38.edge_ref), channel_id=1, source_target_pairs={{0,4},{1,5},{2,6},{3,7},{4,0},{5,1},{6,2},{7,3},{8,12},{9,13},{10,... | collective-permute-start | bytes 884744 | tf_op jit(solution)/shard_map/ppermute | solution.py:363
  91.8 10.7 %copy-start.2 = (bf16[144,2048]{1,0:T(8,128)(2,1)}, bf16[144,2048]{1,0:T(8,128)(2,1)S(1)}, u32[]{:S(2)}) copy-start(bf16[144,2048]{1,0:T(8,128)(2,1)S(1)} %collective-permute-done.2.other_ref) | copy-start | bytes 1769476
  98.1 4.4 %copy-start.3 = (bf16[144,1024]{1,0:T(8,128)(2,1)}, bf16[144,1024]{1,0:T(8,128)(2,1)S(1)}, u32[]{:S(2)}) copy-start(bf16[144,1024]{1,0:T(8,128)(2,1)S(1)} %collective-permute-done.3.across_ref) | copy-start | bytes 884740
  98.1 4.4 %copy-start = (bf16[8,576,256]{2,1,0:T(8,128)(2,1)}, bf16[8,576,256]{2,1,0:T(8,128)(2,1)S(1)}, u32[]{:S(2)}) copy-start(bf16[8,576,256]{2,1,0:T(8,128)(2,1)S(1)} %all-to-all-done.2.rows_ref) | copy-start | bytes 7077892
  98.1 28.0 %all-to-all-start.1 = ((bf16[8,432,256]{2,1,0:T(8,128)(2,1)}), bf16[8,432,256]{2,1,0:T(8,128)(2,1)}, u32[]{:S(2)}, u32[]{:S(2)}) async-start(bf16[8,432,256]{2,1,0:T(8,128)(2,1)} %get-tuple-element.39), calls=%async_computation.1 | async-start | bytes 3538944 | tf_op jit(solution)/shard_map/all_to_all | solution.py:366
  106.9 7.0 %collective-permute-start.4 = (bf16[144,288]{1,0:T(8,128)(2,1)}, bf16[144,288]{1,0:T(8,128)(2,1)S(1)}, u32[]{:S(2)}, u32[]{:S(2)}) collective-permute-start(bf16[144,288]{1,0:T(8,128)(2,1)} %get-tuple-element.47), channel_id=1, source_target_pairs={{0,8},{1,9},{2,10},{3,11},{4,12},{5,13},{6,14},{7,15},{8,16},{9,17... | collective-permute-start | bytes 248840 | tf_op jit(solution)/shard_map/ppermute | solution.py:384
  108.5 8.7 %collective-permute-start.5 = (bf16[144,288]{1,0:T(8,128)(2,1)}, bf16[144,288]{1,0:T(8,128)(2,1)S(1)}, u32[]{:S(2)}, u32[]{:S(2)}) collective-permute-start(bf16[144,288]{1,0:T(8,128)(2,1)} %get-tuple-element.48), channel_id=1, source_target_pairs={{0,16},{1,17},{2,18},{3,19},{4,20},{5,21},{6,22},{7,23},{8,24},{9,... | collective-permute-start | bytes 248840 | tf_op jit(solution)/shard_map/ppermute | solution.py:384
  111.8 5.4 %collective-permute-start.6 = (bf16[144,288]{1,0:T(8,128)(2,1)}, bf16[144,288]{1,0:T(8,128)(2,1)S(1)}, u32[]{:S(2)}, u32[]{:S(2)}) collective-permute-start(bf16[144,288]{1,0:T(8,128)(2,1)} %get-tuple-element.49), channel_id=1, source_target_pairs={{0,24},{1,25},{2,26},{3,27},{4,28},{5,29},{6,30},{7,31},{8,0},{9,1... | collective-permute-start | bytes 248840 | tf_op jit(solution)/shard_map/ppermute | solution.py:384
  114.0 3.2 %copy-start.4 = (bf16[144,288]{1,0:T(8,128)(2,1)}, bf16[144,288]{1,0:T(8,128)(2,1)S(1)}, u32[]{:S(2)}) copy-start(bf16[144,288]{1,0:T(8,128)(2,1)S(1)} %collective-permute-done.4.refs_1_) | copy-start | bytes 248836
  117.2 0.7 copy-start.6
  119.8 9.2 %collective-permute-start.7 = (f32[36,288]{1,0:T(8,128)}, f32[36,288]{1,0:T(8,128)S(1)}, u32[]{:S(2)}, u32[]{:S(2)}) collective-permute-start(f32[36,288]{1,0:T(8,128)} %get-tuple-element.50), channel_id=1, source_target_pairs={{0,1},{1,2},{2,3},{3,0},{4,5},{5,6},{6,7},{7,4},{8,9},{9,10},{10,1... | collective-permute-start | bytes 124424 | tf_op jit(solution)/shard_map/ppermute | solution.py:384
  120.4 8.6 %collective-permute-start.8 = (f32[36,288]{1,0:T(8,128)}, f32[36,288]{1,0:T(8,128)S(1)}, u32[]{:S(2)}, u32[]{:S(2)}) collective-permute-start(f32[36,288]{1,0:T(8,128)} %get-tuple-element.51), channel_id=1, source_target_pairs={{0,2},{1,3},{2,0},{3,1},{4,6},{5,7},{6,4},{7,5},{8,10},{9,11},{10,... | collective-permute-start | bytes 124424 | tf_op jit(solution)/shard_map/ppermute | solution.py:384
  122.8 6.4 %collective-permute-start.9 = (f32[36,288]{1,0:T(8,128)}, f32[36,288]{1,0:T(8,128)S(1)}, u32[]{:S(2)}, u32[]{:S(2)}) collective-permute-start(f32[36,288]{1,0:T(8,128)} %get-tuple-element.52), channel_id=1, source_target_pairs={{0,3},{1,0},{2,1},{3,2},{4,7},{5,4},{6,5},{7,6},{8,11},{9,8},{10,9... | collective-permute-start | bytes 124424 | tf_op jit(solution)/shard_map/ppermute | solution.py:384
  131.6 8.4 %collective-permute-start.12 = (f32[36,1152]{1,0:T(8,128)}, f32[36,1152]{1,0:T(8,128)S(1)}, u32[]{:S(2)}, u32[]{:S(2)}) collective-permute-start(f32[36,1152]{1,0:T(8,128)} %shard_map.99), channel_id=1, source_target_pairs={{0,96},{32,64},{64,32},{96,0},{1,97},{33,65},{65,33},{97,1},{2,98}... | collective-permute-start | bytes 497672 | tf_op jit(solution)/shard_map/ppermute | solution.py:363
  134.7 9.5 %collective-permute-start.11 = (f32[36,1152]{1,0:T(8,128)}, f32[36,1152]{1,0:T(8,128)S(1)}, u32[]{:S(2)}, u32[]{:S(2)}) collective-permute-start(f32[36,1152]{1,0:T(8,128)} %shard_map.99), channel_id=1, source_target_pairs={{0,64},{32,96},{64,0},{96,32},{1,65},{33,97},{65,1},{97,33},{2,66}... | collective-permute-start | bytes 497672 | tf_op jit(solution)/shard_map/ppermute | solution.py:363
  135.7 8.4 %collective-permute-start.10 = (f32[36,1152]{1,0:T(8,128)}, f32[36,1152]{1,0:T(8,128)S(1)}, u32[]{:S(2)}, u32[]{:S(2)}) collective-permute-start(f32[36,1152]{1,0:T(8,128)} %shard_map.99), channel_id=1, source_target_pairs={{0,32},{32,0},{64,96},{96,64},{1,33},{33,1},{65,97},{97,65},{2,34}... | collective-permute-start | bytes 497672 | tf_op jit(solution)/shard_map/ppermute | solution.py:363
  (4 other events, 2.5 us)

commit v4 on v3

--- a/solution.py
+++ b/solution.py
@@ -25,7 +25,8 @@
 FAR = 1e30
 BF16 = jnp.bfloat16
 F32 = jnp.float32
-VMEM_LIMIT = 56 * 1024 * 1024
+VMEM_LIMIT = 24 * 1024 * 1024
+ALL_VMEM = 56 * 1024 * 1024
 
 NN = (((1,), (0,)), ((), ()))
 NT = (((1,), (1,)), ((), ()))
@@ -39,24 +40,24 @@
     return lax.dot_general(a, b, dims, preferred_element_type=F32)
 
 
-def call(kernel, out_shape, in_specs, scratch, flops):
+def call(kernel, out_shape, in_specs, scratch, flops, limit=VMEM_LIMIT):
     return pl.pallas_call(
         kernel,
         out_shape=out_shape,
         in_specs=in_specs,
         out_specs=jax.tree.map(lambda _: WHOLE, out_shape),
         scratch_shapes=scratch,
-        compiler_params=pltpu.CompilerParams(vmem_limit_bytes=VMEM_LIMIT),
+        compiler_params=pltpu.CompilerParams(vmem_limit_bytes=limit),
         cost_estimate=pl.CostEstimate(flops=flops, bytes_accessed=1000, transcendentals=0),
     )
 
 
-def pack_kernel(q_ref, k_ref, v_ref, go_ref, proj_ref, out_ref, go_out):
-    go = jnp.transpose(go_ref[...])
-    for g in range(GROUP):
-        for z in range(4):
-            at = (2 * z + g // 4) * PAIR
-            go_out[g, z * PAIR : (z + 1) * PAIR, :] = go[at : at + PAIR]
+def pack_kernel(at_ref, q_ref, k_ref, v_ref, go_ref, proj_ref, out_ref, same_ref, other_ref, turned_go):
+    turned_go[...] = jnp.transpose(go_ref[...])
+    for z in range(4):
+        for y, half_ref in ((at_ref[1], same_ref), (1 - at_ref[1], other_ref)):
+            begin = pl.multiple_of((2 * z + y) * PAIR, PAIR)
+            half_ref[z * PAIR : (z + 1) * PAIR, :] = turned_go[pl.ds(begin, PAIR), :]
     d_attn = jnp.transpose(dot(go_ref[...], proj_ref[...], NN).astype(BF16))
     turned = [jnp.transpose(ref[...]) for ref in (q_ref, k_ref, v_ref)] + [d_attn]
     for at in range(4):
@@ -64,37 +65,48 @@
             out_ref[g, at * PAIR : (at + 1) * PAIR, :] = turned[at][g * PAIR : (g + 1) * PAIR]
 
 
-def pack(q, k, v, go, proj):
-    shape = jax.ShapeDtypeStruct((GROUP, SLAB, ROWS), BF16)
-    return call(pack_kernel, (shape, shape), [WHOLE] * 5, [], 4 * 10**9)(q, k, v, go, proj)
-
-
-def attend(slab, marks):
+def pack(at, q, k, v, go, proj):
+    half = jax.ShapeDtypeStruct((SLAB, ROWS), BF16)
+    shapes = (jax.ShapeDtypeStruct((GROUP, SLAB, ROWS), BF16), half, half)
+    scratch = [pltpu.VMEM((WIDTH, ROWS), BF16)]
+    return call(pack_kernel, shapes, [SCALAR] + [WHOLE] * 5, scratch, 1000, ALL_VMEM)(
+        at, q, k, v, go, proj
+    )
+
+
+def weigh(slab, marks):
     own = jnp.sum(marks, axis=0, keepdims=True)
     marks = marks.astype(BF16)
     bias = (dot(marks, marks, TN) - 1.0) * FAR
-    heads = []
+    heads, found = [], []
     for h in range(2):
         q, k, v, do = (
             slab[a * PAIR + h * HEAD_DIM : a * PAIR + (h + 1) * HEAD_DIM] for a in range(4)
         )
         heads.append((q, k.astype(BF16), v.astype(BF16), do * own))
     scores = [dot(k, q.astype(BF16), TN) + bias for q, k, v, do in heads]
-    dprob = [dot(v, do.astype(BF16), TN) for q, k, v, do in heads]
-    found = [[], [], [], []]
-    for h, (q, k, v, do) in enumerate(heads):
-        top = jnp.max(scores[h], axis=0, keepdims=True)
-        weights = jnp.exp2((scores[h] - top) * (SCALE * LOG2E))
+    for (q, k, v, do), score in zip(heads, scores):
+        top = jnp.max(score, axis=0, keepdims=True)
+        weights = jnp.exp2((score - top) * (SCALE * LOG2E))
         inverse = 1.0 / jnp.sum(weights, axis=0, keepdims=True)
         weights = weights.astype(BF16)
         attn = (dot(v, weights, NN) * (inverse * own)).astype(BF16).astype(F32)
+        found.append((weights, inverse, attn))
+    return heads, found
+
+
+def attend(slab, marks):
+    heads, found = weigh(slab, marks)
+    dprob = [dot(v, do.astype(BF16), TN) for q, k, v, do in heads]
+    outs = [[], [], [], []]
+    for (q, k, v, do), (weights, inverse, attn), dp in zip(heads, found, dprob):
         dots = jnp.sum(do * attn, axis=0, keepdims=True)
-        dscore = (weights.astype(F32) * (dprob[h] - dots)).astype(BF16)
-        found[0].append(dot(k, dscore, NN) * (inverse * SCALE))
-        found[1].append(dot((q * inverse).astype(BF16), dscore, NT) * SCALE)
-        found[2].append(dot((do * inverse).astype(BF16), weights, NT))
-        found[3].append(attn)
-    return jnp.concatenate([one for pair in found for one in pair], axis=0)
+        dscore = (weights.astype(F32) * (dp - dots)).astype(BF16)
+        outs[0].append(dot(k, dscore, NN) * (inverse * SCALE))
+        outs[1].append(dot((q * inverse).astype(BF16), dscore, NT) * SCALE)
+        outs[2].append(dot((do * inverse).astype(BF16), weights, NT))
+        outs[3].append(attn)
+    return jnp.concatenate([one for pair in outs for one in pair], axis=0)
 
 
 def ends_of(length_ref):
@@ -199,7 +211,7 @@
         inner_kernel,
         out_shape=RESULT,
         in_specs=[SCALAR, SCALAR, WHOLE, hbm],
-        out_specs=(hbm, hbm),
+        out_specs=(pl.BlockSpec(memory_space=pltpu.HBM), hbm),
         scratch_shapes=[
             pltpu.VMEM((SLAB, FRAME), BF16),
             pltpu.VMEM((SLAB, FRAME), BF16),
@@ -208,17 +220,13 @@
             pltpu.SemaphoreType.DMA((GROUP + 1,)),
         ],
         compiler_params=pltpu.CompilerParams(vmem_limit_bytes=VMEM_LIMIT),
-        cost_estimate=pl.CostEstimate(flops=20 * 10**9, bytes_accessed=4 << 20, transcendentals=0),
+        cost_estimate=pl.CostEstimate(flops=1000, bytes_accessed=1000, transcendentals=0),
     )(place, lengths, lengths, mid)
 
 
-def edge_kernel(
-    place_ref, count_ref, length_ref, mid_ref, left_ref, right_ref, grads_in, grads_ref, attn_ref, frame
-):
+def edge_image(place_ref, count_ref, length_ref, mid_ref, left_ref, right_ref, frame, step):
     side = pl.program_id(0)
     border = (place_ref[0] + side) * SPAN
-    grads_ref[...] = grads_in[...]
-    attn_ref[...] = jnp.zeros((PAIR, WINDOW), BF16)
 
     def scan(i, carry):
         start, first, last = carry
@@ -246,39 +254,70 @@
         starts, ends = ends_of(length_ref)
         offset = first - (border - WINDOW)
 
-        def step(size):
+        def sized(size):
             slab = pltpu.roll(frame[...].astype(F32), EDGE - offset, 1)[:, :size]
-            found = attend(slab, marks_of(starts, ends, first, last, size))
-            wide = jnp.concatenate([found, jnp.zeros((SLAB, EDGE - size), F32)], axis=1)
-            frame[...] = pltpu.roll(wide, offset, 1).astype(BF16)
-
-        by_size(last - first, step)
-        mine = frame[:, pl.ds(pl.multiple_of((1 - side) * WINDOW, WINDOW), WINDOW)]
-        attn_ref[...] = mine[GRADS:]
-        for at in range(2):
-            term = mine[:GRADS, at * ROWS : (at + 1) * ROWS]
-            grads_ref[at] = (grads_in[at].astype(F32) + term.astype(F32)).astype(BF16)
-
-
-def edge(place, lengths, mid, left, right, grads):
+            found = step(slab, marks_of(starts, ends, first, last, size))
+            count = found.shape[0]
+            wide = jnp.concatenate([found, jnp.zeros((count, EDGE - size), F32)], axis=1)
+            frame[:count, :] = pltpu.roll(wide, offset, 1).astype(BF16)
+
+        by_size(last - first, sized)
+
+    @pl.when(last <= 0)
+    def _():
+        frame[...] = jnp.zeros((SLAB, EDGE), BF16)
+
+    return pl.ds(pl.multiple_of((1 - side) * WINDOW, WINDOW), WINDOW)
+
+
+def edge_attn_kernel(place_ref, count_ref, length_ref, mid_ref, left_ref, right_ref, attn_ref, frame):
+    def step(slab, marks):
+        return jnp.concatenate([attn for _, _, attn in weigh(slab, marks)[1]], axis=0)
+
+    mine = edge_image(place_ref, count_ref, length_ref, mid_ref, left_ref, right_ref, frame, step)
+    attn_ref[...] = frame[:PAIR, mine]
+
+
+def edge_grads_kernel(
+    place_ref, count_ref, length_ref, mid_ref, left_ref, right_ref, grads_in, *more
+):
+    grads_ref, frame = more[-2:]
+    mine = edge_image(place_ref, count_ref, length_ref, mid_ref, left_ref, right_ref, frame, attend)
+    found = frame[:GRADS, mine]
+    for at in range(2):
+        term = found[:, at * ROWS : (at + 1) * ROWS]
+        grads_ref[at] = (grads_in[at].astype(F32) + term.astype(F32)).astype(BF16)
+
+
+def edge(place, lengths, mid, left, right, grads=None, after=()):
     ends = lambda rows: pl.BlockSpec((2, rows, ROWS), lambda i: (i * (GROUP // 2 - 1), 0, 0))
     halo = pl.BlockSpec((2, SLAB, ROWS), lambda i: (0, 0, 0))
-    return pl.pallas_call(
-        edge_kernel,
+    specs = [SCALAR, SCALAR, pl.BlockSpec((1, IMAGES), lambda i: (0, 0)), ends(SLAB), halo, halo]
+    args = (place, lengths, lengths, mid, left, right)
+    more = dict(
         grid=(2,),
-        out_shape=(RESULT[0], jax.ShapeDtypeStruct((PAIR, EDGE), BF16)),
-        in_specs=[
-            SCALAR, SCALAR, pl.BlockSpec((1, IMAGES), lambda i: (0, 0)),
-            ends(SLAB), halo, halo, ends(GRADS),
-        ],
-        out_specs=(ends(GRADS), pl.BlockSpec((PAIR, WINDOW), lambda i: (0, i))),
         scratch_shapes=[pltpu.VMEM((SLAB, EDGE), BF16)],
-        input_output_aliases={6: 0},
         compiler_params=pltpu.CompilerParams(
             vmem_limit_bytes=VMEM_LIMIT, dimension_semantics=("arbitrary",)
         ),
-        cost_estimate=pl.CostEstimate(flops=8 * 10**9, bytes_accessed=4 << 20, transcendentals=0),
-    )(place, lengths, lengths, mid, left, right, grads)
+        cost_estimate=pl.CostEstimate(flops=1000, bytes_accessed=1000, transcendentals=0),
+    )
+    if grads is None:
+        return pl.pallas_call(
+            edge_attn_kernel,
+            out_shape=jax.ShapeDtypeStruct((PAIR, EDGE), BF16),
+            in_specs=specs,
+            out_specs=pl.BlockSpec((PAIR, WINDOW), lambda i: (0, i)),
+            **more,
+        )(*args)
+    return pl.pallas_call(
+        edge_grads_kernel,
+        out_shape=RESULT[0],
+        in_specs=specs + [ends(GRADS)] + [pl.BlockSpec(memory_space=pl.ANY)] * len(after),
+        out_specs=ends(GRADS),
+        input_output_aliases={6: 0},
+        **more,
+    )(*args, grads, *after)
 
 
 def unpack_kernel(back_ref, *out_refs):
@@ -290,34 +329,41 @@
 
 def unpack(back):
     shape = jax.ShapeDtypeStruct((ROWS, WIDTH), BF16)
-    return call(unpack_kernel, (shape,) * 3, [WHOLE], [], 1 << 20)(back)
-
-
-def proj_kernel(at_ref, rows_ref, mine_ref, other_ref, edge_ref, across_ref, *refs):
-    outs, total = refs[:-1], refs[-1]
+    return call(unpack_kernel, (shape,) * 3, [WHOLE], [], 1000)(back)
+
+
+def proj_kernel(at_ref, mine_ref, other_ref, edge_ref, across_ref, _, *refs):
+    rows, outs, (attn, total) = refs[:4], refs[4:-2], refs[-2:]
     first = at_ref[1] == 0
 
     def columns(mine, other):
         return jnp.concatenate([jnp.where(first, mine, other), jnp.where(first, other, mine)], axis=0)
 
-    attn = columns(mine_ref[...], other_ref[...])
-    edges = columns(edge_ref[...], across_ref[...])
-    low = (attn[:, :WINDOW].astype(F32) + edges[:, :WINDOW].astype(F32)).astype(BF16)
-    high = (attn[:, SPAN - WINDOW :].astype(F32) + edges[:, WINDOW:].astype(F32)).astype(BF16)
-    attn = jnp.concatenate([low, attn[:, WINDOW : SPAN - WINDOW], high], axis=1)
-    rows = jnp.concatenate([rows_ref[b] for b in range(GROUP)], axis=1)
-    total[...] = dot(rows, attn, NT)
+    inner_attn = columns(mine_ref[...], other_ref[...])
+    edges = columns(edge_ref[...], across_ref[...]).astype(F32)
+    low = inner_attn[:, :WINDOW].astype(F32) + edges[:, :WINDOW]
+    high = inner_attn[:, SPAN - WINDOW :].astype(F32) + edges[:, WINDOW:]
+    attn[:, :WINDOW] = low.astype(BF16)
+    attn[:, WINDOW : SPAN - WINDOW] = inner_attn[:, WINDOW : SPAN - WINDOW]
+    attn[:, SPAN - WINDOW :] = high.astype(BF16)
+    found = jnp.zeros((SLAB, 2 * PAIR), F32)
+    for k in range(GROUP):
+        begin = pl.multiple_of((at_ref[3] ^ k) * ROWS, ROWS)
+        part = rows[k % 4][k // 4 * SLAB : (k // 4 + 1) * SLAB, :]
+        found = found + dot(part, attn[:, pl.ds(begin, ROWS)], NT)
+    total[...] = found
     for k, out_ref in enumerate(outs):
         begin = pl.multiple_of(lax.rem(at_ref[0] + k, 4) * PAIR, PAIR)
         out_ref[...] = total[pl.ds(begin, PAIR), :].astype(out_ref.dtype)
 
 
-def partial_proj(at, rows, mine, other, edges, across):
+def partial_proj(at, rows, mine, other, edges, across, token):
     block = lambda dtype: jax.ShapeDtypeStruct((PAIR, 2 * PAIR), dtype)
     shapes = (block(F32),) + (block(BF16),) * 3
-    scratch = [pltpu.VMEM((SLAB, 2 * PAIR), F32)]
-    specs = [SCALAR] + [WHOLE] * 5
-    return call(proj_kernel, shapes, specs, scratch, 1000)(at, rows, mine, other, edges, across)
+    scratch = [pltpu.VMEM((2 * PAIR, SPAN), BF16), pltpu.VMEM((SLAB, 2 * PAIR), F32)]
+    specs = [SCALAR] + [WHOLE] * 4 + [pl.BlockSpec(memory_space=pl.ANY)] + [WHOLE] * 4
+    args = (at, mine, other, edges, across, token, *rows)
+    return call(proj_kernel, shapes, specs, scratch, 1000, ALL_VMEM)(*args)
 
 
 def select(blocks, at):
@@ -352,32 +398,38 @@
 
 def per_device(query, key, value, grad_out, out_proj, lengths):
     seq = lax.axis_index("seq")
-    place = jnp.stack([seq // GROUP, (seq // 4) % 2, seq % 4])
+    place = jnp.stack([seq // GROUP, (seq // 4) % 2, seq % 4, seq % GROUP])
     count = lax.axis_size("seq")
     within_z = [[GROUP * z + g for g in range(GROUP)] for z in range(4)]
 
     def shift(block, by):
         return lax.ppermute(block, "seq", [(i, i + by) for i in range(count) if 0 <= i + by < count])
 
+    def corner(block):
+        return block[:16, :128]
+
     def swap(block, axis, by):
         return lax.ppermute(block, axis, [(i, i ^ by) for i in range(lax.axis_size(axis))])
 
     def exchange(blocks, groups):
         return lax.all_to_all(blocks, "seq", 0, 0, axis_index_groups=groups)
 
-    packed, rows = pack(query[0], key[0], value[0], grad_out[0], out_proj)
+    packed, same, across_y = pack(place, query[0], key[0], value[0], grad_out[0], out_proj)
     mid = exchange(packed, within_z)
+    rows = jnp.concatenate([same, swap(across_y, "seq", 4)], axis=0)
+    rows = [rows] + [swap(rows, "seq", k) for k in range(1, 4)]
+    tokens = [corner(block) for block in rows[1:]]
     left = shift(mid[GROUP - 2 :], GROUP)
     right = shift(mid[:2], -GROUP)
-    rows, mid = lax.optimization_barrier((rows, mid))
-    rows = exchange(rows, within_z)
     grads, attn = inner(place, lengths, mid)
     other = swap(attn, "seq", 4)
-    grads, edges = edge(place, lengths, mid, left, right, grads)
+    edges = edge(place, lengths, mid, left, right)
     across = swap(edges, "seq", 4)
-    grads, other, across = lax.optimization_barrier((grads, other, across))
+    grads = edge(place, lengths, mid, left, right, grads, [edges] + tokens)
+    token = corner(other) + corner(across)
+    grads, token = lax.optimization_barrier((grads, token))
     grads = exchange(grads, within_z)
-    part, *away = partial_proj(place, rows, attn, other, edges, across)
+    part, *away = partial_proj(place, rows, attn, other, edges, across, token)
 
     def ahead(block, step, k):
         to = lambda i: i + ((i // step + k) % 4 - i // step % 4) * step

time: 148 us -> 136 us (0.919); the launches traced: 146 us -> 136 us
  waiting for transfers between devices: 61.8 us -> 21 us
  blocking collectives: 0 us -> 34.8 us
  local copies, waits for them, and re-layouts: 5.03 us -> 1.92 us
    all_to_all x0 -> x1, blocking collectives: none -> 34.8 us  [exchange(): return lax.all_to_all(blocks, 'seq', 0, 0, axis_index_groups=groups)]
    all_to_all x3 -> x1, waiting for transfers between devices: 31.3 us -> 1.56 us  [exchange(): return lax.all_to_all(blocks, 'seq', 0, 0, axis_index_groups=groups)]
    all_to_all x3 -> x1, starting transfers between devices: 16.3 us -> 3.81 us  [exchange(): return lax.all_to_all(blocks, 'seq', 0, 0, axis_index_groups=groups)]
    ppermute x5 -> x9, starting transfers between devices: 5.92 us -> 15 us  [swap(): lax.ppermute(block, axis, [(i, i ^ by) for i in range(lax.axis_size(axis))])]
    ppermute x5 -> x9, waiting for transfers between devices: 24.9 us -> 17.4 us  [swap(): lax.ppermute(block, axis, [(i, i ^ by) for i in range(lax.axis_size(axis))])]
    ppermute x6, starting transfers between devices: 9.1 us -> 13.2 us  [ahead(): return lax.ppermute(block, 'seq', [(i, to(i)) for i in range(count)])]
    ppermute x6, waiting for transfers between devices: 5.59 us -> 2.11 us  [ahead(): return lax.ppermute(block, 'seq', [(i, to(i)) for i in range(count)])]
    pallas_call x4 -> x5, Pallas kernels: 17.6 us -> 20.8 us  [the longest x1 6.44 us: edge(): pl.pallas_call(edge_grads_kernel, out_shape=RESULT[0], in_specs=specs + [...]
  transfers between devices with their start and end apart: 16 -> 18, of which waited for: 9 -> 6; matrix products, arithmetic and copies ran while one was open for 1% -> 0% of each run, Pallas kernels for 22% -> 24%
where the time goes in v4:
time: 136 us
  Pallas kernels  38.4 us (28%)
  starting transfers between devices  36.9 us (27%)
  blocking collectives  34.8 us (26%)
  waiting for transfers between devices  21 us (15%)
  other arithmetic  1.96 us (1%)
  local copies, waits for them, and re-layouts  1.92 us (1%)
    all_to_all x1, blocking collectives, exchange(): return lax.all_to_all(blocks, 'seq', 0, 0, axis_index_groups=groups)  34.8 us
    ppermute x9, waiting for transfers between devices, swap(): lax.ppermute(block, axis, [(i, i ^ by) for i in range(lax.axis_size(axis))])  17.4 us
    pallas_call x1, Pallas kernels, inner(): pl.pallas_call(inner_kernel, out_shape=RESULT, in_specs=[SCALAR, SCALAR,...  16.3 us
    ppermute x9, starting transfers between devices, swap(): lax.ppermute(block, axis, [(i, i ^ by) for i in range(lax.axis_size(axis))])  15 us
    ppermute x6, starting transfers between devices, ahead(): return lax.ppermute(block, 'seq', [(i, to(i)) for i in range(count)])  13.2 us
    pallas_call x1, Pallas kernels, edge(): pl.pallas_call(edge_grads_kernel, out_shape=RESULT[0], in_specs=specs + [...  6.44 us
    pallas_call x1, Pallas kernels, pack(): call(pack_kernel, shapes, [SCALAR] + [WHOLE] * 5, scratch, 1000, ALL_VMEM)  5 us
    ppermute x2, starting transfers between devices, shift(): lax.ppermute(block, 'seq', [(i, i + by) for i in range(count) if 0 <= i +...  4.99 us
  transfers between devices with their start and end apart: 18, of which 6 were waited for; matrix products, arithmetic and copies ran while one was open for 0% of the time, Pallas kernels for 24%

profile of v4, /device:TPU:1, one launch (start us, length us, event | category | flops | bytes accessed | tf_op | source)
XLA Modules:
  0.0 136.0 jit_solution(3356020813493052721)
XLA Ops:
  1.3 5.0 %shard_map.93 = (bf16[8,576,256]{2,1,0:T(8,128)(2,1)}, bf16[576,256]{1,0:T(8,128)(2,1)}, bf16[576,256]{1,0:T(8,128)(2,1)}) custom-call(s32[4]{0:T(128)} %pad_add_fusion.at_ref.place_ref, bf16[256,1152]{1,0:T(8,128)(2,1)} %bitcast.11, bf16[256,1152]{1,0:T(8,128)(2,1)} %bitcast.12, bf16[256,1152]{1,0:T(8,128)(2,1)} %bitcast.13, bf16[256,1152]{1,0:T(8,128)(2,1)} %bitcast.14, ...), custom_call_target="tpu_custom_call" | custom-call | flops 1000 | bytes 1000 | tf_op jit(solution)/shard_map/pallas_call | solution.py:72
  6.3 34.8 %all_to_all.10.mid_ref = bf16[8,576,256]{2,1,0:T(8,128)(2,1)S(1)} all-to-all(bf16[8,576,256]{2,1,0:T(8,128)(2,1)} %get-tuple-element.28), channel_id=1, replica_groups={{0,1,2,3,4,5,6,7},{8,9,10,11,12,13,14,15},{16,17,18,19,20,21,22,23},{24..., dimensions={0} | all-to-all | bytes 4718592 | tf_op jit(solution)/shard_map/all_to_all | solution.py:415
  41.1 3.7 %collective-permute-start = (bf16[2,576,256]{2,1,0:T(8,128)(2,1)S(1)}, bf16[2,576,256]{2,1,0:T(8,128)(2,1)S(1)}, u32[]{:S(2)}, u32[]{:S(2)}) collective-permute-start(bf16[2,576,256]{2,1,0:T(8,128)(2,1)S(1)} %get-tuple-element.53), channel_id=1, source_target_pairs={{0,8},{1,9},{2,10},{3,11},{4,12},{5,13},{6,14},{7,15},{8,16},{9,17... | collective-permute-start | bytes 1769480 | tf_op jit(solution)/shard_map/ppermute | solution.py:406
  45.2 1.3 collective-permute-start.1
  46.6 4.8 %collective-permute-done.2 = bf16[576,256]{1,0:T(8,128)(2,1)S(1)} collective-permute-done((bf16[576,256]{1,0:T(8,128)(2,1)S(1)}, bf16[576,256]{1,0:T(8,128)(2,1)S(1)}, u32[]{:S(2)}, u32[]{:S(2)}) %collective-permute-start.2) | collective-permute-done | bytes 294944 | tf_op jit(solution)/shard_map/ppermute | solution.py:412
  53.0 2.4 %collective-permute-start.5 = (bf16[1152,256]{1,0:T(8,128)(2,1)S(1)}, bf16[1152,256]{1,0:T(8,128)(2,1)S(1)}, u32[]{:S(2)}, u32[]{:S(2)}) collective-permute-start(bf16[1152,256]{1,0:T(8,128)(2,1)S(1)} %constant_dynamic-update-slice_fusion.refs_0_), channel_id=1, source_target_pairs={{0,3},{1,2},{2,1},{3,0},{4,7},{5,6},{6,5},{7,4},{8,11},{9,10},{10,... | collective-permute-start | bytes 1769480 | tf_op jit(solution)/shard_map/ppermute | solution.py:412
  55.3 16.3 %shard_map.94 = (bf16[8,432,256]{2,1,0:T(8,128)(2,1)}, bf16[144,2048]{1,0:T(8,128)(2,1)S(1)}) custom-call(s32[4]{0:T(128)S(1)} %copy-done.3, s32[1,32]{1,0:T(1,128)S(1)} %copy-done.5, s32[1,32]{1,0:T(1,128)S(1)} %copy-done.5, bf16[8,576,256]{2,1,0:T(8,128)(2,1)S(1)} %all_to_all.10.mid_ref), custom_call_target="tpu_custom_call" | custom-call | flops 1000 | bytes 1000 | tf_op jit(solution)/shard_map/pallas_call | solution.py:210
  72.2 3.0 %shard_map.95.more_0_.edge_ref = bf16[144,1024]{1,0:T(8,128)(2,1)S(1)} custom-call(s32[4]{0:T(128)S(1)} %copy-done.3, s32[1,32]{1,0:T(1,128)S(1)} %copy-done.5, s32[1,32]{1,0:T(1,128)S(1)} %copy-done.5, bf16[8,576,256]{2,1,0:T(8,128)(2,1)S(1)} %all_to_all.10.mid_ref, bf16[2,576,256]{2,1,0:T(8,128)(2,1)S(1)} %collective-permute-done.left_ref, ...), custom_call_target="tpu_custom_call" | custom-call | flops 1000 | bytes 1000 | tf_op jit(solution)/shard_map/pallas_call | solution.py:306
  75.3 1.3 collective-permute-start.7
  77.4 6.4 %shard_map.96 = bf16[8,432,256]{2,1,0:T(8,128)(2,1)} custom-call(s32[4]{0:T(128)S(1)} %copy-done.3, s32[1,32]{1,0:T(1,128)S(1)} %copy-done.5, s32[1,32]{1,0:T(1,128)S(1)} %copy-done.5, bf16[8,576,256]{2,1,0:T(8,128)(2,1)S(1)} %all_to_all.10.mid_ref, bf16[2,576,256]{2,1,0:T(8,128)(2,1)S(1)} %collective-permute-done.left_ref, ...), custom_call_target="tpu_custom_call", output_to_operand_aliasing={{}: (6, {})} | custom-call | flops 1000 | bytes 1000 | tf_op jit(solution)/shard_map/pallas_call | solution.py:313
  83.9 5.4 %collective-permute-done.7.across_ref = bf16[144,1024]{1,0:T(8,128)(2,1)S(1)} collective-permute-done((bf16[144,1024]{1,0:T(8,128)(2,1)S(1)}, bf16[144,1024]{1,0:T(8,128)(2,1)S(1)}, u32[]{:S(2)}, u32[]{:S(2)}) %collective-permute-start.7) | collective-permute-done | bytes 294944 | tf_op jit(solution)/shard_map/ppermute | solution.py:412
  89.9 3.8 %all-to-all-start.1 = ((bf16[8,432,256]{2,1,0:T(8,128)(2,1)}), bf16[8,432,256]{2,1,0:T(8,128)(2,1)S(1)}, u32[]{:S(2)}, u32[]{:S(2)}) async-start(bf16[8,432,256]{2,1,0:T(8,128)(2,1)} %shard_map.96), calls=%async_computation.1 | async-start | bytes 3538944 | tf_op jit(solution)/shard_map/all_to_all | solution.py:415
  93.7 4.9 %shard_map.98 = (f32[144,288]{1,0:T(8,128)}, bf16[144,288]{1,0:T(8,128)(2,1)}, bf16[144,288]{1,0:T(8,128)(2,1)}, bf16[144,288]{1,0:T(8,128)(2,1)}) custom-call(s32[4]{0:T(128)} %pad_add_fusion.at_ref.place_ref, bf16[144,2048]{1,0:T(8,128)(2,1)} %copy-done.1, bf16[144,2048]{1,0:T(8,128)(2,1)} %copy-done.10, bf16[144,1024]{1,0:T(8,128)(2,1)} %copy-done, ...), custom_call_target="tpu_custom_call" | custom-call | flops 1000 | bytes 1000 | tf_op jit(solution)/shard_map/pallas_call | solution.py:366
  98.6 6.4 %collective-permute-start.9 = (bf16[144,288]{1,0:T(8,128)(2,1)}, bf16[144,288]{1,0:T(8,128)(2,1)S(1)}, u32[]{:S(2)}, u32[]{:S(2)}) collective-permute-start(bf16[144,288]{1,0:T(8,128)(2,1)} %get-tuple-element.40), channel_id=1, source_target_pairs={{0,16},{1,17},{2,18},{3,19},{4,20},{5,21},{6,22},{7,23},{8,24},{9,... | collective-permute-start | bytes 248840 | tf_op jit(solution)/shard_map/ppermute | solution.py:436
  105.0 2.0 %collective-permute-start.10 = (bf16[144,288]{1,0:T(8,128)(2,1)}, bf16[144,288]{1,0:T(8,128)(2,1)S(1)}, u32[]{:S(2)}, u32[]{:S(2)}) collective-permute-start(bf16[144,288]{1,0:T(8,128)(2,1)} %get-tuple-element.41), channel_id=1, source_target_pairs={{0,24},{1,25},{2,26},{3,27},{4,28},{5,29},{6,30},{7,31},{8,0},{9,1... | collective-permute-start | bytes 248840 | tf_op jit(solution)/shard_map/ppermute | solution.py:436
  107.0 1.5 %collective-permute-done.9.refs_2_ = bf16[144,288]{1,0:T(8,128)(2,1)S(1)} collective-permute-done((bf16[144,288]{1,0:T(8,128)(2,1)}, bf16[144,288]{1,0:T(8,128)(2,1)S(1)}, u32[]{:S(2)}, u32[]{:S(2)}) %collective-permute-start.9) | collective-permute-done | bytes 82976 | tf_op jit(solution)/shard_map/ppermute | solution.py:436
  110.7 1.2 collective-permute-start.11
  111.9 2.4 %collective-permute-start.12 = (f32[36,288]{1,0:T(8,128)S(1)}, f32[36,288]{1,0:T(8,128)S(1)}, u32[]{:S(2)}, u32[]{:S(2)}) collective-permute-start(f32[36,288]{1,0:T(8,128)S(1)} %get-tuple-element.43), channel_id=1, source_target_pairs={{0,2},{1,3},{2,0},{3,1},{4,6},{5,7},{6,4},{7,5},{8,10},{9,11},{10,... | collective-permute-start | bytes 124424 | tf_op jit(solution)/shard_map/ppermute | solution.py:436
  114.3 1.2 collective-permute-start.13
  115.5 1.6 %all-to-all-done.1.back_ref = bf16[8,432,256]{2,1,0:T(8,128)(2,1)S(1)} async-done(((bf16[8,432,256]{2,1,0:T(8,128)(2,1)}), bf16[8,432,256]{2,1,0:T(8,128)(2,1)S(1)}, u32[]{:S(2)}, u32[]{:S(2)}) %all-to-all-start.1) | async-done | bytes 1769504 | tf_op jit(solution)/shard_map/all_to_all | solution.py:415
  117.1 1.4 %shard_map.97 = (bf16[256,1152]{1,0:T(8,128)(2,1)}, bf16[256,1152]{1,0:T(8,128)(2,1)}, bf16[256,1152]{1,0:T(8,128)(2,1)}) custom-call(bf16[8,432,256]{2,1,0:T(8,128)(2,1)S(1)} %all-to-all-done.1.back_ref), custom_call_target="tpu_custom_call" | custom-call | flops 1000 | bytes 1000 | tf_op jit(solution)/shard_map/pallas_call | solution.py:332
  119.2 3.7 %collective-permute-start.15 = (f32[36,1152]{1,0:T(8,128)S(1)}, f32[36,1152]{1,0:T(8,128)S(1)}, u32[]{:S(2)}, u32[]{:S(2)}) collective-permute-start(f32[36,1152]{1,0:T(8,128)S(1)} %shard_map.100), channel_id=1, source_target_pairs={{0,64},{32,96},{64,0},{96,32},{1,65},{33,97},{65,1},{97,33},{2,66}... | collective-permute-start | bytes 497672 | tf_op jit(solution)/shard_map/ppermute | solution.py:412
  122.9 5.1 %collective-permute-start.16 = (f32[36,1152]{1,0:T(8,128)S(1)}, f32[36,1152]{1,0:T(8,128)S(1)}, u32[]{:S(2)}, u32[]{:S(2)}) collective-permute-start(f32[36,1152]{1,0:T(8,128)S(1)} %shard_map.100), channel_id=1, source_target_pairs={{0,96},{32,64},{64,32},{96,0},{1,97},{33,65},{65,33},{97,1},{2,98}... | collective-permute-start | bytes 497672 | tf_op jit(solution)/shard_map/ppermute | solution.py:412
  128.1 7.2 %collective-permute-done.16 = f32[36,1152]{1,0:T(8,128)S(1)} collective-permute-done((f32[36,1152]{1,0:T(8,128)S(1)}, f32[36,1152]{1,0:T(8,128)S(1)}, u32[]{:S(2)}, u32[]{:S(2)}) %collective-permute-start.16) | collective-permute-done | bytes 165920 | tf_op jit(solution)/shard_map/ppermute | solution.py:412
  (58 shorter events, 8.3 us)
Async XLA Ops:
  41.1 14.3 %copy-start.3 = (s32[4]{0:T(128)S(1)}, s32[4]{0:T(128)}, u32[]{:S(2)}) copy-start(s32[4]{0:T(128)} %pad_add_fusion.at_ref.place_ref) | copy-start | bytes 52
  41.1 14.3 %copy-start.5 = (s32[1,32]{1,0:T(1,128)S(1)}, s32[1,32]{1,0:T(1,128)}, u32[]{:S(2)}) copy-start(s32[1,32]{1,0:T(1,128)} %length_ref.5) | copy-start | bytes 388
  41.1 30.5 %collective-permute-start = (bf16[2,576,256]{2,1,0:T(8,128)(2,1)S(1)}, bf16[2,576,256]{2,1,0:T(8,128)(2,1)S(1)}, u32[]{:S(2)}, u32[]{:S(2)}) collective-permute-start(bf16[2,576,256]{2,1,0:T(8,128)(2,1)S(1)} %get-tuple-element.53), channel_id=1, source_target_pairs={{0,8},{1,9},{2,10},{3,11},{4,12},{5,13},{6,14},{7,15},{8,16},{9,17... | collective-permute-start | bytes 1769480 | tf_op jit(solution)/shard_map/ppermute | solution.py:406
  44.9 6.5 %collective-permute-start.2 = (bf16[576,256]{1,0:T(8,128)(2,1)S(1)}, bf16[576,256]{1,0:T(8,128)(2,1)S(1)}, u32[]{:S(2)}, u32[]{:S(2)}) collective-permute-start(bf16[576,256]{1,0:T(8,128)(2,1)S(1)} %copy-done.13), channel_id=1, source_target_pairs={{0,4},{1,5},{2,6},{3,7},{4,0},{5,1},{6,2},{7,3},{8,12},{9,13},{10,... | collective-permute-start | bytes 884744 | tf_op jit(solution)/shard_map/ppermute | solution.py:412
  45.2 27.0 %collective-permute-start.1 = (bf16[2,576,256]{2,1,0:T(8,128)(2,1)S(1)}, bf16[2,576,256]{2,1,0:T(8,128)(2,1)S(1)}, u32[]{:S(2)}, u32[]{:S(2)}) collective-permute-start(bf16[2,576,256]{2,1,0:T(8,128)(2,1)S(1)} %get-tuple-element.52), channel_id=1, source_target_pairs={{8,0},{9,1},{10,2},{11,3},{12,4},{13,5},{14,6},{15,7},{16,8},{17,9... | collective-permute-start | bytes 1769480 | tf_op jit(solution)/shard_map/ppermute | solution.py:406
  51.4 23.9 %copy-start.6 = (bf16[1152,256]{1,0:T(8,128)(2,1)}, bf16[1152,256]{1,0:T(8,128)(2,1)S(1)}, u32[]{:S(2)}) copy-start(bf16[1152,256]{1,0:T(8,128)(2,1)S(1)} %constant_dynamic-update-slice_fusion.refs_0_) | copy-start | bytes 1769476
  51.4 25.2 %collective-permute-start.3 = (bf16[1152,256]{1,0:T(8,128)(2,1)S(1)}, bf16[1152,256]{1,0:T(8,128)(2,1)S(1)}, u32[]{:S(2)}, u32[]{:S(2)}) collective-permute-start(bf16[1152,256]{1,0:T(8,128)(2,1)S(1)} %constant_dynamic-update-slice_fusion.refs_0_), channel_id=1, source_target_pairs={{0,1},{1,0},{2,3},{3,2},{4,5},{5,4},{6,7},{7,6},{8,9},{9,8},{10,11... | collective-permute-start | bytes 1769480 | tf_op jit(solution)/shard_map/ppermute | solution.py:412
  52.3 25.1 %collective-permute-start.4 = (bf16[1152,256]{1,0:T(8,128)(2,1)S(1)}, bf16[1152,256]{1,0:T(8,128)(2,1)S(1)}, u32[]{:S(2)}, u32[]{:S(2)}) collective-permute-start(bf16[1152,256]{1,0:T(8,128)(2,1)S(1)} %constant_dynamic-update-slice_fusion.refs_0_), channel_id=1, source_target_pairs={{0,2},{1,3},{2,0},{3,1},{4,6},{5,7},{6,4},{7,5},{8,10},{9,11},{10,... | collective-permute-start | bytes 1769480 | tf_op jit(solution)/shard_map/ppermute | solution.py:412
  53.0 24.4 %collective-permute-start.5 = (bf16[1152,256]{1,0:T(8,128)(2,1)S(1)}, bf16[1152,256]{1,0:T(8,128)(2,1)S(1)}, u32[]{:S(2)}, u32[]{:S(2)}) collective-permute-start(bf16[1152,256]{1,0:T(8,128)(2,1)S(1)} %constant_dynamic-update-slice_fusion.refs_0_), channel_id=1, source_target_pairs={{0,3},{1,2},{2,1},{3,0},{4,7},{5,6},{6,5},{7,4},{8,11},{9,10},{10,... | collective-permute-start | bytes 1769480 | tf_op jit(solution)/shard_map/ppermute | solution.py:412
  71.7 12.2 %copy-start.1 = (bf16[144,2048]{1,0:T(8,128)(2,1)}, bf16[144,2048]{1,0:T(8,128)(2,1)S(1)}, u32[]{:S(2)}) copy-start(bf16[144,2048]{1,0:T(8,128)(2,1)S(1)} %get-tuple-element.32.mine_ref) | copy-start | bytes 1769476
  71.7 12.2 %collective-permute-start.6 = (bf16[144,2048]{1,0:T(8,128)(2,1)S(1)}, bf16[144,2048]{1,0:T(8,128)(2,1)S(1)}, u32[]{:S(2)}, u32[]{:S(2)}) collective-permute-start(bf16[144,2048]{1,0:T(8,128)(2,1)S(1)} %get-tuple-element.32.mine_ref), channel_id=1, source_target_pairs={{0,4},{1,5},{2,6},{3,7},{4,0},{5,1},{6,2},{7,3},{8,12},{9,13},{10,... | collective-permute-start | bytes 1769480 | tf_op jit(solution)/shard_map/ppermute | solution.py:412
  75.3 8.6 %copy-start = (bf16[144,1024]{1,0:T(8,128)(2,1)}, bf16[144,1024]{1,0:T(8,128)(2,1)S(1)}, u32[]{:S(2)}) copy-start(bf16[144,1024]{1,0:T(8,128)(2,1)S(1)} %shard_map.95.more_0_.edge_ref) | copy-start | bytes 884740
  75.3 14.0 %collective-permute-start.7 = (bf16[144,1024]{1,0:T(8,128)(2,1)S(1)}, bf16[144,1024]{1,0:T(8,128)(2,1)S(1)}, u32[]{:S(2)}, u32[]{:S(2)}) collective-permute-start(bf16[144,1024]{1,0:T(8,128)(2,1)S(1)} %shard_map.95.more_0_.edge_ref), channel_id=1, source_target_pairs={{0,4},{1,5},{2,6},{3,7},{4,0},{5,1},{6,2},{7,3},{8,12},{9,13},{10,... | collective-permute-start | bytes 884744 | tf_op jit(solution)/shard_map/ppermute | solution.py:412
  89.9 27.2 %all-to-all-start.1 = ((bf16[8,432,256]{2,1,0:T(8,128)(2,1)}), bf16[8,432,256]{2,1,0:T(8,128)(2,1)S(1)}, u32[]{:S(2)}, u32[]{:S(2)}) async-start(bf16[8,432,256]{2,1,0:T(8,128)(2,1)} %shard_map.96), calls=%async_computation.1 | async-start | bytes 3538944 | tf_op jit(solution)/shard_map/all_to_all | solution.py:415
  93.7 15.4 %copy-start.4 = (s32[4]{0:T(128)S(1)}, s32[4]{0:T(128)}, u32[]{:S(2)}) copy-start(s32[4]{0:T(128)} %pad_add_fusion.at_ref.place_ref) | copy-start | bytes 52
  98.6 8.4 %collective-permute-start.8 = (bf16[144,288]{1,0:T(8,128)(2,1)}, bf16[144,288]{1,0:T(8,128)(2,1)S(1)}, u32[]{:S(2)}, u32[]{:S(2)}) collective-permute-start(bf16[144,288]{1,0:T(8,128)(2,1)} %get-tuple-element.39), channel_id=1, source_target_pairs={{0,8},{1,9},{2,10},{3,11},{4,12},{5,13},{6,14},{7,15},{8,16},{9,17... | collective-permute-start | bytes 248840 | tf_op jit(solution)/shard_map/ppermute | solution.py:436
  98.6 9.9 %collective-permute-start.9 = (bf16[144,288]{1,0:T(8,128)(2,1)}, bf16[144,288]{1,0:T(8,128)(2,1)S(1)}, u32[]{:S(2)}, u32[]{:S(2)}) collective-permute-start(bf16[144,288]{1,0:T(8,128)(2,1)} %get-tuple-element.40), channel_id=1, source_target_pairs={{0,16},{1,17},{2,18},{3,19},{4,20},{5,21},{6,22},{7,23},{8,24},{9,... | collective-permute-start | bytes 248840 | tf_op jit(solution)/shard_map/ppermute | solution.py:436
  105.0 4.1 %collective-permute-start.10 = (bf16[144,288]{1,0:T(8,128)(2,1)}, bf16[144,288]{1,0:T(8,128)(2,1)S(1)}, u32[]{:S(2)}, u32[]{:S(2)}) collective-permute-start(bf16[144,288]{1,0:T(8,128)(2,1)} %get-tuple-element.41), channel_id=1, source_target_pairs={{0,24},{1,25},{2,26},{3,27},{4,28},{5,29},{6,30},{7,31},{8,0},{9,1... | collective-permute-start | bytes 248840 | tf_op jit(solution)/shard_map/ppermute | solution.py:436
  110.7 7.8 %collective-permute-start.11 = (f32[36,288]{1,0:T(8,128)S(1)}, f32[36,288]{1,0:T(8,128)S(1)}, u32[]{:S(2)}, u32[]{:S(2)}) collective-permute-start(f32[36,288]{1,0:T(8,128)S(1)} %get-tuple-element.42), channel_id=1, source_target_pairs={{0,1},{1,2},{2,3},{3,0},{4,5},{5,6},{6,7},{7,4},{8,9},{9,10},{10,1... | collective-permute-start | bytes 124424 | tf_op jit(solution)/shard_map/ppermute | solution.py:436
  111.9 6.6 %collective-permute-start.12 = (f32[36,288]{1,0:T(8,128)S(1)}, f32[36,288]{1,0:T(8,128)S(1)}, u32[]{:S(2)}, u32[]{:S(2)}) collective-permute-start(f32[36,288]{1,0:T(8,128)S(1)} %get-tuple-element.43), channel_id=1, source_target_pairs={{0,2},{1,3},{2,0},{3,1},{4,6},{5,7},{6,4},{7,5},{8,10},{9,11},{10,... | collective-permute-start | bytes 124424 | tf_op jit(solution)/shard_map/ppermute | solution.py:436
  114.3 4.2 %collective-permute-start.13 = (f32[36,288]{1,0:T(8,128)S(1)}, f32[36,288]{1,0:T(8,128)S(1)}, u32[]{:S(2)}, u32[]{:S(2)}) collective-permute-start(f32[36,288]{1,0:T(8,128)S(1)} %get-tuple-element.44), channel_id=1, source_target_pairs={{0,3},{1,0},{2,1},{3,2},{4,7},{5,4},{6,5},{7,6},{8,11},{9,8},{10,9... | collective-permute-start | bytes 124424 | tf_op jit(solution)/shard_map/ppermute | solution.py:436
  119.2 8.9 %collective-permute-start.15 = (f32[36,1152]{1,0:T(8,128)S(1)}, f32[36,1152]{1,0:T(8,128)S(1)}, u32[]{:S(2)}, u32[]{:S(2)}) collective-permute-start(f32[36,1152]{1,0:T(8,128)S(1)} %shard_map.100), channel_id=1, source_target_pairs={{0,64},{32,96},{64,0},{96,32},{1,65},{33,97},{65,1},{97,33},{2,66}... | collective-permute-start | bytes 497672 | tf_op jit(solution)/shard_map/ppermute | solution.py:412
  122.9 12.3 %collective-permute-start.16 = (f32[36,1152]{1,0:T(8,128)S(1)}, f32[36,1152]{1,0:T(8,128)S(1)}, u32[]{:S(2)}, u32[]{:S(2)}) collective-permute-start(f32[36,1152]{1,0:T(8,128)S(1)} %shard_map.100), channel_id=1, source_target_pairs={{0,96},{32,64},{64,32},{96,0},{1,97},{33,65},{65,33},{97,1},{2,98}... | collective-permute-start | bytes 497672 | tf_op jit(solution)/shard_map/ppermute | solution.py:412
  128.1 7.2 %collective-permute-start.14 = (f32[36,1152]{1,0:T(8,128)S(1)}, f32[36,1152]{1,0:T(8,128)S(1)}, u32[]{:S(2)}, u32[]{:S(2)}) collective-permute-start(f32[36,1152]{1,0:T(8,128)S(1)} %shard_map.100), channel_id=1, source_target_pairs={{0,32},{32,0},{64,96},{96,64},{1,33},{33,1},{65,97},{97,65},{2,34}... | collective-permute-start | bytes 497672 | tf_op jit(solution)/shard_map/ppermute | solution.py:412
  (8 other events, 33.8 us)

commit v5 on v4

--- a/solution.py
+++ b/solution.py
@@ -52,12 +52,11 @@
     )
 
 
-def pack_kernel(at_ref, q_ref, k_ref, v_ref, go_ref, proj_ref, out_ref, same_ref, other_ref, turned_go):
-    turned_go[...] = jnp.transpose(go_ref[...])
-    for z in range(4):
-        for y, half_ref in ((at_ref[1], same_ref), (1 - at_ref[1], other_ref)):
-            begin = pl.multiple_of((2 * z + y) * PAIR, PAIR)
-            half_ref[z * PAIR : (z + 1) * PAIR, :] = turned_go[pl.ds(begin, PAIR), :]
+def pack_kernel(q_ref, k_ref, v_ref, go_ref, proj_ref, out_ref, *halves):
+    go = jnp.transpose(go_ref[...])
+    for y, half_ref in enumerate(halves):
+        for z in range(4):
+            half_ref[z * PAIR : (z + 1) * PAIR, :] = go[(2 * z + y) * PAIR : (2 * z + y + 1) * PAIR]
     d_attn = jnp.transpose(dot(go_ref[...], proj_ref[...], NN).astype(BF16))
     turned = [jnp.transpose(ref[...]) for ref in (q_ref, k_ref, v_ref)] + [d_attn]
     for at in range(4):
@@ -65,13 +64,10 @@
             out_ref[g, at * PAIR : (at + 1) * PAIR, :] = turned[at][g * PAIR : (g + 1) * PAIR]
 
 
-def pack(at, q, k, v, go, proj):
+def pack(q, k, v, go, proj):
     half = jax.ShapeDtypeStruct((SLAB, ROWS), BF16)
     shapes = (jax.ShapeDtypeStruct((GROUP, SLAB, ROWS), BF16), half, half)
-    scratch = [pltpu.VMEM((WIDTH, ROWS), BF16)]
-    return call(pack_kernel, shapes, [SCALAR] + [WHOLE] * 5, scratch, 1000, ALL_VMEM)(
-        at, q, k, v, go, proj
-    )
+    return call(pack_kernel, shapes, [WHOLE] * 5, [], 1000, ALL_VMEM)(q, k, v, go, proj)
 
 
 def weigh(slab, marks):
@@ -220,7 +216,7 @@
             pltpu.SemaphoreType.DMA((GROUP + 1,)),
         ],
         compiler_params=pltpu.CompilerParams(vmem_limit_bytes=VMEM_LIMIT),
-        cost_estimate=pl.CostEstimate(flops=1000, bytes_accessed=1000, transcendentals=0),
+        cost_estimate=pl.CostEstimate(flops=20 * 10**9, bytes_accessed=1000, transcendentals=0),
     )(place, lengths, lengths, mid)
 
 
@@ -270,18 +266,19 @@
     return pl.ds(pl.multiple_of((1 - side) * WINDOW, WINDOW), WINDOW)
 
 
-def edge_attn_kernel(place_ref, count_ref, length_ref, mid_ref, left_ref, right_ref, attn_ref, frame):
+def edge_attn_kernel(
+    place_ref, count_ref, length_ref, mid_ref, left_ref, right_ref, attn_in, _, attn_ref, frame
+):
     def step(slab, marks):
         return jnp.concatenate([attn for _, _, attn in weigh(slab, marks)[1]], axis=0)
 
     mine = edge_image(place_ref, count_ref, length_ref, mid_ref, left_ref, right_ref, frame, step)
-    attn_ref[...] = frame[:PAIR, mine]
+    attn_ref[...] = (attn_in[...].astype(F32) + frame[:PAIR, mine].astype(F32)).astype(BF16)
 
 
 def edge_grads_kernel(
-    place_ref, count_ref, length_ref, mid_ref, left_ref, right_ref, grads_in, *more
+    place_ref, count_ref, length_ref, mid_ref, left_ref, right_ref, grads_in, _, grads_ref, frame
 ):
-    grads_ref, frame = more[-2:]
     mine = edge_image(place_ref, count_ref, length_ref, mid_ref, left_ref, right_ref, frame, attend)
     found = frame[:GRADS, mine]
     for at in range(2):
@@ -289,35 +286,29 @@
         grads_ref[at] = (grads_in[at].astype(F32) + term.astype(F32)).astype(BF16)
 
 
-def edge(place, lengths, mid, left, right, grads=None, after=()):
+def edge(place, lengths, mid, left, right, inner_part, after):
     ends = lambda rows: pl.BlockSpec((2, rows, ROWS), lambda i: (i * (GROUP // 2 - 1), 0, 0))
     halo = pl.BlockSpec((2, SLAB, ROWS), lambda i: (0, 0, 0))
-    specs = [SCALAR, SCALAR, pl.BlockSpec((1, IMAGES), lambda i: (0, 0)), ends(SLAB), halo, halo]
-    args = (place, lengths, lengths, mid, left, right)
-    more = dict(
+    kernel, part, flops = edge_grads_kernel, ends(GRADS), 20 * 10**9
+    if inner_part.ndim == 2:
+        last = SPAN // WINDOW - 1
+        kernel, part, flops = edge_attn_kernel, pl.BlockSpec((PAIR, WINDOW), lambda i: (0, i * last)), 1000
+    return pl.pallas_call(
+        kernel,
         grid=(2,),
+        out_shape=jax.ShapeDtypeStruct(inner_part.shape, BF16),
+        in_specs=[
+            SCALAR, SCALAR, pl.BlockSpec((1, IMAGES), lambda i: (0, 0)), ends(SLAB), halo, halo, part,
+            pl.BlockSpec(memory_space=pl.ANY),
+        ],
+        out_specs=part,
+        input_output_aliases={6: 0},
         scratch_shapes=[pltpu.VMEM((SLAB, EDGE), BF16)],
         compiler_params=pltpu.CompilerParams(
             vmem_limit_bytes=VMEM_LIMIT, dimension_semantics=("arbitrary",)
         ),
-        cost_estimate=pl.CostEstimate(flops=1000, bytes_accessed=1000, transcendentals=0),
-    )
-    if grads is None:
-        return pl.pallas_call(
-            edge_attn_kernel,
-            out_shape=jax.ShapeDtypeStruct((PAIR, EDGE), BF16),
-            in_specs=specs,
-            out_specs=pl.BlockSpec((PAIR, WINDOW), lambda i: (0, i)),
-            **more,
-        )(*args)
-    return pl.pallas_call(
-        edge_grads_kernel,
-        out_shape=RESULT[0],
-        in_specs=specs + [ends(GRADS)] + [pl.BlockSpec(memory_space=pl.ANY)] * len(after),
-        out_specs=ends(GRADS),
-        input_output_aliases={6: 0},
-        **more,
-    )(*args, grads, *after)
+        cost_estimate=pl.CostEstimate(flops=flops, bytes_accessed=1000, transcendentals=0),
+    )(place, lengths, lengths, mid, left, right, inner_part, after)
 
 
 def unpack_kernel(back_ref, *out_refs):
@@ -332,37 +323,28 @@
     return call(unpack_kernel, (shape,) * 3, [WHOLE], [], 1000)(back)
 
 
-def proj_kernel(at_ref, mine_ref, other_ref, edge_ref, across_ref, _, *refs):
-    rows, outs, (attn, total) = refs[:4], refs[4:-2], refs[-2:]
+def proj_kernel(at_ref, mine_ref, other_ref, _, *refs):
+    rows, outs, (attn, total) = refs[:GROUP], refs[GROUP:-2], refs[-2:]
     first = at_ref[1] == 0
-
-    def columns(mine, other):
-        return jnp.concatenate([jnp.where(first, mine, other), jnp.where(first, other, mine)], axis=0)
-
-    inner_attn = columns(mine_ref[...], other_ref[...])
-    edges = columns(edge_ref[...], across_ref[...]).astype(F32)
-    low = inner_attn[:, :WINDOW].astype(F32) + edges[:, :WINDOW]
-    high = inner_attn[:, SPAN - WINDOW :].astype(F32) + edges[:, WINDOW:]
-    attn[:, :WINDOW] = low.astype(BF16)
-    attn[:, WINDOW : SPAN - WINDOW] = inner_attn[:, WINDOW : SPAN - WINDOW]
-    attn[:, SPAN - WINDOW :] = high.astype(BF16)
+    mine, other = mine_ref[...], other_ref[...]
+    attn[:PAIR, :] = jnp.where(first, mine, other)
+    attn[PAIR:, :] = jnp.where(first, other, mine)
     found = jnp.zeros((SLAB, 2 * PAIR), F32)
     for k in range(GROUP):
         begin = pl.multiple_of((at_ref[3] ^ k) * ROWS, ROWS)
-        part = rows[k % 4][k // 4 * SLAB : (k // 4 + 1) * SLAB, :]
-        found = found + dot(part, attn[:, pl.ds(begin, ROWS)], NT)
+        found = found + dot(rows[k][...], attn[:, pl.ds(begin, ROWS)], NT)
     total[...] = found
     for k, out_ref in enumerate(outs):
         begin = pl.multiple_of(lax.rem(at_ref[0] + k, 4) * PAIR, PAIR)
         out_ref[...] = total[pl.ds(begin, PAIR), :].astype(out_ref.dtype)
 
 
-def partial_proj(at, rows, mine, other, edges, across, token):
+def partial_proj(at, rows, mine, other, token):
     block = lambda dtype: jax.ShapeDtypeStruct((PAIR, 2 * PAIR), dtype)
     shapes = (block(F32),) + (block(BF16),) * 3
     scratch = [pltpu.VMEM((2 * PAIR, SPAN), BF16), pltpu.VMEM((SLAB, 2 * PAIR), F32)]
-    specs = [SCALAR] + [WHOLE] * 4 + [pl.BlockSpec(memory_space=pl.ANY)] + [WHOLE] * 4
-    args = (at, mine, other, edges, across, token, *rows)
+    specs = [SCALAR] + [WHOLE] * 2 + [pl.BlockSpec(memory_space=pl.ANY)] + [WHOLE] * GROUP
+    args = (at, mine, other, token, *rows)
     return call(proj_kernel, shapes, specs, scratch, 1000, ALL_VMEM)(*args)
 
 
@@ -370,16 +352,25 @@
     return sum(jnp.where(at == j, block, 0.0) for j, block in enumerate(blocks))
 
 
-def sum_z_kernel(at_ref, *refs):
-    total = refs[0][...] + sum(ref[...].astype(F32) for ref in refs[1:4])
+def sum_kernel(*refs):
+    refs[4][...] = refs[0][...] + sum(ref[...].astype(F32) for ref in refs[1:4])
+
+
+def sum_z(terms):
+    shape = jax.ShapeDtypeStruct((PAIR, 2 * PAIR), F32)
+    return call(sum_kernel, shape, [WHOLE] * 4, [], 1000)(*terms)
+
+
+def pick_x_kernel(at_ref, one_ref, two_ref, *outs):
+    total = one_ref[...] + two_ref[...]
     blocks = [total[j * 36 : (j + 1) * 36] for j in range(4)]
-    for k, out_ref in enumerate(refs[4:]):
+    for k, out_ref in enumerate(outs):
         out_ref[...] = select(blocks, lax.rem(at_ref[2] + k, 4))
 
 
-def sum_z(at, terms):
+def pick_x(at, one, two):
     shape = jax.ShapeDtypeStruct((36, 2 * PAIR), F32)
-    return call(sum_z_kernel, (shape,) * 4, [SCALAR] + [WHOLE] * 4, [], 1000)(at, *terms)
+    return call(pick_x_kernel, (shape,) * 4, [SCALAR] + [WHOLE] * 2, [], 1000)(at, one, two)
 
 
 def join_x_kernel(at_ref, *refs):
@@ -414,33 +405,36 @@
     def exchange(blocks, groups):
         return lax.all_to_all(blocks, "seq", 0, 0, axis_index_groups=groups)
 
-    packed, same, across_y = pack(place, query[0], key[0], value[0], grad_out[0], out_proj)
+    packed, low, high = pack(query[0], key[0], value[0], grad_out[0], out_proj)
     mid = exchange(packed, within_z)
-    rows = jnp.concatenate([same, swap(across_y, "seq", 4)], axis=0)
-    rows = [rows] + [swap(rows, "seq", k) for k in range(1, 4)]
-    tokens = [corner(block) for block in rows[1:]]
+    first = place[1] == 0
+    same = jnp.where(first, low, high)
+    near = [same] + [swap(same, "seq", k) for k in range(1, 4)]
+    across_y = swap(jnp.where(first, high, low), "seq", 4)
+    far = [across_y] + [swap(across_y, "seq", k) for k in range(1, 4)]
     left = shift(mid[GROUP - 2 :], GROUP)
     right = shift(mid[:2], -GROUP)
     grads, attn = inner(place, lengths, mid)
+    token = corner(attn) + corner(near[1]) + corner(near[2])
+    attn = edge(place, lengths, mid, left, right, attn, token)
     other = swap(attn, "seq", 4)
-    edges = edge(place, lengths, mid, left, right)
-    across = swap(edges, "seq", 4)
-    grads = edge(place, lengths, mid, left, right, grads, [edges] + tokens)
-    token = corner(other) + corner(across)
+    grads = edge(place, lengths, mid, left, right, grads, corner(attn))
+    token = corner(other) + sum(corner(block) for block in near[3:] + far[1:])
     grads, token = lax.optimization_barrier((grads, token))
     grads = exchange(grads, within_z)
-    part, *away = partial_proj(place, rows, attn, other, edges, across, token)
+    part, *away = partial_proj(place, near + far, attn, other, token)
 
     def ahead(block, step, k):
         to = lambda i: i + ((i // step + k) % 4 - i // step % 4) * step
         return lax.ppermute(block, "seq", [(i, to(i)) for i in range(count)])
 
-    part, *away = sum_z(place, [part] + [ahead(b, GROUP, k + 1) for k, b in enumerate(away)])
+    part = sum_z([part] + [ahead(b, GROUP, k + 1) for k, b in enumerate(away)])
+    part, *away = pick_x(place, part, swap(part, "dp", 1))
     away = [ahead(b, 1, k + 1) for k, b in enumerate(away)]
     grads = unpack(grads)
     grads, away = lax.optimization_barrier((grads, away))
     part = join_x(place, [part] + away)
-    part = (part + swap(part, "dp", 1)) + (swap(part, "dp", 2) + swap(part, "dp", 3))
+    part = part + swap(part, "dp", 2)
     return (*(g[None] for g in grads), part)
 
 

time: 136 us -> 130 us (0.956)
  the two profiles are of different devices: /device:TPU:1 before, /device:TPU:94 now
where the time goes in v5:
time: 130 us; the launch traced here: 132 us
  waiting for transfers between devices  60 us (46%)
  Pallas kernels  36.1 us (28%)
  starting transfers between devices  31 us (24%)
  local copies, waits for them, and re-layouts  2.31 us (2%)
  other arithmetic  1.47 us (1%)
    all_to_all x2, waiting for transfers between devices, exchange(): return lax.all_to_all(blocks, 'seq', 0, 0, axis_index_groups=groups)  37.2 us
    ppermute x10, waiting for transfers between devices, swap(): lax.ppermute(block, axis, [(i, i ^ by) for i in range(lax.axis_size(axis))])  15.3 us
    pallas_call x2, Pallas kernels, edge(): pl.pallas_call(kernel, grid=(2,), out_shape=jax.ShapeDtypeStruct(inner_pa...  13.2 us
    all_to_all x2, starting transfers between devices, exchange(): return lax.all_to_all(blocks, 'seq', 0, 0, axis_index_groups=groups)  12.7 us
    pallas_call x1, Pallas kernels, inner(): pl.pallas_call(inner_kernel, out_shape=RESULT, in_specs=[SCALAR, SCALAR,...  10.7 us
    ppermute x6, waiting for transfers between devices, ahead(): return lax.ppermute(block, 'seq', [(i, to(i)) for i in range(count)])  7.53 us
    ppermute x10, starting transfers between devices, swap(): lax.ppermute(block, axis, [(i, i ^ by) for i in range(lax.axis_size(axis))])  7.43 us
    ppermute x2, starting transfers between devices, shift(): lax.ppermute(block, 'seq', [(i, i + by) for i in range(count) if 0 <= i +...  5.84 us
  transfers between devices with their start and end apart: 20, of which 9 were waited for; matrix products, arithmetic and copies ran while one was open for 0% of the time, Pallas kernels for 23%

profile of v5, /device:TPU:94, one launch (start us, length us, event | category | flops | bytes accessed | tf_op | source)
XLA Modules:
  0.0 131.7 jit_solution(9219714177106832485)
XLA Ops:
  0.6 5.0 %shard_map.93 = (bf16[8,576,256]{2,1,0:T(8,128)(2,1)}, bf16[576,256]{1,0:T(8,128)(2,1)}, bf16[576,256]{1,0:T(8,128)(2,1)}) custom-call(bf16[256,1152]{1,0:T(8,128)(2,1)} %bitcast.11, bf16[256,1152]{1,0:T(8,128)(2,1)} %bitcast.12, bf16[256,1152]{1,0:T(8,128)(2,1)} %bitcast.13, bf16[256,1152]{1,0:T(8,128)(2,1)} %bitcast.14, bf16[1152,1152]{1,0:T(8,128)(2,1)} %proj_ref.1), custom_call_target="tpu_custom_call" | custom-call | flops 1000 | bytes 1000 | tf_op jit(solution)/shard_map/pallas_call | solution.py:70
  5.6 5.8 %all-to-all-start = ((bf16[8,576,256]{2,1,0:T(8,128)(2,1)}), bf16[8,576,256]{2,1,0:T(8,128)(2,1)S(1)}, u32[]{:S(2)}, u32[]{:S(2)}) async-start(bf16[8,576,256]{2,1,0:T(8,128)(2,1)} %get-tuple-element.28), calls=%async_computation | async-start | bytes 4718592 | tf_op jit(solution)/shard_map/all_to_all | solution.py:406
  11.5 1.5 %collective-permute-start.3 = (bf16[576,256]{1,0:T(8,128)(2,1)S(1)}, bf16[576,256]{1,0:T(8,128)(2,1)S(1)}, u32[]{:S(2)}, u32[]{:S(2)}) collective-permute-start(bf16[576,256]{1,0:T(8,128)(2,1)S(1)} %get-tuple-element.55.refs_0_), channel_id=1, source_target_pairs={{0,2},{1,3},{2,0},{3,1},{4,6},{5,7},{6,4},{7,5},{8,10},{9,11},{10,... | collective-permute-start | bytes 884744 | tf_op jit(solution)/shard_map/ppermute | solution.py:403
  13.7 31.2 %all-to-all-done.mid_ref = bf16[8,576,256]{2,1,0:T(8,128)(2,1)S(1)} async-done(((bf16[8,576,256]{2,1,0:T(8,128)(2,1)}), bf16[8,576,256]{2,1,0:T(8,128)(2,1)S(1)}, u32[]{:S(2)}, u32[]{:S(2)}) %all-to-all-start) | async-done | bytes 2359328 | tf_op jit(solution)/shard_map/all_to_all | solution.py:406
  45.0 3.5 %collective-permute-start = (bf16[2,576,256]{2,1,0:T(8,128)(2,1)S(1)}, bf16[2,576,256]{2,1,0:T(8,128)(2,1)S(1)}, u32[]{:S(2)}, u32[]{:S(2)}) collective-permute-start(bf16[2,576,256]{2,1,0:T(8,128)(2,1)S(1)} %get-tuple-element.53), channel_id=1, source_target_pairs={{0,8},{1,9},{2,10},{3,11},{4,12},{5,13},{6,14},{7,15},{8,16},{9,17... | collective-permute-start | bytes 1769480 | tf_op jit(solution)/shard_map/ppermute | solution.py:397
  48.5 2.3 %collective-permute-start.1 = (bf16[2,576,256]{2,1,0:T(8,128)(2,1)S(1)}, bf16[2,576,256]{2,1,0:T(8,128)(2,1)S(1)}, u32[]{:S(2)}, u32[]{:S(2)}) collective-permute-start(bf16[2,576,256]{2,1,0:T(8,128)(2,1)S(1)} %get-tuple-element.52), channel_id=1, source_target_pairs={{8,0},{9,1},{10,2},{11,3},{12,4},{13,5},{14,6},{15,7},{16,8},{17,9... | collective-permute-start | bytes 1769480 | tf_op jit(solution)/shard_map/ppermute | solution.py:397
  50.9 10.7 %shard_map.94 = (bf16[8,432,256]{2,1,0:T(8,128)(2,1)S(1)}, bf16[144,2048]{1,0:T(8,128)(2,1)S(1)}) custom-call(s32[4]{0:T(128)S(1)} %pad_add_fusion.place_ref.at_ref, s32[1,32]{1,0:T(1,128)S(1)} %copy-done.5, s32[1,32]{1,0:T(1,128)S(1)} %copy-done.5, bf16[8,576,256]{2,1,0:T(8,128)(2,1)S(1)} %all-to-all-done.mid_ref), custom_call_target="tpu_custom_call" | custom-call | flops 20000000000 | bytes 1000 | tf_op jit(solution)/shard_map/pallas_call | solution.py:206
  61.7 3.2 %collective-permute-start.9 = (bf16[576,256]{1,0:T(8,128)(2,1)}, bf16[576,256]{1,0:T(8,128)(2,1)S(1)}, u32[]{:S(2)}, u32[]{:S(2)}) collective-permute-start(bf16[576,256]{1,0:T(8,128)(2,1)} %collective-permute-done.6.refs_4_), channel_id=1, source_target_pairs={{0,3},{1,2},{2,1},{3,0},{4,7},{5,6},{6,5},{7,4},{8,11},{9,10},{10,... | collective-permute-start | bytes 884744 | tf_op jit(solution)/shard_map/ppermute | solution.py:403
  65.0 1.2 collective-permute-start.7
  66.2 4.9 %shard_map.95.mine_ref = bf16[144,2048]{1,0:T(8,128)(2,1)S(1)} custom-call(s32[4]{0:T(128)S(1)} %pad_add_fusion.place_ref.at_ref, s32[1,32]{1,0:T(1,128)S(1)} %copy-done.5, s32[1,32]{1,0:T(1,128)S(1)} %copy-done.5, bf16[8,576,256]{2,1,0:T(8,128)(2,1)S(1)} %all-to-all-done.mid_ref, ...), custom_call_target="tpu_custom_call", output_to_operand_aliasing={{}: (6, {})} | custom-call | flops 1000 | bytes 1000 | tf_op jit(solution)/shard_map/pallas_call | solution.py:296
  71.7 8.3 %shard_map.96 = bf16[8,432,256]{2,1,0:T(8,128)(2,1)S(1)} custom-call(s32[4]{0:T(128)S(1)} %pad_add_fusion.place_ref.at_ref, s32[1,32]{1,0:T(1,128)S(1)} %copy-done.5, s32[1,32]{1,0:T(1,128)S(1)} %copy-done.5, bf16[8,576,256]{2,1,0:T(8,128)(2,1)S(1)} %all-to-all-done.mid_ref, ...), custom_call_target="tpu_custom_call", output_to_operand_aliasing={{}: (6, {})} | custom-call | flops 20000000000 | bytes 1000 | tf_op jit(solution)/shard_map/pallas_call | solution.py:296
  80.1 1.2 copy-done.1
  81.3 1.9 %collective-permute-done.9.refs_7_ = bf16[576,256]{1,0:T(8,128)(2,1)S(1)} collective-permute-done((bf16[576,256]{1,0:T(8,128)(2,1)}, bf16[576,256]{1,0:T(8,128)(2,1)S(1)}, u32[]{:S(2)}, u32[]{:S(2)}) %collective-permute-start.9) | collective-permute-done | bytes 294944 | tf_op jit(solution)/shard_map/ppermute | solution.py:403
  83.3 3.8 %collective-permute-done.4.other_ref = bf16[144,2048]{1,0:T(8,128)(2,1)S(1)} collective-permute-done((bf16[144,2048]{1,0:T(8,128)(2,1)S(1)}, bf16[144,2048]{1,0:T(8,128)(2,1)S(1)}, u32[]{:S(2)}, u32[]{:S(2)}) %collective-permute-start.4) | collective-permute-done | bytes 589856 | tf_op jit(solution)/shard_map/ppermute | solution.py:403
  87.8 6.9 %all-to-all-start.1 = ((bf16[8,432,256]{2,1,0:T(8,128)(2,1)}), bf16[8,432,256]{2,1,0:T(8,128)(2,1)S(1)}, u32[]{:S(2)}, u32[]{:S(2)}) async-start(bf16[8,432,256]{2,1,0:T(8,128)(2,1)} %copy-done.1), calls=%async_computation.1 | async-start | bytes 3538944 | tf_op jit(solution)/shard_map/all_to_all | solution.py:406
  94.7 4.4 %shard_map.98 = (f32[144,288]{1,0:T(8,128)}, bf16[144,288]{1,0:T(8,128)(2,1)}, bf16[144,288]{1,0:T(8,128)(2,1)}, bf16[144,288]{1,0:T(8,128)(2,1)}) custom-call(s32[4]{0:T(128)} %copy-done.3, bf16[144,2048]{1,0:T(8,128)(2,1)} %copy-done, bf16[144,2048]{1,0:T(8,128)(2,1)} %copy-done.7, bf16[16,128]{1,0:T(8,128)(2,1)} %fusion._, bf16[576,256]{1,0:T(8,128)(2,1)} %copy-done.6, ...), custom_call_target="tpu_custom_call" | custom-call | flops 1000 | bytes 1000 | tf_op jit(solution)/shard_map/pallas_call | solution.py:348
  99.1 1.9 %collective-permute-start.12 = (bf16[144,288]{1,0:T(8,128)(2,1)}, bf16[144,288]{1,0:T(8,128)(2,1)S(1)}, u32[]{:S(2)}, u32[]{:S(2)}) collective-permute-start(bf16[144,288]{1,0:T(8,128)(2,1)} %get-tuple-element.41), channel_id=1, source_target_pairs={{0,24},{1,25},{2,26},{3,27},{4,28},{5,29},{6,30},{7,31},{8,0},{9,1... | collective-permute-start | bytes 248840 | tf_op jit(solution)/shard_map/ppermute | solution.py:429
  101.1 5.3 %collective-permute-done.10.refs_1_ = bf16[144,288]{1,0:T(8,128)(2,1)S(1)} collective-permute-done((bf16[144,288]{1,0:T(8,128)(2,1)}, bf16[144,288]{1,0:T(8,128)(2,1)S(1)}, u32[]{:S(2)}, u32[]{:S(2)}) %collective-permute-start.10) | collective-permute-done | bytes 82976 | tf_op jit(solution)/shard_map/ppermute | solution.py:429
  106.4 1.8 %collective-permute-done.12.refs_3_ = bf16[144,288]{1,0:T(8,128)(2,1)S(1)} collective-permute-done((bf16[144,288]{1,0:T(8,128)(2,1)}, bf16[144,288]{1,0:T(8,128)(2,1)S(1)}, u32[]{:S(2)}, u32[]{:S(2)}) %collective-permute-start.12) | collective-permute-done | bytes 82976 | tf_op jit(solution)/shard_map/ppermute | solution.py:429
  109.3 1.5 %collective-permute-done.13.two_ref = f32[144,288]{1,0:T(8,128)S(1)} collective-permute-done((f32[144,288]{1,0:T(8,128)S(1)}, f32[144,288]{1,0:T(8,128)S(1)}, u32[]{:S(2)}, u32[]{:S(2)}) %collective-permute-start.13) | collective-permute-done | bytes 165920 | tf_op jit(solution)/shard_map/ppermute | solution.py:403
  112.1 2.4 %collective-permute-start.15 = (f32[36,288]{1,0:T(8,128)S(1)}, f32[36,288]{1,0:T(8,128)S(1)}, u32[]{:S(2)}, u32[]{:S(2)}) collective-permute-start(f32[36,288]{1,0:T(8,128)S(1)} %get-tuple-element.43), channel_id=1, source_target_pairs={{0,2},{1,3},{2,0},{3,1},{4,6},{5,7},{6,4},{7,5},{8,10},{9,11},{10,... | collective-permute-start | bytes 124424 | tf_op jit(solution)/shard_map/ppermute | solution.py:429
  114.4 6.0 %all-to-all-done.1.back_ref = bf16[8,432,256]{2,1,0:T(8,128)(2,1)S(1)} async-done(((bf16[8,432,256]{2,1,0:T(8,128)(2,1)}), bf16[8,432,256]{2,1,0:T(8,128)(2,1)S(1)}, u32[]{:S(2)}, u32[]{:S(2)}) %all-to-all-start.1) | async-done | bytes 1769504 | tf_op jit(solution)/shard_map/all_to_all | solution.py:406
  120.4 1.4 %shard_map.97 = (bf16[256,1152]{1,0:T(8,128)(2,1)}, bf16[256,1152]{1,0:T(8,128)(2,1)}, bf16[256,1152]{1,0:T(8,128)(2,1)}) custom-call(bf16[8,432,256]{2,1,0:T(8,128)(2,1)S(1)} %all-to-all-done.1.back_ref), custom_call_target="tpu_custom_call" | custom-call | flops 1000 | bytes 1000 | tf_op jit(solution)/shard_map/pallas_call | solution.py:323
  123.0 8.1 %collective-permute-done.17 = f32[36,1152]{1,0:T(8,128)S(1)} collective-permute-done((f32[36,1152]{1,0:T(8,128)S(1)}, f32[36,1152]{1,0:T(8,128)S(1)}, u32[]{:S(2)}, u32[]{:S(2)}) %collective-permute-start.17) | collective-permute-done | bytes 165920 | tf_op jit(solution)/shard_map/ppermute | solution.py:403
  (64 shorter events, 6.5 us)
Async XLA Ops:
  5.6 39.3 %all-to-all-start = ((bf16[8,576,256]{2,1,0:T(8,128)(2,1)}), bf16[8,576,256]{2,1,0:T(8,128)(2,1)S(1)}, u32[]{:S(2)}, u32[]{:S(2)}) async-start(bf16[8,576,256]{2,1,0:T(8,128)(2,1)} %get-tuple-element.28), calls=%async_computation | async-start | bytes 4718592 | tf_op jit(solution)/shard_map/all_to_all | solution.py:406
  11.4 39.4 %copy-start.5 = (s32[1,32]{1,0:T(1,128)S(1)}, s32[1,32]{1,0:T(1,128)}, u32[]{:S(2)}) copy-start(s32[1,32]{1,0:T(1,128)} %length_ref.5) | copy-start | bytes 388
  11.5 50.1 %copy-start.6 = (bf16[576,256]{1,0:T(8,128)(2,1)}, bf16[576,256]{1,0:T(8,128)(2,1)S(1)}, u32[]{:S(2)}) copy-start(bf16[576,256]{1,0:T(8,128)(2,1)S(1)} %get-tuple-element.55.refs_0_) | copy-start | bytes 884740
  11.5 50.1 %collective-permute-start.3 = (bf16[576,256]{1,0:T(8,128)(2,1)S(1)}, bf16[576,256]{1,0:T(8,128)(2,1)S(1)}, u32[]{:S(2)}, u32[]{:S(2)}) collective-permute-start(bf16[576,256]{1,0:T(8,128)(2,1)S(1)} %get-tuple-element.55.refs_0_), channel_id=1, source_target_pairs={{0,2},{1,3},{2,0},{3,1},{4,6},{5,7},{6,4},{7,5},{8,10},{9,11},{10,... | collective-permute-start | bytes 884744 | tf_op jit(solution)/shard_map/ppermute | solution.py:403
  13.0 51.9 %collective-permute-start.2 = (bf16[576,256]{1,0:T(8,128)(2,1)S(1)}, bf16[576,256]{1,0:T(8,128)(2,1)S(1)}, u32[]{:S(2)}, u32[]{:S(2)}) collective-permute-start(bf16[576,256]{1,0:T(8,128)(2,1)S(1)} %get-tuple-element.55.refs_0_), channel_id=1, source_target_pairs={{0,1},{1,0},{2,3},{3,2},{4,5},{5,4},{6,7},{7,6},{8,9},{9,8},{10,11... | collective-permute-start | bytes 884744 | tf_op jit(solution)/shard_map/ppermute | solution.py:403
  13.1 48.7 %collective-permute-start.6 = (bf16[576,256]{1,0:T(8,128)(2,1)S(1)}, bf16[576,256]{1,0:T(8,128)(2,1)}, u32[]{:S(2)}, u32[]{:S(2)}) collective-permute-start(bf16[576,256]{1,0:T(8,128)(2,1)S(1)} %get-tuple-element.54), channel_id=1, source_target_pairs={{0,4},{1,5},{2,6},{3,7},{4,0},{5,1},{6,2},{7,3},{8,12},{9,13},{10,... | collective-permute-start | bytes 884744 | tf_op jit(solution)/shard_map/ppermute | solution.py:403
  13.7 58.1 %copy-start.3 = (s32[4]{0:T(128)}, s32[4]{0:T(128)S(1)}, u32[]{:S(2)}) copy-start(s32[4]{0:T(128)S(1)} %pad_add_fusion.place_ref.at_ref) | copy-start | bytes 52
  45.0 20.0 %collective-permute-start = (bf16[2,576,256]{2,1,0:T(8,128)(2,1)S(1)}, bf16[2,576,256]{2,1,0:T(8,128)(2,1)S(1)}, u32[]{:S(2)}, u32[]{:S(2)}) collective-permute-start(bf16[2,576,256]{2,1,0:T(8,128)(2,1)S(1)} %get-tuple-element.53), channel_id=1, source_target_pairs={{0,8},{1,9},{2,10},{3,11},{4,12},{5,13},{6,14},{7,15},{8,16},{9,17... | collective-permute-start | bytes 1769480 | tf_op jit(solution)/shard_map/ppermute | solution.py:397
  48.5 17.7 %collective-permute-start.1 = (bf16[2,576,256]{2,1,0:T(8,128)(2,1)S(1)}, bf16[2,576,256]{2,1,0:T(8,128)(2,1)S(1)}, u32[]{:S(2)}, u32[]{:S(2)}) collective-permute-start(bf16[2,576,256]{2,1,0:T(8,128)(2,1)S(1)} %get-tuple-element.52), channel_id=1, source_target_pairs={{8,0},{9,1},{10,2},{11,3},{12,4},{13,5},{14,6},{15,7},{16,8},{17,9... | collective-permute-start | bytes 1769480 | tf_op jit(solution)/shard_map/ppermute | solution.py:397
  61.6 19.7 %collective-permute-start.5 = (bf16[576,256]{1,0:T(8,128)(2,1)S(1)}, bf16[576,256]{1,0:T(8,128)(2,1)S(1)}, u32[]{:S(2)}, u32[]{:S(2)}) collective-permute-start(bf16[576,256]{1,0:T(8,128)(2,1)S(1)} %get-tuple-element.55.refs_0_), channel_id=1, source_target_pairs={{0,3},{1,2},{2,1},{3,0},{4,7},{5,6},{6,5},{7,4},{8,11},{9,10},{10,... | collective-permute-start | bytes 884744 | tf_op jit(solution)/shard_map/ppermute | solution.py:403
  61.7 21.5 %collective-permute-start.9 = (bf16[576,256]{1,0:T(8,128)(2,1)}, bf16[576,256]{1,0:T(8,128)(2,1)S(1)}, u32[]{:S(2)}, u32[]{:S(2)}) collective-permute-start(bf16[576,256]{1,0:T(8,128)(2,1)} %collective-permute-done.6.refs_4_), channel_id=1, source_target_pairs={{0,3},{1,2},{2,1},{3,0},{4,7},{5,6},{6,5},{7,4},{8,11},{9,10},{10,... | collective-permute-start | bytes 884744 | tf_op jit(solution)/shard_map/ppermute | solution.py:403
  65.0 18.3 %collective-permute-start.8 = (bf16[576,256]{1,0:T(8,128)(2,1)}, bf16[576,256]{1,0:T(8,128)(2,1)S(1)}, u32[]{:S(2)}, u32[]{:S(2)}) collective-permute-start(bf16[576,256]{1,0:T(8,128)(2,1)} %collective-permute-done.6.refs_4_), channel_id=1, source_target_pairs={{0,2},{1,3},{2,0},{3,1},{4,6},{5,7},{6,4},{7,5},{8,10},{9,11},{10,... | collective-permute-start | bytes 884744 | tf_op jit(solution)/shard_map/ppermute | solution.py:403
  65.0 18.3 %collective-permute-start.7 = (bf16[576,256]{1,0:T(8,128)(2,1)}, bf16[576,256]{1,0:T(8,128)(2,1)S(1)}, u32[]{:S(2)}, u32[]{:S(2)}) collective-permute-start(bf16[576,256]{1,0:T(8,128)(2,1)} %collective-permute-done.6.refs_4_), channel_id=1, source_target_pairs={{0,1},{1,0},{2,3},{3,2},{4,5},{5,4},{6,7},{7,6},{8,9},{9,8},{10,11... | collective-permute-start | bytes 884744 | tf_op jit(solution)/shard_map/ppermute | solution.py:403
  71.1 16.0 %collective-permute-start.4 = (bf16[144,2048]{1,0:T(8,128)(2,1)S(1)}, bf16[144,2048]{1,0:T(8,128)(2,1)S(1)}, u32[]{:S(2)}, u32[]{:S(2)}) collective-permute-start(bf16[144,2048]{1,0:T(8,128)(2,1)S(1)} %shard_map.95.mine_ref), channel_id=1, source_target_pairs={{0,4},{1,5},{2,6},{3,7},{4,0},{5,1},{6,2},{7,3},{8,12},{9,13},{10,... | collective-permute-start | bytes 1769480 | tf_op jit(solution)/shard_map/ppermute | solution.py:403
  87.8 32.6 %all-to-all-start.1 = ((bf16[8,432,256]{2,1,0:T(8,128)(2,1)}), bf16[8,432,256]{2,1,0:T(8,128)(2,1)S(1)}, u32[]{:S(2)}, u32[]{:S(2)}) async-start(bf16[8,432,256]{2,1,0:T(8,128)(2,1)} %copy-done.1), calls=%async_computation.1 | async-start | bytes 3538944 | tf_op jit(solution)/shard_map/all_to_all | solution.py:406
  94.7 16.1 %copy-start.4 = (s32[4]{0:T(128)S(1)}, s32[4]{0:T(128)}, u32[]{:S(2)}) copy-start(s32[4]{0:T(128)} %copy-done.3) | copy-start | bytes 52
  99.0 7.4 %collective-permute-start.10 = (bf16[144,288]{1,0:T(8,128)(2,1)}, bf16[144,288]{1,0:T(8,128)(2,1)S(1)}, u32[]{:S(2)}, u32[]{:S(2)}) collective-permute-start(bf16[144,288]{1,0:T(8,128)(2,1)} %get-tuple-element.39), channel_id=1, source_target_pairs={{0,8},{1,9},{2,10},{3,11},{4,12},{5,13},{6,14},{7,15},{8,16},{9,17... | collective-permute-start | bytes 248840 | tf_op jit(solution)/shard_map/ppermute | solution.py:429
  99.0 7.4 %collective-permute-start.11 = (bf16[144,288]{1,0:T(8,128)(2,1)}, bf16[144,288]{1,0:T(8,128)(2,1)S(1)}, u32[]{:S(2)}, u32[]{:S(2)}) collective-permute-start(bf16[144,288]{1,0:T(8,128)(2,1)} %get-tuple-element.40), channel_id=1, source_target_pairs={{0,16},{1,17},{2,18},{3,19},{4,20},{5,21},{6,22},{7,23},{8,24},{9,... | collective-permute-start | bytes 248840 | tf_op jit(solution)/shard_map/ppermute | solution.py:429
  99.1 9.1 %collective-permute-start.12 = (bf16[144,288]{1,0:T(8,128)(2,1)}, bf16[144,288]{1,0:T(8,128)(2,1)S(1)}, u32[]{:S(2)}, u32[]{:S(2)}) collective-permute-start(bf16[144,288]{1,0:T(8,128)(2,1)} %get-tuple-element.41), channel_id=1, source_target_pairs={{0,24},{1,25},{2,26},{3,27},{4,28},{5,29},{6,30},{7,31},{8,0},{9,1... | collective-permute-start | bytes 248840 | tf_op jit(solution)/shard_map/ppermute | solution.py:429
  109.2 1.6 %collective-permute-start.13 = (f32[144,288]{1,0:T(8,128)S(1)}, f32[144,288]{1,0:T(8,128)S(1)}, u32[]{:S(2)}, u32[]{:S(2)}) collective-permute-start(f32[144,288]{1,0:T(8,128)S(1)} %shard_map.99.one_ref), channel_id=1, source_target_pairs={{0,32},{32,0},{64,96},{96,64},{1,33},{33,1},{65,97},{97,65},{2,34}... | collective-permute-start | bytes 497672 | tf_op jit(solution)/shard_map/ppermute | solution.py:403
  111.5 10.4 %collective-permute-start.14 = (f32[36,288]{1,0:T(8,128)S(1)}, f32[36,288]{1,0:T(8,128)S(1)}, u32[]{:S(2)}, u32[]{:S(2)}) collective-permute-start(f32[36,288]{1,0:T(8,128)S(1)} %get-tuple-element.42), channel_id=1, source_target_pairs={{0,1},{1,2},{2,3},{3,0},{4,5},{5,6},{6,7},{7,4},{8,9},{9,10},{10,1... | collective-permute-start | bytes 124424 | tf_op jit(solution)/shard_map/ppermute | solution.py:429
  112.1 9.8 %collective-permute-start.15 = (f32[36,288]{1,0:T(8,128)S(1)}, f32[36,288]{1,0:T(8,128)S(1)}, u32[]{:S(2)}, u32[]{:S(2)}) collective-permute-start(f32[36,288]{1,0:T(8,128)S(1)} %get-tuple-element.43), channel_id=1, source_target_pairs={{0,2},{1,3},{2,0},{3,1},{4,6},{5,7},{6,4},{7,5},{8,10},{9,11},{10,... | collective-permute-start | bytes 124424 | tf_op jit(solution)/shard_map/ppermute | solution.py:429
  114.4 7.7 %collective-permute-start.16 = (f32[36,288]{1,0:T(8,128)S(1)}, f32[36,288]{1,0:T(8,128)S(1)}, u32[]{:S(2)}, u32[]{:S(2)}) collective-permute-start(f32[36,288]{1,0:T(8,128)S(1)} %get-tuple-element.44), channel_id=1, source_target_pairs={{0,3},{1,0},{2,1},{3,2},{4,7},{5,4},{6,5},{7,6},{8,11},{9,8},{10,9... | collective-permute-start | bytes 124424 | tf_op jit(solution)/shard_map/ppermute | solution.py:429
  122.9 8.1 %collective-permute-start.17 = (f32[36,1152]{1,0:T(8,128)S(1)}, f32[36,1152]{1,0:T(8,128)S(1)}, u32[]{:S(2)}, u32[]{:S(2)}) collective-permute-start(f32[36,1152]{1,0:T(8,128)S(1)} %shard_map.101), channel_id=1, source_target_pairs={{0,64},{32,96},{64,0},{96,32},{1,65},{33,97},{65,1},{97,33},{2,66}... | collective-permute-start | bytes 497672 | tf_op jit(solution)/shard_map/ppermute | solution.py:403
  (12 other events, 63.2 us)

commit v6 on v5

--- a/solution.py
+++ b/solution.py
@@ -17,7 +17,6 @@
 SPAN = GROUP * ROWS
 WINDOW = 512
 SIZES = (256, 384, WINDOW)
-FILL = 256
 FRAME = SPAN + WINDOW
 EDGE = 2 * WINDOW
 SCALE = HEAD_DIM ** (-0.5)
@@ -145,7 +144,8 @@
         start, n, first = carry
         end = start + count_ref[0, i]
         inside = (start >= base) & (end <= base + SPAN)
-        opens = inside & ((n == 0) | (end - first > FILL))
+        short = (start - first <= SIZES[0]) & (end - start <= SIZES[0])
+        opens = inside & ((n == 0) | (end - first > jnp.where(short, SIZES[1], WINDOW)))
         n = jnp.where(opens, n + 1, n)
         first = jnp.where(opens, start, first)
 

time: 130 us -> 129 us (level)
  the two profiles are of different devices: /device:TPU:94 before, /device:TPU:1 now
where the time goes in v6:
time: 129 us; the launch traced here: 126 us
  waiting for transfers between devices  44.4 us (34%)
  starting transfers between devices  40 us (31%)
  Pallas kernels  36.5 us (28%)
  local copies, waits for them, and re-layouts  3.19 us (2%)
  other arithmetic  1.44 us (1%)
    all_to_all x2, waiting for transfers between devices, exchange(): return lax.all_to_all(blocks, 'seq', 0, 0, axis_index_groups=groups)  26.6 us
    pallas_call x1, Pallas kernels, inner(): pl.pallas_call(inner_kernel, out_shape=RESULT, in_specs=[SCALAR, SCALAR,...  17.4 us
    ppermute x10, starting transfers between devices, swap(): lax.ppermute(block, axis, [(i, i ^ by) for i in range(lax.axis_size(axis))])  16.8 us
    ppermute x10, waiting for transfers between devices, swap(): lax.ppermute(block, axis, [(i, i ^ by) for i in range(lax.axis_size(axis))])  13 us
    all_to_all x2, starting transfers between devices, exchange(): return lax.all_to_all(blocks, 'seq', 0, 0, axis_index_groups=groups)  10.5 us
    ppermute x6, starting transfers between devices, ahead(): return lax.ppermute(block, 'seq', [(i, to(i)) for i in range(count)])  7.77 us
    pallas_call x2, Pallas kernels, edge(): pl.pallas_call(kernel, grid=(2,), out_shape=jax.ShapeDtypeStruct(inner_pa...  6.98 us
    pallas_call x1, Pallas kernels, pack(): call(pack_kernel, shapes, [WHOLE] * 5, [], 1000, ALL_VMEM)  4.99 us
  transfers between devices with their start and end apart: 20, of which 8 were waited for; matrix products, arithmetic and copies ran while one was open for 0% of the time, Pallas kernels for 24%

profile of v6, /device:TPU:1, one launch (start us, length us, event | category | flops | bytes accessed | tf_op | source)
XLA Modules:
  0.0 126.4 jit_solution(572087315822138504)
XLA Ops:
  0.6 5.0 %shard_map.93 = (bf16[8,576,256]{2,1,0:T(8,128)(2,1)}, bf16[576,256]{1,0:T(8,128)(2,1)}, bf16[576,256]{1,0:T(8,128)(2,1)}) custom-call(bf16[256,1152]{1,0:T(8,128)(2,1)} %bitcast.11, bf16[256,1152]{1,0:T(8,128)(2,1)} %bitcast.12, bf16[256,1152]{1,0:T(8,128)(2,1)} %bitcast.13, bf16[256,1152]{1,0:T(8,128)(2,1)} %bitcast.14, bf16[1152,1152]{1,0:T(8,128)(2,1)} %proj_ref.1), custom_call_target="tpu_custom_call" | custom-call | flops 1000 | bytes 1000 | tf_op jit(solution)/shard_map/pallas_call | solution.py:69
  5.6 6.0 %all-to-all-start = ((bf16[8,576,256]{2,1,0:T(8,128)(2,1)}), bf16[8,576,256]{2,1,0:T(8,128)(2,1)S(1)}, u32[]{:S(2)}, u32[]{:S(2)}) async-start(bf16[8,576,256]{2,1,0:T(8,128)(2,1)} %get-tuple-element.28), calls=%async_computation | async-start | bytes 4718592 | tf_op jit(solution)/shard_map/all_to_all | solution.py:406
  11.7 3.0 %collective-permute-start.3 = (bf16[576,256]{1,0:T(8,128)(2,1)S(1)}, bf16[576,256]{1,0:T(8,128)(2,1)S(1)}, u32[]{:S(2)}, u32[]{:S(2)}) collective-permute-start(bf16[576,256]{1,0:T(8,128)(2,1)S(1)} %get-tuple-element.55.refs_0_), channel_id=1, source_target_pairs={{0,2},{1,3},{2,0},{3,1},{4,6},{5,7},{6,4},{7,5},{8,10},{9,11},{10,... | collective-permute-start | bytes 884744 | tf_op jit(solution)/shard_map/ppermute | solution.py:403
  16.3 25.2 %all-to-all-done.mid_ref = bf16[8,576,256]{2,1,0:T(8,128)(2,1)S(1)} async-done(((bf16[8,576,256]{2,1,0:T(8,128)(2,1)}), bf16[8,576,256]{2,1,0:T(8,128)(2,1)S(1)}, u32[]{:S(2)}, u32[]{:S(2)}) %all-to-all-start) | async-done | bytes 2359328 | tf_op jit(solution)/shard_map/all_to_all | solution.py:406
  41.6 3.6 %collective-permute-start = (bf16[2,576,256]{2,1,0:T(8,128)(2,1)S(1)}, bf16[2,576,256]{2,1,0:T(8,128)(2,1)S(1)}, u32[]{:S(2)}, u32[]{:S(2)}) collective-permute-start(bf16[2,576,256]{2,1,0:T(8,128)(2,1)S(1)} %get-tuple-element.53), channel_id=1, source_target_pairs={{0,8},{1,9},{2,10},{3,11},{4,12},{5,13},{6,14},{7,15},{8,16},{9,17... | collective-permute-start | bytes 1769480 | tf_op jit(solution)/shard_map/ppermute | solution.py:397
  45.2 1.3 %collective-permute-start.1 = (bf16[2,576,256]{2,1,0:T(8,128)(2,1)S(1)}, bf16[2,576,256]{2,1,0:T(8,128)(2,1)S(1)}, u32[]{:S(2)}, u32[]{:S(2)}) collective-permute-start(bf16[2,576,256]{2,1,0:T(8,128)(2,1)S(1)} %get-tuple-element.52), channel_id=1, source_target_pairs={{8,0},{9,1},{10,2},{11,3},{12,4},{13,5},{14,6},{15,7},{16,8},{17,9... | collective-permute-start | bytes 1769480 | tf_op jit(solution)/shard_map/ppermute | solution.py:397
  46.5 17.4 %shard_map.94 = (bf16[8,432,256]{2,1,0:T(8,128)(2,1)S(1)}, bf16[144,2048]{1,0:T(8,128)(2,1)S(1)}) custom-call(s32[4]{0:T(128)S(1)} %pad_add_fusion.place_ref.at_ref, s32[1,32]{1,0:T(1,128)S(1)} %copy-done.5, s32[1,32]{1,0:T(1,128)S(1)} %copy-done.5, bf16[8,576,256]{2,1,0:T(8,128)(2,1)S(1)} %all-to-all-done.mid_ref), custom_call_target="tpu_custom_call" | custom-call | flops 20000000000 | bytes 1000 | tf_op jit(solution)/shard_map/pallas_call | solution.py:206
  63.9 4.2 %collective-permute-start.5 = (bf16[576,256]{1,0:T(8,128)(2,1)S(1)}, bf16[576,256]{1,0:T(8,128)(2,1)S(1)}, u32[]{:S(2)}, u32[]{:S(2)}) collective-permute-start(bf16[576,256]{1,0:T(8,128)(2,1)S(1)} %get-tuple-element.55.refs_0_), channel_id=1, source_target_pairs={{0,3},{1,2},{2,1},{3,0},{4,7},{5,6},{6,5},{7,4},{8,11},{9,10},{10,... | collective-permute-start | bytes 884744 | tf_op jit(solution)/shard_map/ppermute | solution.py:403
  68.2 3.4 %collective-permute-start.7 = (bf16[576,256]{1,0:T(8,128)(2,1)}, bf16[576,256]{1,0:T(8,128)(2,1)S(1)}, u32[]{:S(2)}, u32[]{:S(2)}) collective-permute-start(bf16[576,256]{1,0:T(8,128)(2,1)} %collective-permute-done.6.refs_4_), channel_id=1, source_target_pairs={{0,1},{1,0},{2,3},{3,2},{4,5},{5,4},{6,7},{7,6},{8,9},{9,8},{10,11... | collective-permute-start | bytes 884744 | tf_op jit(solution)/shard_map/ppermute | solution.py:403
  71.6 2.8 %shard_map.95.mine_ref = bf16[144,2048]{1,0:T(8,128)(2,1)S(1)} custom-call(s32[4]{0:T(128)S(1)} %pad_add_fusion.place_ref.at_ref, s32[1,32]{1,0:T(1,128)S(1)} %copy-done.5, s32[1,32]{1,0:T(1,128)S(1)} %copy-done.5, bf16[8,576,256]{2,1,0:T(8,128)(2,1)S(1)} %all-to-all-done.mid_ref, ...), custom_call_target="tpu_custom_call", output_to_operand_aliasing={{}: (6, {})} | custom-call | flops 1000 | bytes 1000 | tf_op jit(solution)/shard_map/pallas_call | solution.py:296
  74.5 1.3 %collective-permute-start.4 = (bf16[144,2048]{1,0:T(8,128)(2,1)S(1)}, bf16[144,2048]{1,0:T(8,128)(2,1)S(1)}, u32[]{:S(2)}, u32[]{:S(2)}) collective-permute-start(bf16[144,2048]{1,0:T(8,128)(2,1)S(1)} %shard_map.95.mine_ref), channel_id=1, source_target_pairs={{0,4},{1,5},{2,6},{3,7},{4,0},{5,1},{6,2},{7,3},{8,12},{9,13},{10,... | collective-permute-start | bytes 1769480 | tf_op jit(solution)/shard_map/ppermute | solution.py:403
  75.8 4.2 %shard_map.96 = bf16[8,432,256]{2,1,0:T(8,128)(2,1)S(1)} custom-call(s32[4]{0:T(128)S(1)} %pad_add_fusion.place_ref.at_ref, s32[1,32]{1,0:T(1,128)S(1)} %copy-done.5, s32[1,32]{1,0:T(1,128)S(1)} %copy-done.5, bf16[8,576,256]{2,1,0:T(8,128)(2,1)S(1)} %all-to-all-done.mid_ref, ...), custom_call_target="tpu_custom_call", output_to_operand_aliasing={{}: (6, {})} | custom-call | flops 20000000000 | bytes 1000 | tf_op jit(solution)/shard_map/pallas_call | solution.py:296
  79.9 1.2 copy-done.1
  81.6 6.3 %collective-permute-done.9.refs_7_ = bf16[576,256]{1,0:T(8,128)(2,1)S(1)} collective-permute-done((bf16[576,256]{1,0:T(8,128)(2,1)}, bf16[576,256]{1,0:T(8,128)(2,1)S(1)}, u32[]{:S(2)}, u32[]{:S(2)}) %collective-permute-start.9) | collective-permute-done | bytes 294944 | tf_op jit(solution)/shard_map/ppermute | solution.py:403
  89.5 4.6 %all-to-all-start.1 = ((bf16[8,432,256]{2,1,0:T(8,128)(2,1)}), bf16[8,432,256]{2,1,0:T(8,128)(2,1)S(1)}, u32[]{:S(2)}, u32[]{:S(2)}) async-start(bf16[8,432,256]{2,1,0:T(8,128)(2,1)} %copy-done.1), calls=%async_computation.1 | async-start | bytes 3538944 | tf_op jit(solution)/shard_map/all_to_all | solution.py:406
  94.1 4.4 %shard_map.98 = (f32[144,288]{1,0:T(8,128)}, bf16[144,288]{1,0:T(8,128)(2,1)}, bf16[144,288]{1,0:T(8,128)(2,1)}, bf16[144,288]{1,0:T(8,128)(2,1)}) custom-call(s32[4]{0:T(128)} %copy-done.3, bf16[144,2048]{1,0:T(8,128)(2,1)} %copy-done, bf16[144,2048]{1,0:T(8,128)(2,1)} %copy-done.7, bf16[16,128]{1,0:T(8,128)(2,1)} %fusion._, bf16[576,256]{1,0:T(8,128)(2,1)} %copy-done.6, ...), custom_call_target="tpu_custom_call" | custom-call | flops 1000 | bytes 1000 | tf_op jit(solution)/shard_map/pallas_call | solution.py:348
  98.5 2.6 %collective-permute-start.12 = (bf16[144,288]{1,0:T(8,128)(2,1)}, bf16[144,288]{1,0:T(8,128)(2,1)S(1)}, u32[]{:S(2)}, u32[]{:S(2)}) collective-permute-start(bf16[144,288]{1,0:T(8,128)(2,1)} %get-tuple-element.41), channel_id=1, source_target_pairs={{0,24},{1,25},{2,26},{3,27},{4,28},{5,29},{6,30},{7,31},{8,0},{9,1... | collective-permute-start | bytes 248840 | tf_op jit(solution)/shard_map/ppermute | solution.py:429
  101.1 4.3 %collective-permute-done.10.refs_1_ = bf16[144,288]{1,0:T(8,128)(2,1)S(1)} collective-permute-done((bf16[144,288]{1,0:T(8,128)(2,1)}, bf16[144,288]{1,0:T(8,128)(2,1)S(1)}, u32[]{:S(2)}, u32[]{:S(2)}) %collective-permute-start.10) | collective-permute-done | bytes 82976 | tf_op jit(solution)/shard_map/ppermute | solution.py:429
  106.9 2.5 %collective-permute-start.13 = (f32[144,288]{1,0:T(8,128)S(1)}, f32[144,288]{1,0:T(8,128)S(1)}, u32[]{:S(2)}, u32[]{:S(2)}) collective-permute-start(f32[144,288]{1,0:T(8,128)S(1)} %shard_map.99.one_ref), channel_id=1, source_target_pairs={{0,32},{32,0},{64,96},{96,64},{1,33},{33,1},{65,97},{97,65},{2,34}... | collective-permute-start | bytes 497672 | tf_op jit(solution)/shard_map/ppermute | solution.py:403
  111.2 1.5 %collective-permute-start.14 = (f32[36,288]{1,0:T(8,128)S(1)}, f32[36,288]{1,0:T(8,128)S(1)}, u32[]{:S(2)}, u32[]{:S(2)}) collective-permute-start(f32[36,288]{1,0:T(8,128)S(1)} %get-tuple-element.42), channel_id=1, source_target_pairs={{0,1},{1,2},{2,3},{3,0},{4,5},{5,6},{6,7},{7,4},{8,9},{9,10},{10,1... | collective-permute-start | bytes 124424 | tf_op jit(solution)/shard_map/ppermute | solution.py:429
  112.7 2.4 %collective-permute-start.15 = (f32[36,288]{1,0:T(8,128)S(1)}, f32[36,288]{1,0:T(8,128)S(1)}, u32[]{:S(2)}, u32[]{:S(2)}) collective-permute-start(f32[36,288]{1,0:T(8,128)S(1)} %get-tuple-element.43), channel_id=1, source_target_pairs={{0,2},{1,3},{2,0},{3,1},{4,6},{5,7},{6,4},{7,5},{8,10},{9,11},{10,... | collective-permute-start | bytes 124424 | tf_op jit(solution)/shard_map/ppermute | solution.py:429
  116.3 1.3 %all-to-all-done.1.back_ref = bf16[8,432,256]{2,1,0:T(8,128)(2,1)S(1)} async-done(((bf16[8,432,256]{2,1,0:T(8,128)(2,1)}), bf16[8,432,256]{2,1,0:T(8,128)(2,1)S(1)}, u32[]{:S(2)}, u32[]{:S(2)}) %all-to-all-start.1) | async-done | bytes 1769504 | tf_op jit(solution)/shard_map/all_to_all | solution.py:406
  117.6 1.4 %shard_map.97 = (bf16[256,1152]{1,0:T(8,128)(2,1)}, bf16[256,1152]{1,0:T(8,128)(2,1)}, bf16[256,1152]{1,0:T(8,128)(2,1)}) custom-call(bf16[8,432,256]{2,1,0:T(8,128)(2,1)S(1)} %all-to-all-done.1.back_ref), custom_call_target="tpu_custom_call" | custom-call | flops 1000 | bytes 1000 | tf_op jit(solution)/shard_map/pallas_call | solution.py:323
  120.6 5.1 %collective-permute-done.17 = f32[36,1152]{1,0:T(8,128)S(1)} collective-permute-done((f32[36,1152]{1,0:T(8,128)S(1)}, f32[36,1152]{1,0:T(8,128)S(1)}, u32[]{:S(2)}, u32[]{:S(2)}) %collective-permute-start.17) | collective-permute-done | bytes 165920 | tf_op jit(solution)/shard_map/ppermute | solution.py:403
  (64 shorter events, 10.6 us)
Async XLA Ops:
  5.6 35.9 %all-to-all-start = ((bf16[8,576,256]{2,1,0:T(8,128)(2,1)}), bf16[8,576,256]{2,1,0:T(8,128)(2,1)S(1)}, u32[]{:S(2)}, u32[]{:S(2)}) async-start(bf16[8,576,256]{2,1,0:T(8,128)(2,1)} %get-tuple-element.28), calls=%async_computation | async-start | bytes 4718592 | tf_op jit(solution)/shard_map/all_to_all | solution.py:406
  11.6 34.9 %copy-start.5 = (s32[1,32]{1,0:T(1,128)S(1)}, s32[1,32]{1,0:T(1,128)}, u32[]{:S(2)}) copy-start(s32[1,32]{1,0:T(1,128)} %length_ref.5) | copy-start | bytes 388
  11.7 52.1 %copy-start.6 = (bf16[576,256]{1,0:T(8,128)(2,1)}, bf16[576,256]{1,0:T(8,128)(2,1)S(1)}, u32[]{:S(2)}) copy-start(bf16[576,256]{1,0:T(8,128)(2,1)S(1)} %get-tuple-element.55.refs_0_) | copy-start | bytes 884740
  11.7 52.1 %collective-permute-start.3 = (bf16[576,256]{1,0:T(8,128)(2,1)S(1)}, bf16[576,256]{1,0:T(8,128)(2,1)S(1)}, u32[]{:S(2)}, u32[]{:S(2)}) collective-permute-start(bf16[576,256]{1,0:T(8,128)(2,1)S(1)} %get-tuple-element.55.refs_0_), channel_id=1, source_target_pairs={{0,2},{1,3},{2,0},{3,1},{4,6},{5,7},{6,4},{7,5},{8,10},{9,11},{10,... | collective-permute-start | bytes 884744 | tf_op jit(solution)/shard_map/ppermute | solution.py:403
  14.7 53.4 %collective-permute-start.2 = (bf16[576,256]{1,0:T(8,128)(2,1)S(1)}, bf16[576,256]{1,0:T(8,128)(2,1)S(1)}, u32[]{:S(2)}, u32[]{:S(2)}) collective-permute-start(bf16[576,256]{1,0:T(8,128)(2,1)S(1)} %get-tuple-element.55.refs_0_), channel_id=1, source_target_pairs={{0,1},{1,0},{2,3},{3,2},{4,5},{5,4},{6,7},{7,6},{8,9},{9,8},{10,11... | collective-permute-start | bytes 884744 | tf_op jit(solution)/shard_map/ppermute | solution.py:403
  15.0 53.1 %collective-permute-start.6 = (bf16[576,256]{1,0:T(8,128)(2,1)S(1)}, bf16[576,256]{1,0:T(8,128)(2,1)}, u32[]{:S(2)}, u32[]{:S(2)}) collective-permute-start(bf16[576,256]{1,0:T(8,128)(2,1)S(1)} %get-tuple-element.54), channel_id=1, source_target_pairs={{0,4},{1,5},{2,6},{3,7},{4,0},{5,1},{6,2},{7,3},{8,12},{9,13},{10,... | collective-permute-start | bytes 884744 | tf_op jit(solution)/shard_map/ppermute | solution.py:403
  16.3 59.5 %copy-start.3 = (s32[4]{0:T(128)}, s32[4]{0:T(128)S(1)}, u32[]{:S(2)}) copy-start(s32[4]{0:T(128)S(1)} %pad_add_fusion.place_ref.at_ref) | copy-start | bytes 52
  41.6 26.6 %collective-permute-start = (bf16[2,576,256]{2,1,0:T(8,128)(2,1)S(1)}, bf16[2,576,256]{2,1,0:T(8,128)(2,1)S(1)}, u32[]{:S(2)}, u32[]{:S(2)}) collective-permute-start(bf16[2,576,256]{2,1,0:T(8,128)(2,1)S(1)} %get-tuple-element.53), channel_id=1, source_target_pairs={{0,8},{1,9},{2,10},{3,11},{4,12},{5,13},{6,14},{7,15},{8,16},{9,17... | collective-permute-start | bytes 1769480 | tf_op jit(solution)/shard_map/ppermute | solution.py:397
  45.2 26.4 %collective-permute-start.1 = (bf16[2,576,256]{2,1,0:T(8,128)(2,1)S(1)}, bf16[2,576,256]{2,1,0:T(8,128)(2,1)S(1)}, u32[]{:S(2)}, u32[]{:S(2)}) collective-permute-start(bf16[2,576,256]{2,1,0:T(8,128)(2,1)S(1)} %get-tuple-element.52), channel_id=1, source_target_pairs={{8,0},{9,1},{10,2},{11,3},{12,4},{13,5},{14,6},{15,7},{16,8},{17,9... | collective-permute-start | bytes 1769480 | tf_op jit(solution)/shard_map/ppermute | solution.py:397
  63.9 17.7 %collective-permute-start.5 = (bf16[576,256]{1,0:T(8,128)(2,1)S(1)}, bf16[576,256]{1,0:T(8,128)(2,1)S(1)}, u32[]{:S(2)}, u32[]{:S(2)}) collective-permute-start(bf16[576,256]{1,0:T(8,128)(2,1)S(1)} %get-tuple-element.55.refs_0_), channel_id=1, source_target_pairs={{0,3},{1,2},{2,1},{3,0},{4,7},{5,6},{6,5},{7,4},{8,11},{9,10},{10,... | collective-permute-start | bytes 884744 | tf_op jit(solution)/shard_map/ppermute | solution.py:403
  68.1 19.9 %collective-permute-start.9 = (bf16[576,256]{1,0:T(8,128)(2,1)}, bf16[576,256]{1,0:T(8,128)(2,1)S(1)}, u32[]{:S(2)}, u32[]{:S(2)}) collective-permute-start(bf16[576,256]{1,0:T(8,128)(2,1)} %collective-permute-done.6.refs_4_), channel_id=1, source_target_pairs={{0,3},{1,2},{2,1},{3,0},{4,7},{5,6},{6,5},{7,4},{8,11},{9,10},{10,... | collective-permute-start | bytes 884744 | tf_op jit(solution)/shard_map/ppermute | solution.py:403
  68.2 19.8 %collective-permute-start.8 = (bf16[576,256]{1,0:T(8,128)(2,1)}, bf16[576,256]{1,0:T(8,128)(2,1)S(1)}, u32[]{:S(2)}, u32[]{:S(2)}) collective-permute-start(bf16[576,256]{1,0:T(8,128)(2,1)} %collective-permute-done.6.refs_4_), channel_id=1, source_target_pairs={{0,2},{1,3},{2,0},{3,1},{4,6},{5,7},{6,4},{7,5},{8,10},{9,11},{10,... | collective-permute-start | bytes 884744 | tf_op jit(solution)/shard_map/ppermute | solution.py:403
  68.2 19.8 %collective-permute-start.7 = (bf16[576,256]{1,0:T(8,128)(2,1)}, bf16[576,256]{1,0:T(8,128)(2,1)S(1)}, u32[]{:S(2)}, u32[]{:S(2)}) collective-permute-start(bf16[576,256]{1,0:T(8,128)(2,1)} %collective-permute-done.6.refs_4_), channel_id=1, source_target_pairs={{0,1},{1,0},{2,3},{3,2},{4,5},{5,4},{6,7},{7,6},{8,9},{9,8},{10,11... | collective-permute-start | bytes 884744 | tf_op jit(solution)/shard_map/ppermute | solution.py:403
  74.5 13.5 %collective-permute-start.4 = (bf16[144,2048]{1,0:T(8,128)(2,1)S(1)}, bf16[144,2048]{1,0:T(8,128)(2,1)S(1)}, u32[]{:S(2)}, u32[]{:S(2)}) collective-permute-start(bf16[144,2048]{1,0:T(8,128)(2,1)S(1)} %shard_map.95.mine_ref), channel_id=1, source_target_pairs={{0,4},{1,5},{2,6},{3,7},{4,0},{5,1},{6,2},{7,3},{8,12},{9,13},{10,... | collective-permute-start | bytes 1769480 | tf_op jit(solution)/shard_map/ppermute | solution.py:403
  89.5 28.1 %all-to-all-start.1 = ((bf16[8,432,256]{2,1,0:T(8,128)(2,1)}), bf16[8,432,256]{2,1,0:T(8,128)(2,1)S(1)}, u32[]{:S(2)}, u32[]{:S(2)}) async-start(bf16[8,432,256]{2,1,0:T(8,128)(2,1)} %copy-done.1), calls=%async_computation.1 | async-start | bytes 3538944 | tf_op jit(solution)/shard_map/all_to_all | solution.py:406
  94.1 16.4 %copy-start.4 = (s32[4]{0:T(128)S(1)}, s32[4]{0:T(128)}, u32[]{:S(2)}) copy-start(s32[4]{0:T(128)} %copy-done.3) | copy-start | bytes 52
  98.5 7.0 %collective-permute-start.10 = (bf16[144,288]{1,0:T(8,128)(2,1)}, bf16[144,288]{1,0:T(8,128)(2,1)S(1)}, u32[]{:S(2)}, u32[]{:S(2)}) collective-permute-start(bf16[144,288]{1,0:T(8,128)(2,1)} %get-tuple-element.39), channel_id=1, source_target_pairs={{0,8},{1,9},{2,10},{3,11},{4,12},{5,13},{6,14},{7,15},{8,16},{9,17... | collective-permute-start | bytes 248840 | tf_op jit(solution)/shard_map/ppermute | solution.py:429
  98.5 7.0 %collective-permute-start.11 = (bf16[144,288]{1,0:T(8,128)(2,1)}, bf16[144,288]{1,0:T(8,128)(2,1)S(1)}, u32[]{:S(2)}, u32[]{:S(2)}) collective-permute-start(bf16[144,288]{1,0:T(8,128)(2,1)} %get-tuple-element.40), channel_id=1, source_target_pairs={{0,16},{1,17},{2,18},{3,19},{4,20},{5,21},{6,22},{7,23},{8,24},{9,... | collective-permute-start | bytes 248840 | tf_op jit(solution)/shard_map/ppermute | solution.py:429
  98.5 7.3 %collective-permute-start.12 = (bf16[144,288]{1,0:T(8,128)(2,1)}, bf16[144,288]{1,0:T(8,128)(2,1)S(1)}, u32[]{:S(2)}, u32[]{:S(2)}) collective-permute-start(bf16[144,288]{1,0:T(8,128)(2,1)} %get-tuple-element.41), channel_id=1, source_target_pairs={{0,24},{1,25},{2,26},{3,27},{4,28},{5,29},{6,30},{7,31},{8,0},{9,1... | collective-permute-start | bytes 248840 | tf_op jit(solution)/shard_map/ppermute | solution.py:429
  106.9 3.6 %collective-permute-start.13 = (f32[144,288]{1,0:T(8,128)S(1)}, f32[144,288]{1,0:T(8,128)S(1)}, u32[]{:S(2)}, u32[]{:S(2)}) collective-permute-start(f32[144,288]{1,0:T(8,128)S(1)} %shard_map.99.one_ref), channel_id=1, source_target_pairs={{0,32},{32,0},{64,96},{96,64},{1,33},{33,1},{65,97},{97,65},{2,34}... | collective-permute-start | bytes 497672 | tf_op jit(solution)/shard_map/ppermute | solution.py:403
  111.2 7.8 %collective-permute-start.14 = (f32[36,288]{1,0:T(8,128)S(1)}, f32[36,288]{1,0:T(8,128)S(1)}, u32[]{:S(2)}, u32[]{:S(2)}) collective-permute-start(f32[36,288]{1,0:T(8,128)S(1)} %get-tuple-element.42), channel_id=1, source_target_pairs={{0,1},{1,2},{2,3},{3,0},{4,5},{5,6},{6,7},{7,4},{8,9},{9,10},{10,1... | collective-permute-start | bytes 124424 | tf_op jit(solution)/shard_map/ppermute | solution.py:429
  112.7 6.3 %collective-permute-start.15 = (f32[36,288]{1,0:T(8,128)S(1)}, f32[36,288]{1,0:T(8,128)S(1)}, u32[]{:S(2)}, u32[]{:S(2)}) collective-permute-start(f32[36,288]{1,0:T(8,128)S(1)} %get-tuple-element.43), channel_id=1, source_target_pairs={{0,2},{1,3},{2,0},{3,1},{4,6},{5,7},{6,4},{7,5},{8,10},{9,11},{10,... | collective-permute-start | bytes 124424 | tf_op jit(solution)/shard_map/ppermute | solution.py:429
  115.1 3.9 %collective-permute-start.16 = (f32[36,288]{1,0:T(8,128)S(1)}, f32[36,288]{1,0:T(8,128)S(1)}, u32[]{:S(2)}, u32[]{:S(2)}) collective-permute-start(f32[36,288]{1,0:T(8,128)S(1)} %get-tuple-element.44), channel_id=1, source_target_pairs={{0,3},{1,0},{2,1},{3,2},{4,7},{5,4},{6,5},{7,6},{8,11},{9,8},{10,9... | collective-permute-start | bytes 124424 | tf_op jit(solution)/shard_map/ppermute | solution.py:429
  119.7 6.0 %collective-permute-start.17 = (f32[36,1152]{1,0:T(8,128)S(1)}, f32[36,1152]{1,0:T(8,128)S(1)}, u32[]{:S(2)}, u32[]{:S(2)}) collective-permute-start(f32[36,1152]{1,0:T(8,128)S(1)} %shard_map.101), channel_id=1, source_target_pairs={{0,64},{32,96},{64,0},{96,32},{1,65},{33,97},{65,1},{97,33},{2,66}... | collective-permute-start | bytes 497672 | tf_op jit(solution)/shard_map/ppermute | solution.py:403
  (12 other events, 50.6 us)

commit v7 on v6

--- a/solution.py
+++ b/solution.py
@@ -374,17 +374,19 @@
 
 
 def join_x_kernel(at_ref, *refs):
-    terms = [ref[...] for ref in refs[:4]]
+    terms, out_ref, joined = [ref[...] for ref in refs[:4]], refs[4], refs[5]
     for j in range(4):
         block = select(terms, lax.rem(at_ref[2] + 4 - j, 4))
         for y in range(2):
             begin = (4 * y + j) * PAIR
-            refs[4][:, begin : begin + PAIR] = block[:, y * PAIR : (y + 1) * PAIR]
+            joined[:, begin : begin + PAIR] = block[:, y * PAIR : (y + 1) * PAIR]
+    out_ref[...] = joined[...].astype(BF16)
 
 
 def join_x(at, terms):
-    shape = jax.ShapeDtypeStruct((36, WIDTH), F32)
-    return call(join_x_kernel, shape, [SCALAR] + [WHOLE] * 4, [], 1000)(at, *terms)
+    shape = jax.ShapeDtypeStruct((36, WIDTH), BF16)
+    scratch = [pltpu.VMEM((36, WIDTH), F32)]
+    return call(join_x_kernel, shape, [SCALAR] + [WHOLE] * 4, scratch, 1000)(at, *terms)
 
 
 def per_device(query, key, value, grad_out, out_proj, lengths):
@@ -434,7 +436,7 @@
     grads = unpack(grads)
     grads, away = lax.optimization_barrier((grads, away))
     part = join_x(place, [part] + away)
-    part = part + swap(part, "dp", 2)
+    part = part.astype(F32) + swap(part, "dp", 2).astype(F32)
     return (*(g[None] for g in grads), part)
 
 

time: 129 us -> 127 us (0.984)
  waiting for transfers between devices: 44.4 us -> 35.6 us
  starting transfers between devices: 40 us -> 48.3 us
  Pallas kernels: 36.5 us -> 34.8 us
    ppermute x10, waiting for transfers between devices: 13 us -> 5.66 us  [swap(): lax.ppermute(block, axis, [(i, i ^ by) for i in range(lax.axis_size(axis))])]
    ppermute x10, starting transfers between devices: 16.8 us -> 22.7 us  [swap(): lax.ppermute(block, axis, [(i, i ^ by) for i in range(lax.axis_size(axis))])]
    pallas_call x1, Pallas kernels: 17.4 us -> 14.6 us  [inner(): pl.pallas_call(inner_kernel, out_shape=RESULT, in_specs=[SCALAR, SCALAR,...]
    ppermute x6, starting transfers between devices: 7.77 us -> 9.87 us  [ahead(): return lax.ppermute(block, 'seq', [(i, to(i)) for i in range(count)])]
    all_to_all x2, waiting for transfers between devices: 26.6 us -> 25.2 us  [exchange(): return lax.all_to_all(blocks, 'seq', 0, 0, axis_index_groups=groups)]
  transfers between devices with their start and end apart: 20 -> 20, of which waited for: 8 -> 9; matrix products, arithmetic and copies ran while one was open for 0% -> 0% of each run, Pallas kernels for 24% -> 23%
where the time goes in v7:
time: 127 us; the launch traced here: 124 us
  starting transfers between devices  48.3 us (38%)
  waiting for transfers between devices  35.6 us (28%)
  Pallas kernels  34.8 us (27%)
  local copies, waits for them, and re-layouts  3.2 us (3%)
  other arithmetic  1.44 us (1%)
    all_to_all x2, waiting for transfers between devices, exchange(): return lax.all_to_all(blocks, 'seq', 0, 0, axis_index_groups=groups)  25.2 us
    ppermute x10, starting transfers between devices, swap(): lax.ppermute(block, axis, [(i, i ^ by) for i in range(lax.axis_size(axis))])  22.7 us
    pallas_call x1, Pallas kernels, inner(): pl.pallas_call(inner_kernel, out_shape=RESULT, in_specs=[SCALAR, SCALAR,...  14.6 us
    all_to_all x2, starting transfers between devices, exchange(): return lax.all_to_all(blocks, 'seq', 0, 0, axis_index_groups=groups)  10.9 us
    ppermute x6, starting transfers between devices, ahead(): return lax.ppermute(block, 'seq', [(i, to(i)) for i in range(count)])  9.87 us
    pallas_call x2, Pallas kernels, edge(): pl.pallas_call(kernel, grid=(2,), out_shape=jax.ShapeDtypeStruct(inner_pa...  8.07 us
    ppermute x10, waiting for transfers between devices, swap(): lax.ppermute(block, axis, [(i, i ^ by) for i in range(lax.axis_size(axis))])  5.66 us
    pallas_call x1, Pallas kernels, pack(): call(pack_kernel, shapes, [WHOLE] * 5, [], 1000, ALL_VMEM)  4.99 us
  transfers between devices with their start and end apart: 20, of which 9 were waited for; matrix products, arithmetic and copies ran while one was open for 0% of the time, Pallas kernels for 23%

profile of v7, /device:TPU:1, one launch (start us, length us, event | category | flops | bytes accessed | tf_op | source)
XLA Modules:
  0.0 124.3 jit_solution(10446088205096705662)
XLA Ops:
  0.6 5.0 %shard_map.93 = (bf16[8,576,256]{2,1,0:T(8,128)(2,1)}, bf16[576,256]{1,0:T(8,128)(2,1)}, bf16[576,256]{1,0:T(8,128)(2,1)}) custom-call(bf16[256,1152]{1,0:T(8,128)(2,1)} %bitcast.11, bf16[256,1152]{1,0:T(8,128)(2,1)} %bitcast.12, bf16[256,1152]{1,0:T(8,128)(2,1)} %bitcast.13, bf16[256,1152]{1,0:T(8,128)(2,1)} %bitcast.14, bf16[1152,1152]{1,0:T(8,128)(2,1)} %proj_ref.1), custom_call_target="tpu_custom_call" | custom-call | flops 1000 | bytes 1000 | tf_op jit(solution)/shard_map/pallas_call | solution.py:69
  5.6 6.0 %all-to-all-start = ((bf16[8,576,256]{2,1,0:T(8,128)(2,1)}), bf16[8,576,256]{2,1,0:T(8,128)(2,1)S(1)}, u32[]{:S(2)}, u32[]{:S(2)}) async-start(bf16[8,576,256]{2,1,0:T(8,128)(2,1)} %get-tuple-element.28), calls=%async_computation | async-start | bytes 4718592 | tf_op jit(solution)/shard_map/all_to_all | solution.py:408
  11.7 3.0 %collective-permute-start.3 = (bf16[576,256]{1,0:T(8,128)(2,1)S(1)}, bf16[576,256]{1,0:T(8,128)(2,1)S(1)}, u32[]{:S(2)}, u32[]{:S(2)}) collective-permute-start(bf16[576,256]{1,0:T(8,128)(2,1)S(1)} %get-tuple-element.55.refs_0_), channel_id=1, source_target_pairs={{0,2},{1,3},{2,0},{3,1},{4,6},{5,7},{6,4},{7,5},{8,10},{9,11},{10,... | collective-permute-start | bytes 884744 | tf_op jit(solution)/shard_map/ppermute | solution.py:405
  16.3 25.2 %all-to-all-done.mid_ref = bf16[8,576,256]{2,1,0:T(8,128)(2,1)S(1)} async-done(((bf16[8,576,256]{2,1,0:T(8,128)(2,1)}), bf16[8,576,256]{2,1,0:T(8,128)(2,1)S(1)}, u32[]{:S(2)}, u32[]{:S(2)}) %all-to-all-start) | async-done | bytes 2359328 | tf_op jit(solution)/shard_map/all_to_all | solution.py:408
  41.6 3.6 %collective-permute-start = (bf16[2,576,256]{2,1,0:T(8,128)(2,1)S(1)}, bf16[2,576,256]{2,1,0:T(8,128)(2,1)S(1)}, u32[]{:S(2)}, u32[]{:S(2)}) collective-permute-start(bf16[2,576,256]{2,1,0:T(8,128)(2,1)S(1)} %get-tuple-element.53), channel_id=1, source_target_pairs={{0,8},{1,9},{2,10},{3,11},{4,12},{5,13},{6,14},{7,15},{8,16},{9,17... | collective-permute-start | bytes 1769480 | tf_op jit(solution)/shard_map/ppermute | solution.py:399
  45.2 1.3 %collective-permute-start.1 = (bf16[2,576,256]{2,1,0:T(8,128)(2,1)S(1)}, bf16[2,576,256]{2,1,0:T(8,128)(2,1)S(1)}, u32[]{:S(2)}, u32[]{:S(2)}) collective-permute-start(bf16[2,576,256]{2,1,0:T(8,128)(2,1)S(1)} %get-tuple-element.52), channel_id=1, source_target_pairs={{8,0},{9,1},{10,2},{11,3},{12,4},{13,5},{14,6},{15,7},{16,8},{17,9... | collective-permute-start | bytes 1769480 | tf_op jit(solution)/shard_map/ppermute | solution.py:399
  46.5 14.6 %shard_map.94 = (bf16[8,432,256]{2,1,0:T(8,128)(2,1)S(1)}, bf16[144,2048]{1,0:T(8,128)(2,1)S(1)}) custom-call(s32[4]{0:T(128)S(1)} %pad_add_fusion.place_ref.at_ref, s32[1,32]{1,0:T(1,128)S(1)} %copy-done.5, s32[1,32]{1,0:T(1,128)S(1)} %copy-done.5, bf16[8,576,256]{2,1,0:T(8,128)(2,1)S(1)} %all-to-all-done.mid_ref), custom_call_target="tpu_custom_call" | custom-call | flops 20000000000 | bytes 1000 | tf_op jit(solution)/shard_map/pallas_call | solution.py:206
  61.1 4.2 %collective-permute-start.5 = (bf16[576,256]{1,0:T(8,128)(2,1)S(1)}, bf16[576,256]{1,0:T(8,128)(2,1)S(1)}, u32[]{:S(2)}, u32[]{:S(2)}) collective-permute-start(bf16[576,256]{1,0:T(8,128)(2,1)S(1)} %get-tuple-element.55.refs_0_), channel_id=1, source_target_pairs={{0,3},{1,2},{2,1},{3,0},{4,7},{5,6},{6,5},{7,4},{8,11},{9,10},{10,... | collective-permute-start | bytes 884744 | tf_op jit(solution)/shard_map/ppermute | solution.py:405
  65.4 3.4 %collective-permute-start.7 = (bf16[576,256]{1,0:T(8,128)(2,1)}, bf16[576,256]{1,0:T(8,128)(2,1)S(1)}, u32[]{:S(2)}, u32[]{:S(2)}) collective-permute-start(bf16[576,256]{1,0:T(8,128)(2,1)} %collective-permute-done.6.refs_4_), channel_id=1, source_target_pairs={{0,1},{1,0},{2,3},{3,2},{4,5},{5,4},{6,7},{7,6},{8,9},{9,8},{10,11... | collective-permute-start | bytes 884744 | tf_op jit(solution)/shard_map/ppermute | solution.py:405
  68.8 3.1 %shard_map.95.mine_ref = bf16[144,2048]{1,0:T(8,128)(2,1)S(1)} custom-call(s32[4]{0:T(128)S(1)} %pad_add_fusion.place_ref.at_ref, s32[1,32]{1,0:T(1,128)S(1)} %copy-done.5, s32[1,32]{1,0:T(1,128)S(1)} %copy-done.5, bf16[8,576,256]{2,1,0:T(8,128)(2,1)S(1)} %all-to-all-done.mid_ref, ...), custom_call_target="tpu_custom_call", output_to_operand_aliasing={{}: (6, {})} | custom-call | flops 1000 | bytes 1000 | tf_op jit(solution)/shard_map/pallas_call | solution.py:296
  72.0 1.3 %collective-permute-start.4 = (bf16[144,2048]{1,0:T(8,128)(2,1)S(1)}, bf16[144,2048]{1,0:T(8,128)(2,1)S(1)}, u32[]{:S(2)}, u32[]{:S(2)}) collective-permute-start(bf16[144,2048]{1,0:T(8,128)(2,1)S(1)} %shard_map.95.mine_ref), channel_id=1, source_target_pairs={{0,4},{1,5},{2,6},{3,7},{4,0},{5,1},{6,2},{7,3},{8,12},{9,13},{10,... | collective-permute-start | bytes 1769480 | tf_op jit(solution)/shard_map/ppermute | solution.py:405
  73.2 5.0 %shard_map.96 = bf16[8,432,256]{2,1,0:T(8,128)(2,1)S(1)} custom-call(s32[4]{0:T(128)S(1)} %pad_add_fusion.place_ref.at_ref, s32[1,32]{1,0:T(1,128)S(1)} %copy-done.5, s32[1,32]{1,0:T(1,128)S(1)} %copy-done.5, bf16[8,576,256]{2,1,0:T(8,128)(2,1)S(1)} %all-to-all-done.mid_ref, ...), custom_call_target="tpu_custom_call", output_to_operand_aliasing={{}: (6, {})} | custom-call | flops 20000000000 | bytes 1000 | tf_op jit(solution)/shard_map/pallas_call | solution.py:296
  79.5 2.6 %collective-permute-done.9.refs_7_ = bf16[576,256]{1,0:T(8,128)(2,1)S(1)} collective-permute-done((bf16[576,256]{1,0:T(8,128)(2,1)}, bf16[576,256]{1,0:T(8,128)(2,1)S(1)}, u32[]{:S(2)}, u32[]{:S(2)}) %collective-permute-start.9) | collective-permute-done | bytes 294944 | tf_op jit(solution)/shard_map/ppermute | solution.py:405
  83.6 4.9 %all-to-all-start.1 = ((bf16[8,432,256]{2,1,0:T(8,128)(2,1)}), bf16[8,432,256]{2,1,0:T(8,128)(2,1)S(1)}, u32[]{:S(2)}, u32[]{:S(2)}) async-start(bf16[8,432,256]{2,1,0:T(8,128)(2,1)} %copy-done.1), calls=%async_computation.1 | async-start | bytes 3538944 | tf_op jit(solution)/shard_map/all_to_all | solution.py:408
  88.5 4.4 %shard_map.98 = (f32[144,288]{1,0:T(8,128)}, bf16[144,288]{1,0:T(8,128)(2,1)}, bf16[144,288]{1,0:T(8,128)(2,1)}, bf16[144,288]{1,0:T(8,128)(2,1)}) custom-call(s32[4]{0:T(128)} %copy-done.3, bf16[144,2048]{1,0:T(8,128)(2,1)} %copy-done, bf16[144,2048]{1,0:T(8,128)(2,1)} %copy-done.7, bf16[16,128]{1,0:T(8,128)(2,1)} %fusion._, bf16[576,256]{1,0:T(8,128)(2,1)} %copy-done.6, ...), custom_call_target="tpu_custom_call" | custom-call | flops 1000 | bytes 1000 | tf_op jit(solution)/shard_map/pallas_call | solution.py:348
  93.5 3.7 %collective-permute-start.11 = (bf16[144,288]{1,0:T(8,128)(2,1)}, bf16[144,288]{1,0:T(8,128)(2,1)S(1)}, u32[]{:S(2)}, u32[]{:S(2)}) collective-permute-start(bf16[144,288]{1,0:T(8,128)(2,1)} %get-tuple-element.40), channel_id=1, source_target_pairs={{0,16},{1,17},{2,18},{3,19},{4,20},{5,21},{6,22},{7,23},{8,24},{9,... | collective-permute-start | bytes 248840 | tf_op jit(solution)/shard_map/ppermute | solution.py:431
  97.4 1.3 %collective-permute-done.10.refs_1_ = bf16[144,288]{1,0:T(8,128)(2,1)S(1)} collective-permute-done((bf16[144,288]{1,0:T(8,128)(2,1)}, bf16[144,288]{1,0:T(8,128)(2,1)S(1)}, u32[]{:S(2)}, u32[]{:S(2)}) %collective-permute-start.10) | collective-permute-done | bytes 82976 | tf_op jit(solution)/shard_map/ppermute | solution.py:431
  98.7 2.4 %collective-permute-done.11.refs_2_ = bf16[144,288]{1,0:T(8,128)(2,1)S(1)} collective-permute-done((bf16[144,288]{1,0:T(8,128)(2,1)}, bf16[144,288]{1,0:T(8,128)(2,1)S(1)}, u32[]{:S(2)}, u32[]{:S(2)}) %collective-permute-start.11) | collective-permute-done | bytes 82976 | tf_op jit(solution)/shard_map/ppermute | solution.py:431
  102.3 5.5 %collective-permute-start.13 = (f32[144,288]{1,0:T(8,128)S(1)}, f32[144,288]{1,0:T(8,128)S(1)}, u32[]{:S(2)}, u32[]{:S(2)}) collective-permute-start(f32[144,288]{1,0:T(8,128)S(1)} %shard_map.99.one_ref), channel_id=1, source_target_pairs={{0,32},{32,0},{64,96},{96,64},{1,33},{33,1},{65,97},{97,65},{2,34}... | collective-permute-start | bytes 497672 | tf_op jit(solution)/shard_map/ppermute | solution.py:405
  109.6 1.8 %collective-permute-start.14 = (f32[36,288]{1,0:T(8,128)S(1)}, f32[36,288]{1,0:T(8,128)S(1)}, u32[]{:S(2)}, u32[]{:S(2)}) collective-permute-start(f32[36,288]{1,0:T(8,128)S(1)} %get-tuple-element.42), channel_id=1, source_target_pairs={{0,1},{1,2},{2,3},{3,0},{4,5},{5,6},{6,7},{7,4},{8,9},{9,10},{10,1... | collective-permute-start | bytes 124424 | tf_op jit(solution)/shard_map/ppermute | solution.py:431
  111.4 2.4 %collective-permute-start.15 = (f32[36,288]{1,0:T(8,128)S(1)}, f32[36,288]{1,0:T(8,128)S(1)}, u32[]{:S(2)}, u32[]{:S(2)}) collective-permute-start(f32[36,288]{1,0:T(8,128)S(1)} %get-tuple-element.43), channel_id=1, source_target_pairs={{0,2},{1,3},{2,0},{3,1},{4,6},{5,7},{6,4},{7,5},{8,10},{9,11},{10,... | collective-permute-start | bytes 124424 | tf_op jit(solution)/shard_map/ppermute | solution.py:431
  115.0 1.4 %shard_map.97 = (bf16[256,1152]{1,0:T(8,128)(2,1)}, bf16[256,1152]{1,0:T(8,128)(2,1)}, bf16[256,1152]{1,0:T(8,128)(2,1)}) custom-call(bf16[8,432,256]{2,1,0:T(8,128)(2,1)S(1)} %all-to-all-done.1.back_ref), custom_call_target="tpu_custom_call" | custom-call | flops 1000 | bytes 1000 | tf_op jit(solution)/shard_map/pallas_call | solution.py:323
  117.9 3.7 %collective-permute-start.17 = (bf16[36,1152]{1,0:T(8,128)(2,1)S(1)}, bf16[36,1152]{1,0:T(8,128)(2,1)S(1)}, u32[]{:S(2)}, u32[]{:S(2)}) collective-permute-start(bf16[36,1152]{1,0:T(8,128)(2,1)S(1)} %shard_map.101), channel_id=1, source_target_pairs={{0,64},{32,96},{64,0},{96,32},{1,65},{33,97},{65,1},{97,33},{2,66}... | collective-permute-start | bytes 248840 | tf_op jit(solution)/shard_map/ppermute | solution.py:405
  121.7 1.9 %collective-permute-done.17 = bf16[36,1152]{1,0:T(8,128)(2,1)S(1)} collective-permute-done((bf16[36,1152]{1,0:T(8,128)(2,1)S(1)}, bf16[36,1152]{1,0:T(8,128)(2,1)S(1)}, u32[]{:S(2)}, u32[]{:S(2)}) %collective-permute-start.17) | collective-permute-done | bytes 82976 | tf_op jit(solution)/shard_map/ppermute | solution.py:405
  (64 shorter events, 11.8 us)
Async XLA Ops:
  5.6 35.9 %all-to-all-start = ((bf16[8,576,256]{2,1,0:T(8,128)(2,1)}), bf16[8,576,256]{2,1,0:T(8,128)(2,1)S(1)}, u32[]{:S(2)}, u32[]{:S(2)}) async-start(bf16[8,576,256]{2,1,0:T(8,128)(2,1)} %get-tuple-element.28), calls=%async_computation | async-start | bytes 4718592 | tf_op jit(solution)/shard_map/all_to_all | solution.py:408
  11.6 34.9 %copy-start.5 = (s32[1,32]{1,0:T(1,128)S(1)}, s32[1,32]{1,0:T(1,128)}, u32[]{:S(2)}) copy-start(s32[1,32]{1,0:T(1,128)} %length_ref.5) | copy-start | bytes 388
  11.7 49.3 %copy-start.6 = (bf16[576,256]{1,0:T(8,128)(2,1)}, bf16[576,256]{1,0:T(8,128)(2,1)S(1)}, u32[]{:S(2)}) copy-start(bf16[576,256]{1,0:T(8,128)(2,1)S(1)} %get-tuple-element.55.refs_0_) | copy-start | bytes 884740
  11.7 49.3 %collective-permute-start.3 = (bf16[576,256]{1,0:T(8,128)(2,1)S(1)}, bf16[576,256]{1,0:T(8,128)(2,1)S(1)}, u32[]{:S(2)}, u32[]{:S(2)}) collective-permute-start(bf16[576,256]{1,0:T(8,128)(2,1)S(1)} %get-tuple-element.55.refs_0_), channel_id=1, source_target_pairs={{0,2},{1,3},{2,0},{3,1},{4,6},{5,7},{6,4},{7,5},{8,10},{9,11},{10,... | collective-permute-start | bytes 884744 | tf_op jit(solution)/shard_map/ppermute | solution.py:405
  14.7 50.6 %collective-permute-start.2 = (bf16[576,256]{1,0:T(8,128)(2,1)S(1)}, bf16[576,256]{1,0:T(8,128)(2,1)S(1)}, u32[]{:S(2)}, u32[]{:S(2)}) collective-permute-start(bf16[576,256]{1,0:T(8,128)(2,1)S(1)} %get-tuple-element.55.refs_0_), channel_id=1, source_target_pairs={{0,1},{1,0},{2,3},{3,2},{4,5},{5,4},{6,7},{7,6},{8,9},{9,8},{10,11... | collective-permute-start | bytes 884744 | tf_op jit(solution)/shard_map/ppermute | solution.py:405
  15.0 50.3 %collective-permute-start.6 = (bf16[576,256]{1,0:T(8,128)(2,1)S(1)}, bf16[576,256]{1,0:T(8,128)(2,1)}, u32[]{:S(2)}, u32[]{:S(2)}) collective-permute-start(bf16[576,256]{1,0:T(8,128)(2,1)S(1)} %get-tuple-element.54), channel_id=1, source_target_pairs={{0,4},{1,5},{2,6},{3,7},{4,0},{5,1},{6,2},{7,3},{8,12},{9,13},{10,... | collective-permute-start | bytes 884744 | tf_op jit(solution)/shard_map/ppermute | solution.py:405
  16.3 56.9 %copy-start.3 = (s32[4]{0:T(128)}, s32[4]{0:T(128)S(1)}, u32[]{:S(2)}) copy-start(s32[4]{0:T(128)S(1)} %pad_add_fusion.place_ref.at_ref) | copy-start | bytes 52
  41.6 23.8 %collective-permute-start = (bf16[2,576,256]{2,1,0:T(8,128)(2,1)S(1)}, bf16[2,576,256]{2,1,0:T(8,128)(2,1)S(1)}, u32[]{:S(2)}, u32[]{:S(2)}) collective-permute-start(bf16[2,576,256]{2,1,0:T(8,128)(2,1)S(1)} %get-tuple-element.53), channel_id=1, source_target_pairs={{0,8},{1,9},{2,10},{3,11},{4,12},{5,13},{6,14},{7,15},{8,16},{9,17... | collective-permute-start | bytes 1769480 | tf_op jit(solution)/shard_map/ppermute | solution.py:399
  45.2 23.6 %collective-permute-start.1 = (bf16[2,576,256]{2,1,0:T(8,128)(2,1)S(1)}, bf16[2,576,256]{2,1,0:T(8,128)(2,1)S(1)}, u32[]{:S(2)}, u32[]{:S(2)}) collective-permute-start(bf16[2,576,256]{2,1,0:T(8,128)(2,1)S(1)} %get-tuple-element.52), channel_id=1, source_target_pairs={{8,0},{9,1},{10,2},{11,3},{12,4},{13,5},{14,6},{15,7},{16,8},{17,9... | collective-permute-start | bytes 1769480 | tf_op jit(solution)/shard_map/ppermute | solution.py:399
  61.1 18.4 %collective-permute-start.5 = (bf16[576,256]{1,0:T(8,128)(2,1)S(1)}, bf16[576,256]{1,0:T(8,128)(2,1)S(1)}, u32[]{:S(2)}, u32[]{:S(2)}) collective-permute-start(bf16[576,256]{1,0:T(8,128)(2,1)S(1)} %get-tuple-element.55.refs_0_), channel_id=1, source_target_pairs={{0,3},{1,2},{2,1},{3,0},{4,7},{5,6},{6,5},{7,4},{8,11},{9,10},{10,... | collective-permute-start | bytes 884744 | tf_op jit(solution)/shard_map/ppermute | solution.py:405
  65.3 16.8 %collective-permute-start.9 = (bf16[576,256]{1,0:T(8,128)(2,1)}, bf16[576,256]{1,0:T(8,128)(2,1)S(1)}, u32[]{:S(2)}, u32[]{:S(2)}) collective-permute-start(bf16[576,256]{1,0:T(8,128)(2,1)} %collective-permute-done.6.refs_4_), channel_id=1, source_target_pairs={{0,3},{1,2},{2,1},{3,0},{4,7},{5,6},{6,5},{7,4},{8,11},{9,10},{10,... | collective-permute-start | bytes 884744 | tf_op jit(solution)/shard_map/ppermute | solution.py:405
  65.4 16.7 %collective-permute-start.8 = (bf16[576,256]{1,0:T(8,128)(2,1)}, bf16[576,256]{1,0:T(8,128)(2,1)S(1)}, u32[]{:S(2)}, u32[]{:S(2)}) collective-permute-start(bf16[576,256]{1,0:T(8,128)(2,1)} %collective-permute-done.6.refs_4_), channel_id=1, source_target_pairs={{0,2},{1,3},{2,0},{3,1},{4,6},{5,7},{6,4},{7,5},{8,10},{9,11},{10,... | collective-permute-start | bytes 884744 | tf_op jit(solution)/shard_map/ppermute | solution.py:405
  65.4 16.6 %collective-permute-start.7 = (bf16[576,256]{1,0:T(8,128)(2,1)}, bf16[576,256]{1,0:T(8,128)(2,1)S(1)}, u32[]{:S(2)}, u32[]{:S(2)}) collective-permute-start(bf16[576,256]{1,0:T(8,128)(2,1)} %collective-permute-done.6.refs_4_), channel_id=1, source_target_pairs={{0,1},{1,0},{2,3},{3,2},{4,5},{5,4},{6,7},{7,6},{8,9},{9,8},{10,11... | collective-permute-start | bytes 884744 | tf_op jit(solution)/shard_map/ppermute | solution.py:405
  72.0 10.1 %collective-permute-start.4 = (bf16[144,2048]{1,0:T(8,128)(2,1)S(1)}, bf16[144,2048]{1,0:T(8,128)(2,1)S(1)}, u32[]{:S(2)}, u32[]{:S(2)}) collective-permute-start(bf16[144,2048]{1,0:T(8,128)(2,1)S(1)} %shard_map.95.mine_ref), channel_id=1, source_target_pairs={{0,4},{1,5},{2,6},{3,7},{4,0},{5,1},{6,2},{7,3},{8,12},{9,13},{10,... | collective-permute-start | bytes 1769480 | tf_op jit(solution)/shard_map/ppermute | solution.py:405
  83.6 31.4 %all-to-all-start.1 = ((bf16[8,432,256]{2,1,0:T(8,128)(2,1)}), bf16[8,432,256]{2,1,0:T(8,128)(2,1)S(1)}, u32[]{:S(2)}, u32[]{:S(2)}) async-start(bf16[8,432,256]{2,1,0:T(8,128)(2,1)} %copy-done.1), calls=%async_computation.1 | async-start | bytes 3538944 | tf_op jit(solution)/shard_map/all_to_all | solution.py:408
  88.5 20.4 %copy-start.4 = (s32[4]{0:T(128)S(1)}, s32[4]{0:T(128)}, u32[]{:S(2)}) copy-start(s32[4]{0:T(128)} %copy-done.3) | copy-start | bytes 52
  92.9 5.8 %collective-permute-start.10 = (bf16[144,288]{1,0:T(8,128)(2,1)}, bf16[144,288]{1,0:T(8,128)(2,1)S(1)}, u32[]{:S(2)}, u32[]{:S(2)}) collective-permute-start(bf16[144,288]{1,0:T(8,128)(2,1)} %get-tuple-element.39), channel_id=1, source_target_pairs={{0,8},{1,9},{2,10},{3,11},{4,12},{5,13},{6,14},{7,15},{8,16},{9,17... | collective-permute-start | bytes 248840 | tf_op jit(solution)/shard_map/ppermute | solution.py:431
  93.5 7.5 %collective-permute-start.11 = (bf16[144,288]{1,0:T(8,128)(2,1)}, bf16[144,288]{1,0:T(8,128)(2,1)S(1)}, u32[]{:S(2)}, u32[]{:S(2)}) collective-permute-start(bf16[144,288]{1,0:T(8,128)(2,1)} %get-tuple-element.40), channel_id=1, source_target_pairs={{0,16},{1,17},{2,18},{3,19},{4,20},{5,21},{6,22},{7,23},{8,24},{9,... | collective-permute-start | bytes 248840 | tf_op jit(solution)/shard_map/ppermute | solution.py:431
  97.2 4.1 %collective-permute-start.12 = (bf16[144,288]{1,0:T(8,128)(2,1)}, bf16[144,288]{1,0:T(8,128)(2,1)S(1)}, u32[]{:S(2)}, u32[]{:S(2)}) collective-permute-start(bf16[144,288]{1,0:T(8,128)(2,1)} %get-tuple-element.41), channel_id=1, source_target_pairs={{0,24},{1,25},{2,26},{3,27},{4,28},{5,29},{6,30},{7,31},{8,0},{9,1... | collective-permute-start | bytes 248840 | tf_op jit(solution)/shard_map/ppermute | solution.py:431
  102.3 6.6 %collective-permute-start.13 = (f32[144,288]{1,0:T(8,128)S(1)}, f32[144,288]{1,0:T(8,128)S(1)}, u32[]{:S(2)}, u32[]{:S(2)}) collective-permute-start(f32[144,288]{1,0:T(8,128)S(1)} %shard_map.99.one_ref), channel_id=1, source_target_pairs={{0,32},{32,0},{64,96},{96,64},{1,33},{33,1},{65,97},{97,65},{2,34}... | collective-permute-start | bytes 497672 | tf_op jit(solution)/shard_map/ppermute | solution.py:405
  109.6 6.8 %collective-permute-start.14 = (f32[36,288]{1,0:T(8,128)S(1)}, f32[36,288]{1,0:T(8,128)S(1)}, u32[]{:S(2)}, u32[]{:S(2)}) collective-permute-start(f32[36,288]{1,0:T(8,128)S(1)} %get-tuple-element.42), channel_id=1, source_target_pairs={{0,1},{1,2},{2,3},{3,0},{4,5},{5,6},{6,7},{7,4},{8,9},{9,10},{10,1... | collective-permute-start | bytes 124424 | tf_op jit(solution)/shard_map/ppermute | solution.py:431
  111.4 5.2 %collective-permute-start.15 = (f32[36,288]{1,0:T(8,128)S(1)}, f32[36,288]{1,0:T(8,128)S(1)}, u32[]{:S(2)}, u32[]{:S(2)}) collective-permute-start(f32[36,288]{1,0:T(8,128)S(1)} %get-tuple-element.43), channel_id=1, source_target_pairs={{0,2},{1,3},{2,0},{3,1},{4,6},{5,7},{6,4},{7,5},{8,10},{9,11},{10,... | collective-permute-start | bytes 124424 | tf_op jit(solution)/shard_map/ppermute | solution.py:431
  113.8 3.4 %collective-permute-start.16 = (f32[36,288]{1,0:T(8,128)S(1)}, f32[36,288]{1,0:T(8,128)S(1)}, u32[]{:S(2)}, u32[]{:S(2)}) collective-permute-start(f32[36,288]{1,0:T(8,128)S(1)} %get-tuple-element.44), channel_id=1, source_target_pairs={{0,3},{1,0},{2,1},{3,2},{4,7},{5,4},{6,5},{7,6},{8,11},{9,8},{10,9... | collective-permute-start | bytes 124424 | tf_op jit(solution)/shard_map/ppermute | solution.py:431
  117.9 5.7 %collective-permute-start.17 = (bf16[36,1152]{1,0:T(8,128)(2,1)S(1)}, bf16[36,1152]{1,0:T(8,128)(2,1)S(1)}, u32[]{:S(2)}, u32[]{:S(2)}) collective-permute-start(bf16[36,1152]{1,0:T(8,128)(2,1)S(1)} %shard_map.101), channel_id=1, source_target_pairs={{0,64},{32,96},{64,0},{96,32},{1,65},{33,97},{65,1},{97,33},{2,66}... | collective-permute-start | bytes 248840 | tf_op jit(solution)/shard_map/ppermute | solution.py:405
  (12 other events, 48.6 us)

commit v8 on v7

--- a/solution.py
+++ b/solution.py
@@ -353,16 +353,17 @@
 
 
 def sum_kernel(*refs):
-    refs[4][...] = refs[0][...] + sum(ref[...].astype(F32) for ref in refs[1:4])
+    total = refs[0][...] + sum(ref[...].astype(F32) for ref in refs[1:4])
+    refs[4][...] = total.astype(BF16)
 
 
 def sum_z(terms):
-    shape = jax.ShapeDtypeStruct((PAIR, 2 * PAIR), F32)
+    shape = jax.ShapeDtypeStruct((PAIR, 2 * PAIR), BF16)
     return call(sum_kernel, shape, [WHOLE] * 4, [], 1000)(*terms)
 
 
 def pick_x_kernel(at_ref, one_ref, two_ref, *outs):
-    total = one_ref[...] + two_ref[...]
+    total = one_ref[...].astype(F32) + two_ref[...].astype(F32)
     blocks = [total[j * 36 : (j + 1) * 36] for j in range(4)]
     for k, out_ref in enumerate(outs):
         out_ref[...] = select(blocks, lax.rem(at_ref[2] + k, 4))

time: 127 us -> 127 us (level)
  no operation moved by 1% of the time
where the time goes in v8:
time: 127 us; the launch traced here: 125 us
  starting transfers between devices  48.8 us (38%)
  waiting for transfers between devices  35.6 us (28%)
  Pallas kernels  34.8 us (27%)
  local copies, waits for them, and re-layouts  3.2 us (3%)
  other arithmetic  1.44 us (1%)
    all_to_all x2, waiting for transfers between devices, exchange(): return lax.all_to_all(blocks, 'seq', 0, 0, axis_index_groups=groups)  25.2 us
    ppermute x10, starting transfers between devices, swap(): lax.ppermute(block, axis, [(i, i ^ by) for i in range(lax.axis_size(axis))])  23.1 us
    pallas_call x1, Pallas kernels, inner(): pl.pallas_call(inner_kernel, out_shape=RESULT, in_specs=[SCALAR, SCALAR,...  14.5 us
    all_to_all x2, starting transfers between devices, exchange(): return lax.all_to_all(blocks, 'seq', 0, 0, axis_index_groups=groups)  10.9 us
    ppermute x6, starting transfers between devices, ahead(): return lax.ppermute(block, 'seq', [(i, to(i)) for i in range(count)])  9.82 us
    pallas_call x2, Pallas kernels, edge(): pl.pallas_call(kernel, grid=(2,), out_shape=jax.ShapeDtypeStruct(inner_pa...  8.07 us
    ppermute x10, waiting for transfers between devices, swap(): lax.ppermute(block, axis, [(i, i ^ by) for i in range(lax.axis_size(axis))])  5.49 us
    pallas_call x1, Pallas kernels, pack(): call(pack_kernel, shapes, [WHOLE] * 5, [], 1000, ALL_VMEM)  4.99 us
  transfers between devices with their start and end apart: 20, of which 9 were waited for; matrix products, arithmetic and copies ran while one was open for 0% of the time, Pallas kernels for 23%

profile of v8, /device:TPU:1, one launch (start us, length us, event | category | flops | bytes accessed | tf_op | source)
XLA Modules:
  0.0 124.7 jit_solution(3181271477776942585)
XLA Ops:
  0.6 5.0 %shard_map.93 = (bf16[8,576,256]{2,1,0:T(8,128)(2,1)}, bf16[576,256]{1,0:T(8,128)(2,1)}, bf16[576,256]{1,0:T(8,128)(2,1)}) custom-call(bf16[256,1152]{1,0:T(8,128)(2,1)} %bitcast.11, bf16[256,1152]{1,0:T(8,128)(2,1)} %bitcast.12, bf16[256,1152]{1,0:T(8,128)(2,1)} %bitcast.13, bf16[256,1152]{1,0:T(8,128)(2,1)} %bitcast.14, bf16[1152,1152]{1,0:T(8,128)(2,1)} %proj_ref.1), custom_call_target="tpu_custom_call" | custom-call | flops 1000 | bytes 1000 | tf_op jit(solution)/shard_map/pallas_call | solution.py:69
  5.6 6.0 %all-to-all-start = ((bf16[8,576,256]{2,1,0:T(8,128)(2,1)}), bf16[8,576,256]{2,1,0:T(8,128)(2,1)S(1)}, u32[]{:S(2)}, u32[]{:S(2)}) async-start(bf16[8,576,256]{2,1,0:T(8,128)(2,1)} %get-tuple-element.28), calls=%async_computation | async-start | bytes 4718592 | tf_op jit(solution)/shard_map/all_to_all | solution.py:409
  11.7 3.0 %collective-permute-start.3 = (bf16[576,256]{1,0:T(8,128)(2,1)S(1)}, bf16[576,256]{1,0:T(8,128)(2,1)S(1)}, u32[]{:S(2)}, u32[]{:S(2)}) collective-permute-start(bf16[576,256]{1,0:T(8,128)(2,1)S(1)} %get-tuple-element.55.refs_0_), channel_id=1, source_target_pairs={{0,2},{1,3},{2,0},{3,1},{4,6},{5,7},{6,4},{7,5},{8,10},{9,11},{10,... | collective-permute-start | bytes 884744 | tf_op jit(solution)/shard_map/ppermute | solution.py:406
  16.3 25.2 %all-to-all-done.mid_ref = bf16[8,576,256]{2,1,0:T(8,128)(2,1)S(1)} async-done(((bf16[8,576,256]{2,1,0:T(8,128)(2,1)}), bf16[8,576,256]{2,1,0:T(8,128)(2,1)S(1)}, u32[]{:S(2)}, u32[]{:S(2)}) %all-to-all-start) | async-done | bytes 2359328 | tf_op jit(solution)/shard_map/all_to_all | solution.py:409
  41.6 3.6 %collective-permute-start = (bf16[2,576,256]{2,1,0:T(8,128)(2,1)S(1)}, bf16[2,576,256]{2,1,0:T(8,128)(2,1)S(1)}, u32[]{:S(2)}, u32[]{:S(2)}) collective-permute-start(bf16[2,576,256]{2,1,0:T(8,128)(2,1)S(1)} %get-tuple-element.53), channel_id=1, source_target_pairs={{0,8},{1,9},{2,10},{3,11},{4,12},{5,13},{6,14},{7,15},{8,16},{9,17... | collective-permute-start | bytes 1769480 | tf_op jit(solution)/shard_map/ppermute | solution.py:400
  45.2 1.3 %collective-permute-start.1 = (bf16[2,576,256]{2,1,0:T(8,128)(2,1)S(1)}, bf16[2,576,256]{2,1,0:T(8,128)(2,1)S(1)}, u32[]{:S(2)}, u32[]{:S(2)}) collective-permute-start(bf16[2,576,256]{2,1,0:T(8,128)(2,1)S(1)} %get-tuple-element.52), channel_id=1, source_target_pairs={{8,0},{9,1},{10,2},{11,3},{12,4},{13,5},{14,6},{15,7},{16,8},{17,9... | collective-permute-start | bytes 1769480 | tf_op jit(solution)/shard_map/ppermute | solution.py:400
  46.5 14.5 %shard_map.94 = (bf16[8,432,256]{2,1,0:T(8,128)(2,1)S(1)}, bf16[144,2048]{1,0:T(8,128)(2,1)S(1)}) custom-call(s32[4]{0:T(128)S(1)} %pad_add_fusion.place_ref.at_ref, s32[1,32]{1,0:T(1,128)S(1)} %copy-done.5, s32[1,32]{1,0:T(1,128)S(1)} %copy-done.5, bf16[8,576,256]{2,1,0:T(8,128)(2,1)S(1)} %all-to-all-done.mid_ref), custom_call_target="tpu_custom_call" | custom-call | flops 20000000000 | bytes 1000 | tf_op jit(solution)/shard_map/pallas_call | solution.py:206
  61.1 4.2 %collective-permute-start.5 = (bf16[576,256]{1,0:T(8,128)(2,1)S(1)}, bf16[576,256]{1,0:T(8,128)(2,1)S(1)}, u32[]{:S(2)}, u32[]{:S(2)}) collective-permute-start(bf16[576,256]{1,0:T(8,128)(2,1)S(1)} %get-tuple-element.55.refs_0_), channel_id=1, source_target_pairs={{0,3},{1,2},{2,1},{3,0},{4,7},{5,6},{6,5},{7,4},{8,11},{9,10},{10,... | collective-permute-start | bytes 884744 | tf_op jit(solution)/shard_map/ppermute | solution.py:406
  65.4 3.4 %collective-permute-start.7 = (bf16[576,256]{1,0:T(8,128)(2,1)}, bf16[576,256]{1,0:T(8,128)(2,1)S(1)}, u32[]{:S(2)}, u32[]{:S(2)}) collective-permute-start(bf16[576,256]{1,0:T(8,128)(2,1)} %collective-permute-done.6.refs_4_), channel_id=1, source_target_pairs={{0,1},{1,0},{2,3},{3,2},{4,5},{5,4},{6,7},{7,6},{8,9},{9,8},{10,11... | collective-permute-start | bytes 884744 | tf_op jit(solution)/shard_map/ppermute | solution.py:406
  68.8 3.1 %shard_map.95.mine_ref = bf16[144,2048]{1,0:T(8,128)(2,1)S(1)} custom-call(s32[4]{0:T(128)S(1)} %pad_add_fusion.place_ref.at_ref, s32[1,32]{1,0:T(1,128)S(1)} %copy-done.5, s32[1,32]{1,0:T(1,128)S(1)} %copy-done.5, bf16[8,576,256]{2,1,0:T(8,128)(2,1)S(1)} %all-to-all-done.mid_ref, ...), custom_call_target="tpu_custom_call", output_to_operand_aliasing={{}: (6, {})} | custom-call | flops 1000 | bytes 1000 | tf_op jit(solution)/shard_map/pallas_call | solution.py:296
  73.2 5.0 %shard_map.96 = bf16[8,432,256]{2,1,0:T(8,128)(2,1)S(1)} custom-call(s32[4]{0:T(128)S(1)} %pad_add_fusion.place_ref.at_ref, s32[1,32]{1,0:T(1,128)S(1)} %copy-done.5, s32[1,32]{1,0:T(1,128)S(1)} %copy-done.5, bf16[8,576,256]{2,1,0:T(8,128)(2,1)S(1)} %all-to-all-done.mid_ref, ...), custom_call_target="tpu_custom_call", output_to_operand_aliasing={{}: (6, {})} | custom-call | flops 20000000000 | bytes 1000 | tf_op jit(solution)/shard_map/pallas_call | solution.py:296
  79.4 2.6 %collective-permute-done.9.refs_7_ = bf16[576,256]{1,0:T(8,128)(2,1)S(1)} collective-permute-done((bf16[576,256]{1,0:T(8,128)(2,1)}, bf16[576,256]{1,0:T(8,128)(2,1)S(1)}, u32[]{:S(2)}, u32[]{:S(2)}) %collective-permute-start.9) | collective-permute-done | bytes 294944 | tf_op jit(solution)/shard_map/ppermute | solution.py:406
  83.6 4.9 %all-to-all-start.1 = ((bf16[8,432,256]{2,1,0:T(8,128)(2,1)}), bf16[8,432,256]{2,1,0:T(8,128)(2,1)S(1)}, u32[]{:S(2)}, u32[]{:S(2)}) async-start(bf16[8,432,256]{2,1,0:T(8,128)(2,1)} %copy-done.1), calls=%async_computation.1 | async-start | bytes 3538944 | tf_op jit(solution)/shard_map/all_to_all | solution.py:409
  88.5 4.4 %shard_map.98 = (f32[144,288]{1,0:T(8,128)}, bf16[144,288]{1,0:T(8,128)(2,1)}, bf16[144,288]{1,0:T(8,128)(2,1)}, bf16[144,288]{1,0:T(8,128)(2,1)}) custom-call(s32[4]{0:T(128)} %copy-done.3, bf16[144,2048]{1,0:T(8,128)(2,1)} %copy-done, bf16[144,2048]{1,0:T(8,128)(2,1)} %copy-done.7, bf16[16,128]{1,0:T(8,128)(2,1)} %fusion._, bf16[576,256]{1,0:T(8,128)(2,1)} %copy-done.6, ...), custom_call_target="tpu_custom_call" | custom-call | flops 1000 | bytes 1000 | tf_op jit(solution)/shard_map/pallas_call | solution.py:348
  92.9 1.4 %collective-permute-start.10 = (bf16[144,288]{1,0:T(8,128)(2,1)}, bf16[144,288]{1,0:T(8,128)(2,1)S(1)}, u32[]{:S(2)}, u32[]{:S(2)}) collective-permute-start(bf16[144,288]{1,0:T(8,128)(2,1)} %get-tuple-element.39), channel_id=1, source_target_pairs={{0,8},{1,9},{2,10},{3,11},{4,12},{5,13},{6,14},{7,15},{8,16},{9,17... | collective-permute-start | bytes 248840 | tf_op jit(solution)/shard_map/ppermute | solution.py:432
  94.3 3.0 %collective-permute-start.11 = (bf16[144,288]{1,0:T(8,128)(2,1)}, bf16[144,288]{1,0:T(8,128)(2,1)S(1)}, u32[]{:S(2)}, u32[]{:S(2)}) collective-permute-start(bf16[144,288]{1,0:T(8,128)(2,1)} %get-tuple-element.40), channel_id=1, source_target_pairs={{0,16},{1,17},{2,18},{3,19},{4,20},{5,21},{6,22},{7,23},{8,24},{9,... | collective-permute-start | bytes 248840 | tf_op jit(solution)/shard_map/ppermute | solution.py:432
  97.3 1.5 %collective-permute-done.10.refs_1_ = bf16[144,288]{1,0:T(8,128)(2,1)S(1)} collective-permute-done((bf16[144,288]{1,0:T(8,128)(2,1)}, bf16[144,288]{1,0:T(8,128)(2,1)S(1)}, u32[]{:S(2)}, u32[]{:S(2)}) %collective-permute-start.10) | collective-permute-done | bytes 82976 | tf_op jit(solution)/shard_map/ppermute | solution.py:432
  98.8 2.4 %collective-permute-done.11.refs_2_ = bf16[144,288]{1,0:T(8,128)(2,1)S(1)} collective-permute-done((bf16[144,288]{1,0:T(8,128)(2,1)}, bf16[144,288]{1,0:T(8,128)(2,1)S(1)}, u32[]{:S(2)}, u32[]{:S(2)}) %collective-permute-start.11) | collective-permute-done | bytes 82976 | tf_op jit(solution)/shard_map/ppermute | solution.py:432
  102.4 5.5 %collective-permute-start.13 = (bf16[144,288]{1,0:T(8,128)(2,1)S(1)}, bf16[144,288]{1,0:T(8,128)(2,1)S(1)}, u32[]{:S(2)}, u32[]{:S(2)}) collective-permute-start(bf16[144,288]{1,0:T(8,128)(2,1)S(1)} %shard_map.99.one_ref), channel_id=1, source_target_pairs={{0,32},{32,0},{64,96},{96,64},{1,33},{33,1},{65,97},{97,65},{2,34}... | collective-permute-start | bytes 248840 | tf_op jit(solution)/shard_map/ppermute | solution.py:406
  109.6 1.8 %collective-permute-start.14 = (f32[36,288]{1,0:T(8,128)S(1)}, f32[36,288]{1,0:T(8,128)S(1)}, u32[]{:S(2)}, u32[]{:S(2)}) collective-permute-start(f32[36,288]{1,0:T(8,128)S(1)} %get-tuple-element.42), channel_id=1, source_target_pairs={{0,1},{1,2},{2,3},{3,0},{4,5},{5,6},{6,7},{7,4},{8,9},{9,10},{10,1... | collective-permute-start | bytes 124424 | tf_op jit(solution)/shard_map/ppermute | solution.py:432
  111.4 2.4 %collective-permute-start.15 = (f32[36,288]{1,0:T(8,128)S(1)}, f32[36,288]{1,0:T(8,128)S(1)}, u32[]{:S(2)}, u32[]{:S(2)}) collective-permute-start(f32[36,288]{1,0:T(8,128)S(1)} %get-tuple-element.43), channel_id=1, source_target_pairs={{0,2},{1,3},{2,0},{3,1},{4,6},{5,7},{6,4},{7,5},{8,10},{9,11},{10,... | collective-permute-start | bytes 124424 | tf_op jit(solution)/shard_map/ppermute | solution.py:432
  115.0 1.4 %shard_map.97 = (bf16[256,1152]{1,0:T(8,128)(2,1)}, bf16[256,1152]{1,0:T(8,128)(2,1)}, bf16[256,1152]{1,0:T(8,128)(2,1)}) custom-call(bf16[8,432,256]{2,1,0:T(8,128)(2,1)S(1)} %all-to-all-done.1.back_ref), custom_call_target="tpu_custom_call" | custom-call | flops 1000 | bytes 1000 | tf_op jit(solution)/shard_map/pallas_call | solution.py:323
  117.9 4.2 %collective-permute-start.17 = (bf16[36,1152]{1,0:T(8,128)(2,1)S(1)}, bf16[36,1152]{1,0:T(8,128)(2,1)S(1)}, u32[]{:S(2)}, u32[]{:S(2)}) collective-permute-start(bf16[36,1152]{1,0:T(8,128)(2,1)S(1)} %shard_map.101), channel_id=1, source_target_pairs={{0,64},{32,96},{64,0},{96,32},{1,65},{33,97},{65,1},{97,33},{2,66}... | collective-permute-start | bytes 248840 | tf_op jit(solution)/shard_map/ppermute | solution.py:406
  122.1 1.9 %collective-permute-done.17 = bf16[36,1152]{1,0:T(8,128)(2,1)S(1)} collective-permute-done((bf16[36,1152]{1,0:T(8,128)(2,1)S(1)}, bf16[36,1152]{1,0:T(8,128)(2,1)S(1)}, u32[]{:S(2)}, u32[]{:S(2)}) %collective-permute-start.17) | collective-permute-done | bytes 82976 | tf_op jit(solution)/shard_map/ppermute | solution.py:406
  (64 shorter events, 12.1 us)
Async XLA Ops:
  5.6 35.9 %all-to-all-start = ((bf16[8,576,256]{2,1,0:T(8,128)(2,1)}), bf16[8,576,256]{2,1,0:T(8,128)(2,1)S(1)}, u32[]{:S(2)}, u32[]{:S(2)}) async-start(bf16[8,576,256]{2,1,0:T(8,128)(2,1)} %get-tuple-element.28), calls=%async_computation | async-start | bytes 4718592 | tf_op jit(solution)/shard_map/all_to_all | solution.py:409
  11.6 34.9 %copy-start.5 = (s32[1,32]{1,0:T(1,128)S(1)}, s32[1,32]{1,0:T(1,128)}, u32[]{:S(2)}) copy-start(s32[1,32]{1,0:T(1,128)} %length_ref.5) | copy-start | bytes 388
  11.7 49.3 %copy-start.6 = (bf16[576,256]{1,0:T(8,128)(2,1)}, bf16[576,256]{1,0:T(8,128)(2,1)S(1)}, u32[]{:S(2)}) copy-start(bf16[576,256]{1,0:T(8,128)(2,1)S(1)} %get-tuple-element.55.refs_0_) | copy-start | bytes 884740
  11.7 49.3 %collective-permute-start.3 = (bf16[576,256]{1,0:T(8,128)(2,1)S(1)}, bf16[576,256]{1,0:T(8,128)(2,1)S(1)}, u32[]{:S(2)}, u32[]{:S(2)}) collective-permute-start(bf16[576,256]{1,0:T(8,128)(2,1)S(1)} %get-tuple-element.55.refs_0_), channel_id=1, source_target_pairs={{0,2},{1,3},{2,0},{3,1},{4,6},{5,7},{6,4},{7,5},{8,10},{9,11},{10,... | collective-permute-start | bytes 884744 | tf_op jit(solution)/shard_map/ppermute | solution.py:406
  14.7 50.6 %collective-permute-start.2 = (bf16[576,256]{1,0:T(8,128)(2,1)S(1)}, bf16[576,256]{1,0:T(8,128)(2,1)S(1)}, u32[]{:S(2)}, u32[]{:S(2)}) collective-permute-start(bf16[576,256]{1,0:T(8,128)(2,1)S(1)} %get-tuple-element.55.refs_0_), channel_id=1, source_target_pairs={{0,1},{1,0},{2,3},{3,2},{4,5},{5,4},{6,7},{7,6},{8,9},{9,8},{10,11... | collective-permute-start | bytes 884744 | tf_op jit(solution)/shard_map/ppermute | solution.py:406
  15.0 50.2 %collective-permute-start.6 = (bf16[576,256]{1,0:T(8,128)(2,1)S(1)}, bf16[576,256]{1,0:T(8,128)(2,1)}, u32[]{:S(2)}, u32[]{:S(2)}) collective-permute-start(bf16[576,256]{1,0:T(8,128)(2,1)S(1)} %get-tuple-element.54), channel_id=1, source_target_pairs={{0,4},{1,5},{2,6},{3,7},{4,0},{5,1},{6,2},{7,3},{8,12},{9,13},{10,... | collective-permute-start | bytes 884744 | tf_op jit(solution)/shard_map/ppermute | solution.py:406
  16.3 56.9 %copy-start.3 = (s32[4]{0:T(128)}, s32[4]{0:T(128)S(1)}, u32[]{:S(2)}) copy-start(s32[4]{0:T(128)S(1)} %pad_add_fusion.place_ref.at_ref) | copy-start | bytes 52
  41.6 23.8 %collective-permute-start = (bf16[2,576,256]{2,1,0:T(8,128)(2,1)S(1)}, bf16[2,576,256]{2,1,0:T(8,128)(2,1)S(1)}, u32[]{:S(2)}, u32[]{:S(2)}) collective-permute-start(bf16[2,576,256]{2,1,0:T(8,128)(2,1)S(1)} %get-tuple-element.53), channel_id=1, source_target_pairs={{0,8},{1,9},{2,10},{3,11},{4,12},{5,13},{6,14},{7,15},{8,16},{9,17... | collective-permute-start | bytes 1769480 | tf_op jit(solution)/shard_map/ppermute | solution.py:400
  45.2 23.6 %collective-permute-start.1 = (bf16[2,576,256]{2,1,0:T(8,128)(2,1)S(1)}, bf16[2,576,256]{2,1,0:T(8,128)(2,1)S(1)}, u32[]{:S(2)}, u32[]{:S(2)}) collective-permute-start(bf16[2,576,256]{2,1,0:T(8,128)(2,1)S(1)} %get-tuple-element.52), channel_id=1, source_target_pairs={{8,0},{9,1},{10,2},{11,3},{12,4},{13,5},{14,6},{15,7},{16,8},{17,9... | collective-permute-start | bytes 1769480 | tf_op jit(solution)/shard_map/ppermute | solution.py:400
  61.1 18.4 %collective-permute-start.5 = (bf16[576,256]{1,0:T(8,128)(2,1)S(1)}, bf16[576,256]{1,0:T(8,128)(2,1)S(1)}, u32[]{:S(2)}, u32[]{:S(2)}) collective-permute-start(bf16[576,256]{1,0:T(8,128)(2,1)S(1)} %get-tuple-element.55.refs_0_), channel_id=1, source_target_pairs={{0,3},{1,2},{2,1},{3,0},{4,7},{5,6},{6,5},{7,4},{8,11},{9,10},{10,... | collective-permute-start | bytes 884744 | tf_op jit(solution)/shard_map/ppermute | solution.py:406
  65.2 16.8 %collective-permute-start.9 = (bf16[576,256]{1,0:T(8,128)(2,1)}, bf16[576,256]{1,0:T(8,128)(2,1)S(1)}, u32[]{:S(2)}, u32[]{:S(2)}) collective-permute-start(bf16[576,256]{1,0:T(8,128)(2,1)} %collective-permute-done.6.refs_4_), channel_id=1, source_target_pairs={{0,3},{1,2},{2,1},{3,0},{4,7},{5,6},{6,5},{7,4},{8,11},{9,10},{10,... | collective-permute-start | bytes 884744 | tf_op jit(solution)/shard_map/ppermute | solution.py:406
  65.3 16.7 %collective-permute-start.8 = (bf16[576,256]{1,0:T(8,128)(2,1)}, bf16[576,256]{1,0:T(8,128)(2,1)S(1)}, u32[]{:S(2)}, u32[]{:S(2)}) collective-permute-start(bf16[576,256]{1,0:T(8,128)(2,1)} %collective-permute-done.6.refs_4_), channel_id=1, source_target_pairs={{0,2},{1,3},{2,0},{3,1},{4,6},{5,7},{6,4},{7,5},{8,10},{9,11},{10,... | collective-permute-start | bytes 884744 | tf_op jit(solution)/shard_map/ppermute | solution.py:406
  65.4 16.6 %collective-permute-start.7 = (bf16[576,256]{1,0:T(8,128)(2,1)}, bf16[576,256]{1,0:T(8,128)(2,1)S(1)}, u32[]{:S(2)}, u32[]{:S(2)}) collective-permute-start(bf16[576,256]{1,0:T(8,128)(2,1)} %collective-permute-done.6.refs_4_), channel_id=1, source_target_pairs={{0,1},{1,0},{2,3},{3,2},{4,5},{5,4},{6,7},{7,6},{8,9},{9,8},{10,11... | collective-permute-start | bytes 884744 | tf_op jit(solution)/shard_map/ppermute | solution.py:406
  71.9 10.1 %collective-permute-start.4 = (bf16[144,2048]{1,0:T(8,128)(2,1)S(1)}, bf16[144,2048]{1,0:T(8,128)(2,1)S(1)}, u32[]{:S(2)}, u32[]{:S(2)}) collective-permute-start(bf16[144,2048]{1,0:T(8,128)(2,1)S(1)} %shard_map.95.mine_ref), channel_id=1, source_target_pairs={{0,4},{1,5},{2,6},{3,7},{4,0},{5,1},{6,2},{7,3},{8,12},{9,13},{10,... | collective-permute-start | bytes 1769480 | tf_op jit(solution)/shard_map/ppermute | solution.py:406
  83.6 31.4 %all-to-all-start.1 = ((bf16[8,432,256]{2,1,0:T(8,128)(2,1)}), bf16[8,432,256]{2,1,0:T(8,128)(2,1)S(1)}, u32[]{:S(2)}, u32[]{:S(2)}) async-start(bf16[8,432,256]{2,1,0:T(8,128)(2,1)} %copy-done.1), calls=%async_computation.1 | async-start | bytes 3538944 | tf_op jit(solution)/shard_map/all_to_all | solution.py:409
  88.5 20.4 %copy-start.4 = (s32[4]{0:T(128)S(1)}, s32[4]{0:T(128)}, u32[]{:S(2)}) copy-start(s32[4]{0:T(128)} %copy-done.3) | copy-start | bytes 52
  92.9 5.9 %collective-permute-start.10 = (bf16[144,288]{1,0:T(8,128)(2,1)}, bf16[144,288]{1,0:T(8,128)(2,1)S(1)}, u32[]{:S(2)}, u32[]{:S(2)}) collective-permute-start(bf16[144,288]{1,0:T(8,128)(2,1)} %get-tuple-element.39), channel_id=1, source_target_pairs={{0,8},{1,9},{2,10},{3,11},{4,12},{5,13},{6,14},{7,15},{8,16},{9,17... | collective-permute-start | bytes 248840 | tf_op jit(solution)/shard_map/ppermute | solution.py:432
  94.3 6.9 %collective-permute-start.11 = (bf16[144,288]{1,0:T(8,128)(2,1)}, bf16[144,288]{1,0:T(8,128)(2,1)S(1)}, u32[]{:S(2)}, u32[]{:S(2)}) collective-permute-start(bf16[144,288]{1,0:T(8,128)(2,1)} %get-tuple-element.40), channel_id=1, source_target_pairs={{0,16},{1,17},{2,18},{3,19},{4,20},{5,21},{6,22},{7,23},{8,24},{9,... | collective-permute-start | bytes 248840 | tf_op jit(solution)/shard_map/ppermute | solution.py:432
  97.3 4.1 %collective-permute-start.12 = (bf16[144,288]{1,0:T(8,128)(2,1)}, bf16[144,288]{1,0:T(8,128)(2,1)S(1)}, u32[]{:S(2)}, u32[]{:S(2)}) collective-permute-start(bf16[144,288]{1,0:T(8,128)(2,1)} %get-tuple-element.41), channel_id=1, source_target_pairs={{0,24},{1,25},{2,26},{3,27},{4,28},{5,29},{6,30},{7,31},{8,0},{9,1... | collective-permute-start | bytes 248840 | tf_op jit(solution)/shard_map/ppermute | solution.py:432
  102.4 6.5 %collective-permute-start.13 = (bf16[144,288]{1,0:T(8,128)(2,1)S(1)}, bf16[144,288]{1,0:T(8,128)(2,1)S(1)}, u32[]{:S(2)}, u32[]{:S(2)}) collective-permute-start(bf16[144,288]{1,0:T(8,128)(2,1)S(1)} %shard_map.99.one_ref), channel_id=1, source_target_pairs={{0,32},{32,0},{64,96},{96,64},{1,33},{33,1},{65,97},{97,65},{2,34}... | collective-permute-start | bytes 248840 | tf_op jit(solution)/shard_map/ppermute | solution.py:406
  109.6 6.8 %collective-permute-start.14 = (f32[36,288]{1,0:T(8,128)S(1)}, f32[36,288]{1,0:T(8,128)S(1)}, u32[]{:S(2)}, u32[]{:S(2)}) collective-permute-start(f32[36,288]{1,0:T(8,128)S(1)} %get-tuple-element.42), channel_id=1, source_target_pairs={{0,1},{1,2},{2,3},{3,0},{4,5},{5,6},{6,7},{7,4},{8,9},{9,10},{10,1... | collective-permute-start | bytes 124424 | tf_op jit(solution)/shard_map/ppermute | solution.py:432
  111.4 5.2 %collective-permute-start.15 = (f32[36,288]{1,0:T(8,128)S(1)}, f32[36,288]{1,0:T(8,128)S(1)}, u32[]{:S(2)}, u32[]{:S(2)}) collective-permute-start(f32[36,288]{1,0:T(8,128)S(1)} %get-tuple-element.43), channel_id=1, source_target_pairs={{0,2},{1,3},{2,0},{3,1},{4,6},{5,7},{6,4},{7,5},{8,10},{9,11},{10,... | collective-permute-start | bytes 124424 | tf_op jit(solution)/shard_map/ppermute | solution.py:432
  113.8 3.4 %collective-permute-start.16 = (f32[36,288]{1,0:T(8,128)S(1)}, f32[36,288]{1,0:T(8,128)S(1)}, u32[]{:S(2)}, u32[]{:S(2)}) collective-permute-start(f32[36,288]{1,0:T(8,128)S(1)} %get-tuple-element.44), channel_id=1, source_target_pairs={{0,3},{1,0},{2,1},{3,2},{4,7},{5,4},{6,5},{7,6},{8,11},{9,8},{10,9... | collective-permute-start | bytes 124424 | tf_op jit(solution)/shard_map/ppermute | solution.py:432
  117.9 6.2 %collective-permute-start.17 = (bf16[36,1152]{1,0:T(8,128)(2,1)S(1)}, bf16[36,1152]{1,0:T(8,128)(2,1)S(1)}, u32[]{:S(2)}, u32[]{:S(2)}) collective-permute-start(bf16[36,1152]{1,0:T(8,128)(2,1)S(1)} %shard_map.101), channel_id=1, source_target_pairs={{0,64},{32,96},{64,0},{96,32},{1,65},{33,97},{65,1},{97,33},{2,66}... | collective-permute-start | bytes 248840 | tf_op jit(solution)/shard_map/ppermute | solution.py:406
  (12 other events, 48.6 us)
